TPU v7x, 512 devices: a whole 4x4x16 slice. The times are simulated.
512 devices in a mesh: rows: 32 (over y, x, core), vocab: 16 (over z).
Axes of the slice: x: 4, y: 4, z: 16, core: 2. Of those that a mesh axis runs over, the one named last changes fastest.
Arguments:
- expert_hidden: bfloat16 [128, 8192], P('rows'), may hold values from -400 to 400
- expert_gain: bfloat16 [8192], replicated, may hold values from 0.5 to 1.5
- expert_head: bfloat16 [98304, 8192], P(('rows', 'vocab')), may hold values from -1 to 1
- amateur_hidden: bfloat16 [128, 3584], P('rows'), may hold values from -400 to 400
- amateur_gain: bfloat16 [3584], replicated, may hold values from 0.5 to 1.5
- amateur_head: bfloat16 [98304, 3584], P(('rows', 'vocab')), may hold values from -1 to 1
- live_mask: int32 [98304], P(('rows', 'vocab')), may hold values 0 or 1
- token_ids: int32 [128], replicated, may hold values from 0 to 98303
- plaus_level: int32 [128], replicated, may hold values from 5 to 40
Outputs:
- top_scores: float32 [128, 4], P('rows')
- peak_logprob: float32 [128, 2], P('rows')
- chosen_score: float32 [128], P('rows')
All inputs are finite; a program needn't handle non-finite values. No bound on the sum of `live_mask` on one device may be relied on, other than what follows from the above.
Results may differ from a plain program's by a relative error of at most 0.012.
The roundings to bfloat16 on the way count: a program that leaves them out, or rounds other values in their place, can miss the bound.
Values may be sent and summed in bfloat16 or wider, within the bound.
No kernel may reach another device: no remote copies, remote signals or barrier semaphores. Data moves between devices by JAX's collectives and lax.ppermute only.
A program may use at most 128 MiB of HBM per device.

v0:
```python
import jax
import jax.numpy as jnp
from jax import lax
from jax.sharding import PartitionSpec as P

TOP = 4


masked_floor = -1e30
penalty_slope = 2.0
norm_epsilon = 1e-06


def joined_2(part, axis, combine):
    gathered = lax.all_gather(part, axis)

    def take(source):
        return lax.dynamic_index_in_dim(gathered, source, 0, False)

    return lax.fori_loop(
        1, lax.axis_size(axis), lambda source, state: combine(state, take(source)), take(0)
    )


def normed_rows(row_block, gain):
    values = row_block.astype(jnp.float32)
    inverse_rms = lax.rsqrt(jnp.mean(values * values, axis=-1, keepdims=True) + norm_epsilon)
    return (values * inverse_rms * gain.astype(jnp.float32)).astype(jnp.bfloat16)


def head_product(normed, head):
    return lax.dot_general(
        normed, head, (((1,), (1,)), ((), ())), preferred_element_type=jnp.float32
    )


def contrast_scores(logits_e, logits_a, log_total_e, log_total_a, peak_e, alpha_gap):
    logprob_e = logits_e - log_total_e[:, None]
    logprob_a = logits_a - log_total_a[:, None]
    cut_value = peak_e - log_total_e - alpha_gap
    return logprob_e - logprob_a - penalty_slope * jnp.maximum(cut_value[:, None] - logprob_e, 0.0)


def keep_best(left_part, right_part):
    joined = jnp.concatenate([left_part, right_part], axis=1)
    return lax.top_k(joined, left_part.shape[1])[0]


def per_device(
    expert_hidden,
    expert_gain,
    expert_head,
    amateur_hidden,
    amateur_gain,
    amateur_head,
    live_mask,
    token_ids,
    plaus_level,
):
    gathered_e = lax.all_gather(expert_hidden, "rows", axis=0, tiled=True)
    gathered_a = lax.all_gather(amateur_hidden, "rows", axis=0, tiled=True)
    expert_logits = head_product(normed_rows(gathered_e, expert_gain), expert_head)
    amateur_logits = head_product(normed_rows(gathered_a, amateur_gain), amateur_head)
    width_v = expert_head.shape[0]
    shard_index = lax.axis_index("rows") * lax.axis_size("vocab") + lax.axis_index("vocab")
    positions = shard_index * width_v + lax.broadcasted_iota(jnp.int32, (1, width_v), 1)
    id_hits = token_ids[:, None] == positions
    live_cols = live_mask[None, :] == 1
    held_e = jnp.where(live_cols, expert_logits, masked_floor)
    held_a = jnp.where(live_cols, amateur_logits, masked_floor)
    pick_e = jnp.sum(jnp.where(id_hits, expert_logits, 0.0), axis=1)
    pick_a = jnp.sum(jnp.where(id_hits, amateur_logits, 0.0), axis=1)
    alpha_gap = plaus_level.astype(jnp.float32) * 0.1
    local_e = jnp.max(held_e, axis=1)
    local_a = jnp.max(held_a, axis=1)
    peak_e, peak_a = lax.pmax((local_e, local_a), ("rows", "vocab"))
    total_e = jnp.sum(jnp.exp(held_e - peak_e[:, None]), axis=1)
    total_a = jnp.sum(jnp.exp(held_a - peak_a[:, None]), axis=1)
    total_e, total_a, pick_e, pick_a = lax.psum(
        (total_e, total_a, pick_e, pick_a), ("rows", "vocab")
    )
    log_total_e = peak_e + jnp.log(total_e)
    log_total_a = peak_a + jnp.log(total_a)
    score_table = contrast_scores(
        expert_logits, amateur_logits, log_total_e, log_total_a, peak_e, alpha_gap
    )
    candidates = lax.top_k(jnp.where(live_cols, score_table, masked_floor), TOP)[0]
    best_scores = joined_2(candidates, ("rows", "vocab"), keep_best)
    chosen = contrast_scores(
        pick_e[:, None], pick_a[:, None], log_total_e, log_total_a, peak_e, alpha_gap
    )[:, 0]
    peaks = jnp.stack([peak_e - log_total_e, peak_a - log_total_a], axis=1)
    beam_count = expert_hidden.shape[0]
    first_beam = lax.axis_index("rows") * beam_count
    return (
        lax.dynamic_slice_in_dim(best_scores, first_beam, beam_count, 0),
        lax.dynamic_slice_in_dim(peaks, first_beam, beam_count, 0),
        lax.dynamic_slice_in_dim(chosen, first_beam, beam_count, 0),
    )


def solution(mesh):
    in_specs = (
        P("rows", None),
        P(),
        P(("rows", "vocab"), None),
        P("rows", None),
        P(),
        P(("rows", "vocab"), None),
        P(("rows", "vocab")),
        P(),
        P(),
    )
    out_specs = (P("rows", None), P("rows", None), P("rows"))
    return jax.shard_map(
        per_device, mesh=mesh, in_specs=in_specs, out_specs=out_specs, check_vma=False
    )
```

profile of v0, /device:TPU:1, one launch (start us, length us, event | category | flops | bytes accessed | tf_op | source)
XLA Modules:
  0.0 1237.0 jit_solution(9288890468006543860)
XLA Ops:
  8.0 0.8 convert_element_type.25
  8.8 0.7 convert_element_type.22
  9.5 32.2 %all-gather.2 = bf16[32,4,3584]{2,1,0:T(4,128)(2,1)} all-gather(bf16[1,4,3584]{2,1,0:T(4,128)(2,1)} %bitcast.15), channel_id=1, replica_groups=mesh['rows'=32,'vocab'=16] {'rows'}, dimensions={0}, use_global_device_ids=true | all-gather | bytes 946176 | tf_op jit(solution)/shard_map/all_gather | solution.py:61
  41.7 2.6 reshape.55
  44.3 1.7 multiply_reduce_fusion.1
  46.1 30.0 %all-gather.8.cloned.1.call-done = bf16[32,4,8192]{2,1,0:T(4,128)(2,1)} async-done(((bf16[1,4,8192]{2,1,0:T(4,128)(2,1)}), bf16[32,4,8192]{2,1,0:T(4,128)(2,1)}) %all-gather.8.cloned.1.call-update) | async-done | bytes 2097168 | tf_op jit(solution)/shard_map/all_gather | solution.py:60
  76.1 4.2 reshape.54
  80.3 2.7 multiply_reduce_fusion
  83.0 0.7 copy-done.1
  83.7 1.2 fusion
  86.2 103.7 %all-reduce.1 = (f32[128]{0:T(128)S(1)}, f32[128]{0:T(128)S(1)}) all-reduce(f32[128]{0:T(128)S(1)} %get-tuple-element.112, f32[128]{0:T(128)S(1)} %get-tuple-element.111), channel_id=1, replica_groups=mesh['rows'=32,'vocab'=16] {'rows','vocab'}, use_global_device_ids=true, to_apply=%region_2.3 | all-reduce | flops 256 | bytes 2048 | tf_op jit(solution)/shard_map/pmax | solution.py:76
  190.1 100.3 %all-reduce = (f32[128]{0:T(128)S(1)}, f32[128]{0:T(128)S(1)}, f32[128]{0:T(128)S(1)}, f32[128]{0:T(128)S(1)}) all-reduce(f32[128]{0:T(128)S(1)} %get-tuple-element.109, f32[128]{0:T(128)S(1)} %get-tuple-element.108, f32[128]{0:T(128)S(1)} %get-tuple-element.107, ...), channel_id=1, replica_groups=mesh['rows'=32,'vocab'=16] {'rows','vocab'}, use_global_device_ids=true, to_apply=%region_4.5 | all-reduce | flops 512 | bytes 4096 | tf_op jit(solution)/shard_map/psum | solution.py:79
  291.0 3.5 top_k.14
  295.3 1.2 dynamic_slice.26
  297.2 230.8 %all-gather.6.cloned.1.call-done = f32[65536,4]{1,0:T(8,128)} async-done(((f32[128,4]{1,0:T(8,128)}), f32[65536,4]{1,0:T(8,128)}) %all-gather.6.cloned.1.call-update) | async-done | bytes 1048592 | tf_op jit(solution)/shard_map/all_gather | solution.py:15
  528.0 0.8 slice.11
  528.9 18.3 %copy.20 = f32[512,128,4]{1,2,0:T(4,128)} copy(f32[512,128,4]{2,1,0:T(8,128)} %bitcast.13) | data formatting | bytes 2097152 | tf_op jit(solution)/shard_map/while | solution.py:20
  547.2 682.2 %while.15 = (s32[]{:T(128)}, f32[128,4]{0,1:T(4,128)S(1)}, f32[512,128,4]{1,2,0:T(4,128)}, s32[]{:T(128)}, s32[]{:T(128)}, /*index=5*/s32[]{:T(128)}) while((s32[]{:T(128)}, f32[128,4]{0,1:T(4,128)S(1)}, f32[512,128,4]{1,2,0:T(4,128)}, s32[]{:T(128)}, s32[]{:T(128)}, /*index=5*/s32[]{:T(128)}) %tuple.53), condition=%wide.region_13.14_spmd, body=%wide.region_11.13_spmd.sunk | while | flops 11269 | bytes 36971 | solution.py:20
  556.5 0.7 dynamic-slice_bitcast_fusion.2
  580.4 0.7 dynamic-slice_bitcast_fusion.2
  607.1 0.7 dynamic-slice_bitcast_fusion.2
  628.4 0.7 dynamic-slice_bitcast_fusion.2
  639.0 0.7 dynamic-slice_bitcast_fusion.2
  677.7 0.7 dynamic-slice_bitcast_fusion.2
  711.1 0.7 dynamic-slice_bitcast_fusion.2
  725.8 0.7 dynamic-slice_bitcast_fusion.2
  744.4 0.7 dynamic-slice_bitcast_fusion.2
  764.4 0.7 dynamic-slice_bitcast_fusion.2
  799.1 0.7 dynamic-slice_bitcast_fusion.2
  812.4 0.7 dynamic-slice_bitcast_fusion.2
  847.0 0.7 dynamic-slice_bitcast_fusion.2
  877.7 0.7 dynamic-slice_bitcast_fusion.2
  880.4 0.7 dynamic-slice_bitcast_fusion.2
  900.4 0.7 dynamic-slice_bitcast_fusion.2
  908.4 0.7 dynamic-slice_bitcast_fusion.2
  928.5 0.7 dynamic-slice_bitcast_fusion.2
  936.5 0.7 dynamic-slice_bitcast_fusion.2
  984.6 0.7 dynamic-slice_bitcast_fusion.2
  1000.6 0.7 dynamic-slice_bitcast_fusion.2
  1003.3 0.7 dynamic-slice_bitcast_fusion.2
  1031.5 0.7 dynamic-slice_bitcast_fusion.2
  1050.3 0.7 dynamic-slice_bitcast_fusion.2
  1058.3 0.7 dynamic-slice_bitcast_fusion.2
  1111.7 0.7 dynamic-slice_bitcast_fusion.2
  1137.0 0.7 dynamic-slice_bitcast_fusion.2
  1157.2 0.7 dynamic-slice_bitcast_fusion.2
  1173.2 0.7 dynamic-slice_bitcast_fusion.2
  1201.4 0.7 dynamic-slice_bitcast_fusion.2
  (2559 shorter events, 665.4 us)
Async XLA Ops:
  7.2 75.8 %copy-start = (bf16[192,8192]{1,0:T(8,128)(2,1)S(1)}, bf16[192,8192]{1,0:T(8,128)(2,1)}, u32[]{:S(2)}) copy-start(bf16[192,8192]{1,0:T(8,128)(2,1)} %param.13) | copy-start | bytes 9437188
  7.2 68.9 %all-gather.8.cloned.1.call-start = ((), (), s32[]{:S(2)}) async-start(), calls=%async_computation.1 | async-start | bytes 2162688 | tf_op jit(solution)/shard_map/all_gather | solution.py:60
  7.9 520.1 %all-gather.6.cloned.1.call-start = ((), (), s32[]{:S(2)}) async-start(), calls=%async_computation | async-start | bytes 33619968 | tf_op jit(solution)/shard_map/all_gather | solution.py:15
  41.7 4.3 copy-start.6
  80.3 3.4 copy-start.1
  83.7 1.5 copy-start.2
  83.7 1.9 copy-start.3
  85.6 104.3 %copy-start.4 = (s32[128]{0:T(128)S(1)}, s32[128]{0:T(128)}, u32[]{:S(2)}) copy-start(s32[128]{0:T(128)} %param.18) | copy-start | bytes 1540
  85.6 204.7 %copy-start.5 = (s32[128]{0:T(128)S(1)}, s32[128]{0:T(128)}, u32[]{:S(2)}) copy-start(s32[128]{0:T(128)} %param.19) | copy-start | bytes 1540
Sparse Core Ops, SparseCore 0:
  11.1 64.8 all-gather.7
  295.4 232.5 all-gather.5
where the time goes:
time: 1250 us; the launch traced here: 1240 us
  local copies, waits for them, and re-layouts  368 us (29%)
  other arithmetic  354 us (28%)
  waiting for transfers between devices  262 us (21%)
  blocking collectives  236 us (19%)
  between operations  14.1 us (1%)
    top_k x511, other arithmetic, keep_best(): return lax.top_k(joined, left_part.shape[1])[0]  339 us
    squeeze x511, local copies, waits for them, and re-layouts, take(): return lax.dynamic_index_in_dim(gathered, source, 0, False)  334 us
    all_gather x1, waiting for transfers between devices, joined_2(): gathered = lax.all_gather(part, axis)  231 us
    pmax x1, blocking collectives, per_device(): peak_e, peak_a = lax.pmax((local_e, local_a), ('rows', 'vocab'))  104 us
    psum x1, blocking collectives, per_device(): lax.psum((total_e, total_a, pick_e, pick_a), ('rows', 'vocab'))  100 us
    all_gather x1, blocking collectives, per_device(): gathered_a = lax.all_gather(amateur_hidden, 'rows', axis=0, tiled=True)  32.2 us
    all_gather x1, waiting for transfers between devices, per_device(): gathered_e = lax.all_gather(expert_hidden, 'rows', axis=0, tiled=True)  30 us
  transfers between devices with their start and end apart: 2, of which 2 were waited for; matrix products, arithmetic and copies ran while one was open for 1% of the time, Pallas kernels for 0%

commit v1 on v0

v1 whole, which is shorter than its diff:
```python
import functools

import jax
import jax.numpy as jnp
from jax import lax
from jax.experimental import pallas as pl
from jax.experimental.pallas import tpu as pltpu
from jax.sharding import PartitionSpec as P

TOP = 4
NY, NX, NC = 4, 4, 2

masked_floor = -1e30
dead_below = -5e29
penalty_slope = 2.0
norm_epsilon = 1e-06

VMEM = pl.BlockSpec(memory_space=pltpu.VMEM)
SMEM = pl.BlockSpec(memory_space=pltpu.SMEM)
PARAMS = pltpu.CompilerParams(vmem_limit_bytes=40 * 1024 * 1024)


def row_of(y, x, c):
    return ((y % NY) * NX + x % NX) * NC + c % NC


def fetch(block, dy, dx, dc):
    pairs = [
        (row_of(y + dy, x + dx, c + dc), row_of(y, x, c))
        for y in range(NY)
        for x in range(NX)
        for c in range(NC)
    ]
    return lax.ppermute(block, "rows", pairs)


def norm_kernel(core_ref, he_ref, ge_ref, ha_ref, ga_ref, mine_ref, other_ref):
    def normed(values, gain):
        values = values.astype(jnp.float32)
        mean = jnp.mean(values * values, axis=-1, keepdims=True)
        return values * lax.rsqrt(mean + norm_epsilon) * gain.astype(jnp.float32)

    e = normed(he_ref[...], ge_ref[...])
    a = normed(ha_ref[...], ga_ref[...])
    qe, qa = e.shape[1] // 4, a.shape[1] // 4
    first = core_ref[0] == 0
    for p in range(2):
        for low, high, out in ((p, 2 + p, mine_ref), (2 + p, p, other_ref)):
            part_e = jnp.where(first, e[:, low * qe:(low + 1) * qe], e[:, high * qe:(high + 1) * qe])
            part_a = jnp.where(first, a[:, low * qa:(low + 1) * qa], a[:, high * qa:(high + 1) * qa])
            out[p, :, 0:qe] = part_e.astype(jnp.bfloat16)
            out[p, :, qe:qe + qa] = part_a.astype(jnp.bfloat16)


def logits_kernel(pos_ref, mine_ref, recv_ref, he_ref, ha_ref, live_ref, ids_ref, out_ref, acc_ref):
    y, x, c, base = pos_ref[0], pos_ref[1], pos_ref[2], pos_ref[3]
    width = he_ref.shape[0]
    beams = mine_ref.shape[0] // 2
    qe, qa = he_ref.shape[1] // 4, ha_ref.shape[1] // 4
    dims = (((1,), (1,)), ((), ()))
    for p in range(2):
        rows = slice(p * beams, (p + 1) * beams)
        for model, head, low, size in ((0, he_ref, 0, qe), (1, ha_ref, qe, qa)):
            total = None
            for part, core in ((mine_ref, c), (recv_ref, 1 - c)):
                columns = pl.ds(pl.multiple_of((2 * core + p) * size, 128), size)
                product = lax.dot_general(
                    part[rows, low:low + size], head[:, columns], dims,
                    preferred_element_type=jnp.float32,
                )
                total = product if total is None else total + product
            acc_ref[model, p] = total
    live = live_ref[...] == 1
    positions = base + lax.broadcasted_iota(jnp.int32, (1, width), 1)
    for ky in range(NY):
        for kx in range(NX):
            chip = lax.rem(y + ky, NY) * NX + lax.rem(x + kx, NX)
            hits = ids_ref[chip] == positions
            for model in range(2):
                p_row, q_row = (ky * NX + kx) * 8, (kx * NY + ky) * 8
                logits = acc_ref[model, 0, p_row:p_row + 8, :] + acc_ref[model, 1, q_row:q_row + 8, :]
                held = jnp.where(live, logits, masked_floor)
                pick = jnp.sum(jnp.where(hits, logits, 0.0), axis=1, keepdims=True)
                pick = jnp.broadcast_to(pick, (8, 256 - width))
                for core in range(NC):
                    at = 256 * model
                    own = slice(4 * core, 4 * core + 4)
                    out_ref[2 * chip + core, :, at:at + width] = held[own]
                    out_ref[2 * chip + core, :, at + width:at + 256] = pick[own]


def lanes_of(columns, shape):
    lane = lax.broadcasted_iota(jnp.int32, shape, len(shape) - 1)
    result = jnp.zeros(shape, jnp.float32)
    for i, column in enumerate(columns):
        result = jnp.where(lane == i, column, result)
    return result


def lane_at(values, i):
    lane = lax.broadcasted_iota(jnp.int32, values.shape, values.ndim - 1)
    return jnp.sum(jnp.where(lane == i, values, 0.0), axis=-1, keepdims=True)


def stats_kernel(width, table_ref, out_ref):
    columns = []
    for model in range(2):
        part = table_ref[:, :, 256 * model:256 * model + 256]
        real = lax.broadcasted_iota(jnp.int32, part.shape, 2) < width
        peak = jnp.max(jnp.max(jnp.where(real, part, masked_floor), axis=0), axis=1, keepdims=True)
        total = jnp.sum(jnp.where(real, jnp.exp(part - peak[None]), 0.0), axis=0)
        total = jnp.sum(total, axis=1, keepdims=True)
        pick = lane_at(jnp.sum(part, axis=0), width)
        columns.append((peak, total, pick))
    (pe, te, ce), (pa, ta, ca) = columns
    out_ref[...] = lanes_of([pe, pa, te, ta, ce, ca], out_ref.shape)


def best_of(levels):
    lane = lax.broadcasted_iota(jnp.int32, levels[0].shape, 1)
    found = []
    for _ in range(TOP):
        top = jnp.max(levels[0], axis=1, keepdims=True)
        found.append(top)
        at = jnp.min(jnp.where(levels[0] == top, lane, lane.shape[1]), axis=1, keepdims=True)
        hit = lane == at
        lower = levels[1:] + [jnp.full_like(levels[0], -jnp.inf)]
        levels = [jnp.where(hit, low, level) for level, low in zip(levels, lower)]
    return found


def sorted_levels(parts):
    levels = [jnp.full_like(parts[0], -jnp.inf)] * TOP
    for part in parts:
        for i in range(TOP):
            levels[i], part = jnp.maximum(levels[i], part), jnp.minimum(levels[i], part)
    return levels


def score_kernel(width, table_ref, stats_ref, gap_ref, best_ref, peaks_ref, chosen_ref):
    stats = stats_ref[...]
    peak_e, peak_a, sum_e, sum_a, pick_e, pick_a = [lane_at(stats, i) for i in range(6)]

    def total_of(peaks, sums):
        peak = jnp.max(peaks, axis=0)
        return peak, peak + jnp.log(jnp.sum(sums * jnp.exp(peaks - peak[None]), axis=0))

    peak_e, log_total_e = total_of(peak_e, sum_e)
    peak_a, log_total_a = total_of(peak_a, sum_a)
    cut = peak_e - log_total_e - gap_ref[...].astype(jnp.float32) * 0.1

    def score(logits_e, logits_a):
        logprob_e = logits_e - log_total_e
        logprob_a = logits_a - log_total_a
        return logprob_e - logprob_a - penalty_slope * jnp.maximum(cut - logprob_e, 0.0)

    peaks_ref[...] = lanes_of([peak_e - log_total_e, peak_a - log_total_a], peaks_ref.shape)
    chosen_ref[...] = score(jnp.sum(pick_e, axis=0), jnp.sum(pick_a, axis=0))
    real = lax.broadcasted_iota(jnp.int32, (table_ref.shape[1], 256), 1) < width
    parts = []
    for source in range(table_ref.shape[0]):
        e = table_ref[source, :, 0:256]
        a = table_ref[source, :, 256:512]
        parts.append(jnp.where(real & (e > dead_below), score(e, a), masked_floor))
    best_ref[...] = lanes_of(best_of(sorted_levels(parts)), best_ref.shape)


def merge_kernel(parts_ref, out_ref):
    shape = parts_ref.shape[1:]
    real = lax.broadcasted_iota(jnp.int32, shape, 1) < TOP
    parts = [jnp.where(real, parts_ref[i], -jnp.inf) for i in range(parts_ref.shape[0])]
    out_ref[...] = lanes_of(best_of(sorted_levels(parts)), out_ref.shape)


def per_device(
    expert_hidden,
    expert_gain,
    expert_head,
    amateur_hidden,
    amateur_gain,
    amateur_head,
    live_mask,
    token_ids,
    plaus_level,
):
    own, depth_e = expert_hidden.shape
    depth_a = amateur_hidden.shape[1]
    width = expert_head.shape[0]
    rows, planes = lax.axis_size("rows"), lax.axis_size("vocab")
    beams = own * rows
    quarter = (depth_e + depth_a) // 4
    row, plane = lax.axis_index("rows"), lax.axis_index("vocab")
    core, x, y = row % NC, row // NC % NX, row // (NC * NX)
    position = jnp.stack([y, x, core, (row * planes + plane) * width]).astype(jnp.int32)
    ids = token_ids.reshape(rows // NC, NC * own, 1)
    gap = lax.dynamic_slice_in_dim(plaus_level, row * own, own, 0).reshape(own, 1)

    piece = jax.ShapeDtypeStruct((2, own, quarter), jnp.bfloat16)
    mine, other = pl.pallas_call(
        norm_kernel,
        out_shape=(piece, piece),
        in_specs=[SMEM] + [VMEM] * 4,
        out_specs=(VMEM, VMEM),
        compiler_params=PARAMS,
        name="norms",
    )(core.astype(jnp.int32).reshape(1), expert_hidden, expert_gain.reshape(1, -1),
      amateur_hidden, amateur_gain.reshape(1, -1))
    recv = fetch(other, 0, 0, 1)
    chip = jnp.where(core == 0, jnp.concatenate([mine, recv], 1), jnp.concatenate([recv, mine], 1))
    p_part, q_part = chip[0], chip[1]
    p_line = jnp.concatenate([p_part] + [fetch(p_part, 0, k, 0) for k in range(1, NX)])
    q_line = jnp.concatenate([q_part] + [fetch(q_part, k, 0, 0) for k in range(1, NY)])
    p_rest = [fetch(p_line, k, 0, 0) for k in range(1, NY)]
    q_rest = [fetch(q_line, 0, k, 0) for k in range(1, NX)]
    half = jnp.concatenate([p_line] + p_rest + [q_line] + q_rest)
    other_half = fetch(half, 0, 0, 1)

    table = pl.pallas_call(
        logits_kernel,
        out_shape=jax.ShapeDtypeStruct((rows, own, 512), jnp.float32),
        in_specs=[SMEM] + [VMEM] * 6,
        out_specs=VMEM,
        scratch_shapes=[pltpu.VMEM((2, 2, beams, width), jnp.float32)],
        compiler_params=PARAMS,
        name="logits",
    )(position, half, other_half, expert_head, amateur_head, live_mask.reshape(1, -1), ids)
    table = lax.all_to_all(table, "rows", 0, 0, tiled=True)

    small = jax.ShapeDtypeStruct((own, 128), jnp.float32)
    stats = pl.pallas_call(
        functools.partial(stats_kernel, width),
        out_shape=small,
        in_specs=[VMEM],
        out_specs=VMEM,
        compiler_params=PARAMS,
        name="stats",
    )(table)
    stats = lax.all_gather(stats, "vocab")
    best, peaks, chosen = pl.pallas_call(
        functools.partial(score_kernel, width),
        out_shape=(
            small,
            jax.ShapeDtypeStruct((own, 2), jnp.float32),
            jax.ShapeDtypeStruct((own, 1), jnp.float32),
        ),
        in_specs=[VMEM] * 3,
        out_specs=(VMEM,) * 3,
        compiler_params=PARAMS,
        name="scores",
    )(table, stats, gap)
    others = [
        lax.ppermute(best, "vocab", [((z + k) % planes, z) for z in range(planes)])
        for k in range(1, planes)
    ]
    top = pl.pallas_call(
        merge_kernel,
        out_shape=jax.ShapeDtypeStruct((own, TOP), jnp.float32),
        in_specs=[VMEM],
        out_specs=VMEM,
        compiler_params=PARAMS,
        name="merge",
    )(jnp.stack([best] + others))
    return top, peaks, chosen.reshape(own)


def solution(mesh):
    in_specs = (
        P("rows", None),
        P(),
        P(("rows", "vocab"), None),
        P("rows", None),
        P(),
        P(("rows", "vocab"), None),
        P(("rows", "vocab")),
        P(),
        P(),
    )
    out_specs = (P("rows", None), P("rows", None), P("rows"))
    return jax.shard_map(
        per_device, mesh=mesh, in_specs=in_specs, out_specs=out_specs, check_vma=False
    )
```

time: 1250 us -> 203 us (0.16)
  the two profiles are of different devices: /device:TPU:1 before, /device:TPU:32 now
where the time goes in v1:
time: 203 us; the launch traced here: 201 us
  starting transfers between devices  127 us (63%)
  blocking collectives  33.4 us (16%)
  waiting for transfers between devices  16.5 us (8%)
  local copies, waits for them, and re-layouts  14.6 us (7%)
  Pallas kernels  7.39 us (4%)
    ppermute x15, starting transfers between devices, per_device(): lax.ppermute(best, 'vocab', [((z + k) % planes, z) for z in range(planes)])  76.7 us
    ppermute x14, starting transfers between devices, fetch(): return lax.ppermute(block, 'rows', pairs)  43.9 us
    all_gather x1, blocking collectives, per_device(): stats = lax.all_gather(stats, 'vocab')  33.4 us
    unnamed x43, local copies, waits for them, and re-layouts  12.1 us
    all_to_all x1, waiting for transfers between devices, per_device(): table = lax.all_to_all(table, 'rows', 0, 0, tiled=True)  8.71 us
    all_to_all x1, starting transfers between devices, per_device(): table = lax.all_to_all(table, 'rows', 0, 0, tiled=True)  6.74 us
    ppermute x14, waiting for transfers between devices, fetch(): return lax.ppermute(block, 'rows', pairs)  5.31 us
    pallas_call x1, Pallas kernels, per_device(): pl.pallas_call(logits_kernel, out_shape=jax.ShapeDtypeStruct((rows, own,...  4.4 us
  transfers between devices with their start and end apart: 30, of which 5 were waited for; matrix products, arithmetic and copies ran while one was open for 5% of the time, Pallas kernels for 0%

profile of v1, /device:TPU:32, one launch (start us, length us, event | category | flops | bytes accessed | tf_op | source)
XLA Modules:
  0.0 201.4 jit_solution(5618624142346669379)
XLA Ops:
  0.7 0.7 reshape.25.ge_ref
  1.4 0.7 reshape.26.ga_ref
  2.1 0.8 copy-done.3
  3.0 0.7 copy-done.4
  3.9 1.9 collective-permute-start
  5.9 1.2 collective-permute-done
  7.1 4.7 %collective-permute-start.1 = (bf16[8,2944]{1,0:T(8,128)(2,1)S(1)}, bf16[8,2944]{1,0:T(8,128)(2,1)S(1)}, u32[]{:S(2)}, u32[]{:S(2)}) collective-permute-start(bf16[8,2944]{1,0:T(8,128)(2,1)S(1)} %get-tuple-element.23), channel_id=1, source_target_pairs={{32,0},{48,16},{64,32},{80,48},{96,64},{112,80},{0,96},{16,112},{1... | collective-permute-start | bytes 141320 | tf_op jit(solution)/shard_map/ppermute | solution.py:34
  11.8 2.7 %collective-permute-start.2 = (bf16[8,2944]{1,0:T(8,128)(2,1)S(1)}, bf16[8,2944]{1,0:T(8,128)(2,1)S(1)}, u32[]{:S(2)}, u32[]{:S(2)}) collective-permute-start(bf16[8,2944]{1,0:T(8,128)(2,1)S(1)} %get-tuple-element.23), channel_id=1, source_target_pairs={{64,0},{80,16},{96,32},{112,48},{0,64},{16,80},{32,96},{48,112},{1... | collective-permute-start | bytes 141320 | tf_op jit(solution)/shard_map/ppermute | solution.py:34
  14.5 2.8 %collective-permute-start.3 = (bf16[8,2944]{1,0:T(8,128)(2,1)S(1)}, bf16[8,2944]{1,0:T(8,128)(2,1)S(1)}, u32[]{:S(2)}, u32[]{:S(2)}) collective-permute-start(bf16[8,2944]{1,0:T(8,128)(2,1)S(1)} %get-tuple-element.23), channel_id=1, source_target_pairs={{96,0},{112,16},{0,32},{16,48},{32,64},{48,80},{64,96},{80,112},{2... | collective-permute-start | bytes 141320 | tf_op jit(solution)/shard_map/ppermute | solution.py:34
  18.0 4.9 %collective-permute-start.7 = (bf16[8,2944]{1,0:T(8,128)(2,1)S(1)}, bf16[8,2944]{1,0:T(8,128)(2,1)S(1)}, u32[]{:S(2)}, u32[]{:S(2)}) collective-permute-start(bf16[8,2944]{1,0:T(8,128)(2,1)S(1)} %get-tuple-element.22), channel_id=1, source_target_pairs={{128,0},{144,16},{160,32},{176,48},{192,64},{208,80},{224,96},{240... | collective-permute-start | bytes 141320 | tf_op jit(solution)/shard_map/ppermute | solution.py:34
  22.9 2.5 %collective-permute-start.8 = (bf16[8,2944]{1,0:T(8,128)(2,1)S(1)}, bf16[8,2944]{1,0:T(8,128)(2,1)S(1)}, u32[]{:S(2)}, u32[]{:S(2)}) collective-permute-start(bf16[8,2944]{1,0:T(8,128)(2,1)S(1)} %get-tuple-element.22), channel_id=1, source_target_pairs={{256,0},{272,16},{288,32},{304,48},{320,64},{336,80},{352,96},{368... | collective-permute-start | bytes 141320 | tf_op jit(solution)/shard_map/ppermute | solution.py:34
  25.4 2.9 %collective-permute-start.9 = (bf16[8,2944]{1,0:T(8,128)(2,1)S(1)}, bf16[8,2944]{1,0:T(8,128)(2,1)S(1)}, u32[]{:S(2)}, u32[]{:S(2)}) collective-permute-start(bf16[8,2944]{1,0:T(8,128)(2,1)S(1)} %get-tuple-element.22), channel_id=1, source_target_pairs={{384,0},{400,16},{416,32},{432,48},{448,64},{464,80},{480,96},{496... | collective-permute-start | bytes 141320 | tf_op jit(solution)/shard_map/ppermute | solution.py:34
  28.4 4.2 %collective-permute-start.4 = (bf16[32,2944]{1,0:T(8,128)(2,1)S(1)}, bf16[32,2944]{1,0:T(8,128)(2,1)S(1)}, u32[]{:S(2)}, u32[]{:S(2)}) collective-permute-start(bf16[32,2944]{1,0:T(8,128)(2,1)S(1)} %pad_maximum_fusion), channel_id=1, source_target_pairs={{128,0},{144,16},{160,32},{176,48},{192,64},{208,80},{224,96},{240... | collective-permute-start | bytes 565256 | tf_op jit(solution)/shard_map/ppermute | solution.py:34
  32.5 3.6 %collective-permute-start.5 = (bf16[32,2944]{1,0:T(8,128)(2,1)S(1)}, bf16[32,2944]{1,0:T(8,128)(2,1)S(1)}, u32[]{:S(2)}, u32[]{:S(2)}) collective-permute-start(bf16[32,2944]{1,0:T(8,128)(2,1)S(1)} %pad_maximum_fusion), channel_id=1, source_target_pairs={{256,0},{272,16},{288,32},{304,48},{320,64},{336,80},{352,96},{368... | collective-permute-start | bytes 565256 | tf_op jit(solution)/shard_map/ppermute | solution.py:34
  36.2 1.9 collective-permute-start.6
  38.2 4.5 %collective-permute-start.10 = (bf16[32,2944]{1,0:T(8,128)(2,1)S(1)}, bf16[32,2944]{1,0:T(8,128)(2,1)S(1)}, u32[]{:S(2)}, u32[]{:S(2)}) collective-permute-start(bf16[32,2944]{1,0:T(8,128)(2,1)S(1)} %pad_maximum_fusion.1), channel_id=1, source_target_pairs={{32,0},{48,16},{64,32},{80,48},{96,64},{112,80},{0,96},{16,112},{1... | collective-permute-start | bytes 565256 | tf_op jit(solution)/shard_map/ppermute | solution.py:34
  42.7 3.4 %collective-permute-start.11 = (bf16[32,2944]{1,0:T(8,128)(2,1)S(1)}, bf16[32,2944]{1,0:T(8,128)(2,1)S(1)}, u32[]{:S(2)}, u32[]{:S(2)}) collective-permute-start(bf16[32,2944]{1,0:T(8,128)(2,1)S(1)} %pad_maximum_fusion.1), channel_id=1, source_target_pairs={{64,0},{80,16},{96,32},{112,48},{0,64},{16,80},{32,96},{48,112},{1... | collective-permute-start | bytes 565256 | tf_op jit(solution)/shard_map/ppermute | solution.py:34
  48.0 1.9 collective-permute-start.12
  50.6 0.7 constant_dynamic-update-slice_fusion.8
  51.3 0.7 constant_dynamic-update-slice_fusion.7
  54.5 0.7 constant_dynamic-update-slice_fusion.2
  55.9 0.8 collective-permute-done.12
  56.7 0.7 constant_dynamic-update-slice_fusion.mine_ref
  57.4 1.9 collective-permute-start.13
  59.6 3.3 %collective-permute-done.13.recv_ref = bf16[256,2944]{1,0:T(8,128)(2,1)} collective-permute-done((bf16[256,2944]{1,0:T(8,128)(2,1)}, bf16[256,2944]{1,0:T(8,128)(2,1)}, u32[]{:S(2)}, u32[]{:S(2)}) %collective-permute-start.13) | collective-permute-done | bytes 1507360 | tf_op jit(solution)/shard_map/ppermute | solution.py:34
  62.9 1.3 copy-done.2
  64.2 4.4 %logits.1 = f32[32,4,512]{2,1,0:T(4,128)} custom-call(s32[4]{0:T(128)S(1)} %pad_add_fusion.pos_ref, bf16[256,2944]{1,0:T(8,128)(2,1)} %constant_dynamic-update-slice_fusion.mine_ref, bf16[256,2944]{1,0:T(8,128)(2,1)} %collective-permute-done.13.recv_ref, bf16[192,8192]{1,0:T(8,128)(2,1)S(1)} %copy-done.1, bf16[192,3584]{1,0:T(8,128)(2,1)S(1)} %copy-done.2, ...), custom_call_target="tpu_custom_call" | custom-call | tf_op jit(solution)/shard_map/logits/pallas_call | solution.py:218
  68.7 6.7 %all-to-all-start = ((f32[32,4,512]{2,1,0:T(4,128)}), f32[32,4,512]{2,1,0:T(4,128)S(1)}, u32[]{:S(2)}, u32[]{:S(2)}) async-start(f32[32,4,512]{2,1,0:T(4,128)} %logits.1), calls=%async_computation | async-start | bytes 524288 | tf_op jit(solution)/shard_map/all_to_all | solution.py:227
  75.6 8.7 %all-to-all-done.table_ref = f32[32,4,512]{2,1,0:T(4,128)S(1)} async-done(((f32[32,4,512]{2,1,0:T(4,128)}), f32[32,4,512]{2,1,0:T(4,128)S(1)}, u32[]{:S(2)}, u32[]{:S(2)}) %all-to-all-start) | async-done | bytes 262176 | tf_op jit(solution)/shard_map/all_to_all | solution.py:227
  84.6 33.4 %all-gather.1.stats_ref = f32[16,4,128]{2,1,0:T(4,128)S(1)} all-gather(f32[1,4,128]{2,1,0:T(4,128)S(1)} %bitcast.48), channel_id=2, replica_groups=mesh['rows'=32,'vocab'=16] {'vocab'}, dimensions={0}, use_global_device_ids=true | all-gather | bytes 34816 | tf_op jit(solution)/shard_map/all_gather | solution.py:238
  118.0 1.1 scores.1
  119.1 4.1 %collective-permute-start.14 = (f32[4,128]{1,0:T(4,128)S(1)}, f32[4,128]{1,0:T(4,128)S(1)}, u32[]{:S(2)}, u32[]{:S(2)}) collective-permute-start(f32[4,128]{1,0:T(4,128)S(1)} %get-tuple-element.10), channel_id=1, source_target_pairs={{1,0},{2,1},{3,2},{4,3},{5,4},{6,5},{7,6},{8,7},{9,8},{10,9},{11,1... | collective-permute-start | bytes 6152 | tf_op jit(solution)/shard_map/ppermute | solution.py:252
  123.3 3.4 %collective-permute-start.15 = (f32[4,128]{1,0:T(4,128)S(1)}, f32[4,128]{1,0:T(4,128)S(1)}, u32[]{:S(2)}, u32[]{:S(2)}) collective-permute-start(f32[4,128]{1,0:T(4,128)S(1)} %get-tuple-element.10), channel_id=1, source_target_pairs={{2,0},{3,1},{4,2},{5,3},{6,4},{7,5},{8,6},{9,7},{10,8},{11,9},{12,... | collective-permute-start | bytes 6152 | tf_op jit(solution)/shard_map/ppermute | solution.py:252
  126.6 4.0 %collective-permute-start.16 = (f32[4,128]{1,0:T(4,128)S(1)}, f32[4,128]{1,0:T(4,128)S(1)}, u32[]{:S(2)}, u32[]{:S(2)}) collective-permute-start(f32[4,128]{1,0:T(4,128)S(1)} %get-tuple-element.10), channel_id=1, source_target_pairs={{3,0},{4,1},{5,2},{6,3},{7,4},{8,5},{9,6},{10,7},{11,8},{12,9},{13... | collective-permute-start | bytes 6152 | tf_op jit(solution)/shard_map/ppermute | solution.py:252
  130.7 5.3 %collective-permute-start.17 = (f32[4,128]{1,0:T(4,128)S(1)}, f32[4,128]{1,0:T(4,128)S(1)}, u32[]{:S(2)}, u32[]{:S(2)}) collective-permute-start(f32[4,128]{1,0:T(4,128)S(1)} %get-tuple-element.10), channel_id=1, source_target_pairs={{4,0},{5,1},{6,2},{7,3},{8,4},{9,5},{10,6},{11,7},{12,8},{13,9},{1... | collective-permute-start | bytes 6152 | tf_op jit(solution)/shard_map/ppermute | solution.py:252
  135.9 4.7 %collective-permute-start.18 = (f32[4,128]{1,0:T(4,128)S(1)}, f32[4,128]{1,0:T(4,128)S(1)}, u32[]{:S(2)}, u32[]{:S(2)}) collective-permute-start(f32[4,128]{1,0:T(4,128)S(1)} %get-tuple-element.10), channel_id=1, source_target_pairs={{5,0},{6,1},{7,2},{8,3},{9,4},{10,5},{11,6},{12,7},{13,8},{14,9},{... | collective-permute-start | bytes 6152 | tf_op jit(solution)/shard_map/ppermute | solution.py:252
  142.0 7.6 %collective-permute-start.19 = (f32[4,128]{1,0:T(4,128)S(1)}, f32[4,128]{1,0:T(4,128)S(1)}, u32[]{:S(2)}, u32[]{:S(2)}) collective-permute-start(f32[4,128]{1,0:T(4,128)S(1)} %get-tuple-element.10), channel_id=1, source_target_pairs={{6,0},{7,1},{8,2},{9,3},{10,4},{11,5},{12,6},{13,7},{14,8},{15,9},... | collective-permute-start | bytes 6152 | tf_op jit(solution)/shard_map/ppermute | solution.py:252
  149.6 4.4 %collective-permute-start.20 = (f32[4,128]{1,0:T(4,128)S(1)}, f32[4,128]{1,0:T(4,128)S(1)}, u32[]{:S(2)}, u32[]{:S(2)}) collective-permute-start(f32[4,128]{1,0:T(4,128)S(1)} %get-tuple-element.10), channel_id=1, source_target_pairs={{7,0},{8,1},{9,2},{10,3},{11,4},{12,5},{13,6},{14,7},{15,8},{0,9},... | collective-permute-start | bytes 6152 | tf_op jit(solution)/shard_map/ppermute | solution.py:252
  154.0 8.5 %collective-permute-start.21 = (f32[4,128]{1,0:T(4,128)S(1)}, f32[4,128]{1,0:T(4,128)S(1)}, u32[]{:S(2)}, u32[]{:S(2)}) collective-permute-start(f32[4,128]{1,0:T(4,128)S(1)} %get-tuple-element.10), channel_id=1, source_target_pairs={{8,0},{9,1},{10,2},{11,3},{12,4},{13,5},{14,6},{15,7},{0,8},{1,9},... | collective-permute-start | bytes 6152 | tf_op jit(solution)/shard_map/ppermute | solution.py:252
  162.5 5.6 %collective-permute-start.22 = (f32[4,128]{1,0:T(4,128)S(1)}, f32[4,128]{1,0:T(4,128)S(1)}, u32[]{:S(2)}, u32[]{:S(2)}) collective-permute-start(f32[4,128]{1,0:T(4,128)S(1)} %get-tuple-element.10), channel_id=1, source_target_pairs={{9,0},{10,1},{11,2},{12,3},{13,4},{14,5},{15,6},{0,7},{1,8},{2,9},... | collective-permute-start | bytes 6152 | tf_op jit(solution)/shard_map/ppermute | solution.py:252
  168.2 6.4 %collective-permute-start.23 = (f32[4,128]{1,0:T(4,128)S(1)}, f32[4,128]{1,0:T(4,128)S(1)}, u32[]{:S(2)}, u32[]{:S(2)}) collective-permute-start(f32[4,128]{1,0:T(4,128)S(1)} %get-tuple-element.10), channel_id=1, source_target_pairs={{10,0},{11,1},{12,2},{13,3},{14,4},{15,5},{0,6},{1,7},{2,8},{3,9},... | collective-permute-start | bytes 6152 | tf_op jit(solution)/shard_map/ppermute | solution.py:252
  174.6 4.9 %collective-permute-start.24 = (f32[4,128]{1,0:T(4,128)S(1)}, f32[4,128]{1,0:T(4,128)S(1)}, u32[]{:S(2)}, u32[]{:S(2)}) collective-permute-start(f32[4,128]{1,0:T(4,128)S(1)} %get-tuple-element.10), channel_id=1, source_target_pairs={{11,0},{12,1},{13,2},{14,3},{15,4},{0,5},{1,6},{2,7},{3,8},{4,9},{... | collective-permute-start | bytes 6152 | tf_op jit(solution)/shard_map/ppermute | solution.py:252
  179.6 4.1 %collective-permute-start.25 = (f32[4,128]{1,0:T(4,128)S(1)}, f32[4,128]{1,0:T(4,128)S(1)}, u32[]{:S(2)}, u32[]{:S(2)}) collective-permute-start(f32[4,128]{1,0:T(4,128)S(1)} %get-tuple-element.10), channel_id=1, source_target_pairs={{12,0},{13,1},{14,2},{15,3},{0,4},{1,5},{2,6},{3,7},{4,8},{5,9},{6... | collective-permute-start | bytes 6152 | tf_op jit(solution)/shard_map/ppermute | solution.py:252
  183.7 5.2 %collective-permute-start.26 = (f32[4,128]{1,0:T(4,128)S(1)}, f32[4,128]{1,0:T(4,128)S(1)}, u32[]{:S(2)}, u32[]{:S(2)}) collective-permute-start(f32[4,128]{1,0:T(4,128)S(1)} %get-tuple-element.10), channel_id=1, source_target_pairs={{13,0},{14,1},{15,2},{0,3},{1,4},{2,5},{3,6},{4,7},{5,8},{6,9},{7,... | collective-permute-start | bytes 6152 | tf_op jit(solution)/shard_map/ppermute | solution.py:252
  188.9 5.6 %collective-permute-start.27 = (f32[4,128]{1,0:T(4,128)S(1)}, f32[4,128]{1,0:T(4,128)S(1)}, u32[]{:S(2)}, u32[]{:S(2)}) collective-permute-start(f32[4,128]{1,0:T(4,128)S(1)} %get-tuple-element.10), channel_id=1, source_target_pairs={{14,0},{15,1},{0,2},{1,3},{2,4},{3,5},{4,6},{5,7},{6,8},{7,9},{8,1... | collective-permute-start | bytes 6152 | tf_op jit(solution)/shard_map/ppermute | solution.py:252
  194.5 2.9 %collective-permute-start.28 = (f32[4,128]{1,0:T(4,128)S(1)}, f32[4,128]{1,0:T(4,128)S(1)}, u32[]{:S(2)}, u32[]{:S(2)}) collective-permute-start(f32[4,128]{1,0:T(4,128)S(1)} %get-tuple-element.10), channel_id=1, source_target_pairs={{15,0},{0,1},{1,2},{2,3},{3,4},{4,5},{5,6},{6,7},{7,8},{8,9},{9,10... | collective-permute-start | bytes 6152 | tf_op jit(solution)/shard_map/ppermute | solution.py:252
  197.5 2.5 %collective-permute-done.28 = f32[4,128]{1,0:T(4,128)S(1)} collective-permute-done((f32[4,128]{1,0:T(4,128)S(1)}, f32[4,128]{1,0:T(4,128)S(1)}, u32[]{:S(2)}, u32[]{:S(2)}) %collective-permute-start.28) | collective-permute-done | bytes 2080 | tf_op jit(solution)/shard_map/ppermute | solution.py:252
  200.0 1.4 merge.1
  (74 shorter events, 8.9 us)
Async XLA Ops:
  0.6 74.8 %copy-start = (s32[128]{0:T(128)S(1)}, s32[128]{0:T(128)}, u32[]{:S(2)}) copy-start(s32[128]{0:T(128)} %param.17) | copy-start | bytes 1540
  2.1 0.8 copy-start.3
  3.0 0.7 copy-start.4
  3.9 3.1 %collective-permute-start = (bf16[2,4,2944]{2,1,0:T(4,128)(2,1)S(1)}, bf16[2,4,2944]{2,1,0:T(4,128)(2,1)S(1)}, u32[]{:S(2)}, u32[]{:S(2)}) collective-permute-start(bf16[2,4,2944]{2,1,0:T(4,128)(2,1)S(1)} %get-tuple-element.9), channel_id=1, source_target_pairs={{16,0},{0,16},{48,32},{32,48},{80,64},{64,80},{112,96},{96,112},{1... | collective-permute-start | bytes 141320 | tf_op jit(solution)/shard_map/ppermute | solution.py:34
  7.1 18.3 %collective-permute-start.1 = (bf16[8,2944]{1,0:T(8,128)(2,1)S(1)}, bf16[8,2944]{1,0:T(8,128)(2,1)S(1)}, u32[]{:S(2)}, u32[]{:S(2)}) collective-permute-start(bf16[8,2944]{1,0:T(8,128)(2,1)S(1)} %get-tuple-element.23), channel_id=1, source_target_pairs={{32,0},{48,16},{64,32},{80,48},{96,64},{112,80},{0,96},{16,112},{1... | collective-permute-start | bytes 141320 | tf_op jit(solution)/shard_map/ppermute | solution.py:34
  11.8 16.5 %collective-permute-start.2 = (bf16[8,2944]{1,0:T(8,128)(2,1)S(1)}, bf16[8,2944]{1,0:T(8,128)(2,1)S(1)}, u32[]{:S(2)}, u32[]{:S(2)}) collective-permute-start(bf16[8,2944]{1,0:T(8,128)(2,1)S(1)} %get-tuple-element.23), channel_id=1, source_target_pairs={{64,0},{80,16},{96,32},{112,48},{0,64},{16,80},{32,96},{48,112},{1... | collective-permute-start | bytes 141320 | tf_op jit(solution)/shard_map/ppermute | solution.py:34
  14.5 13.8 %collective-permute-start.3 = (bf16[8,2944]{1,0:T(8,128)(2,1)S(1)}, bf16[8,2944]{1,0:T(8,128)(2,1)S(1)}, u32[]{:S(2)}, u32[]{:S(2)}) collective-permute-start(bf16[8,2944]{1,0:T(8,128)(2,1)S(1)} %get-tuple-element.23), channel_id=1, source_target_pairs={{96,0},{112,16},{0,32},{16,48},{32,64},{48,80},{64,96},{80,112},{2... | collective-permute-start | bytes 141320 | tf_op jit(solution)/shard_map/ppermute | solution.py:34
  18.0 18.2 %collective-permute-start.7 = (bf16[8,2944]{1,0:T(8,128)(2,1)S(1)}, bf16[8,2944]{1,0:T(8,128)(2,1)S(1)}, u32[]{:S(2)}, u32[]{:S(2)}) collective-permute-start(bf16[8,2944]{1,0:T(8,128)(2,1)S(1)} %get-tuple-element.22), channel_id=1, source_target_pairs={{128,0},{144,16},{160,32},{176,48},{192,64},{208,80},{224,96},{240... | collective-permute-start | bytes 141320 | tf_op jit(solution)/shard_map/ppermute | solution.py:34
  22.9 15.2 %collective-permute-start.8 = (bf16[8,2944]{1,0:T(8,128)(2,1)S(1)}, bf16[8,2944]{1,0:T(8,128)(2,1)S(1)}, u32[]{:S(2)}, u32[]{:S(2)}) collective-permute-start(bf16[8,2944]{1,0:T(8,128)(2,1)S(1)} %get-tuple-element.22), channel_id=1, source_target_pairs={{256,0},{272,16},{288,32},{304,48},{320,64},{336,80},{352,96},{368... | collective-permute-start | bytes 141320 | tf_op jit(solution)/shard_map/ppermute | solution.py:34
  25.4 12.7 %collective-permute-start.9 = (bf16[8,2944]{1,0:T(8,128)(2,1)S(1)}, bf16[8,2944]{1,0:T(8,128)(2,1)S(1)}, u32[]{:S(2)}, u32[]{:S(2)}) collective-permute-start(bf16[8,2944]{1,0:T(8,128)(2,1)S(1)} %get-tuple-element.22), channel_id=1, source_target_pairs={{384,0},{400,16},{416,32},{432,48},{448,64},{464,80},{480,96},{496... | collective-permute-start | bytes 141320 | tf_op jit(solution)/shard_map/ppermute | solution.py:34
  28.4 19.6 %collective-permute-start.4 = (bf16[32,2944]{1,0:T(8,128)(2,1)S(1)}, bf16[32,2944]{1,0:T(8,128)(2,1)S(1)}, u32[]{:S(2)}, u32[]{:S(2)}) collective-permute-start(bf16[32,2944]{1,0:T(8,128)(2,1)S(1)} %pad_maximum_fusion), channel_id=1, source_target_pairs={{128,0},{144,16},{160,32},{176,48},{192,64},{208,80},{224,96},{240... | collective-permute-start | bytes 565256 | tf_op jit(solution)/shard_map/ppermute | solution.py:34
  32.5 18.0 %collective-permute-start.5 = (bf16[32,2944]{1,0:T(8,128)(2,1)S(1)}, bf16[32,2944]{1,0:T(8,128)(2,1)S(1)}, u32[]{:S(2)}, u32[]{:S(2)}) collective-permute-start(bf16[32,2944]{1,0:T(8,128)(2,1)S(1)} %pad_maximum_fusion), channel_id=1, source_target_pairs={{256,0},{272,16},{288,32},{304,48},{320,64},{336,80},{352,96},{368... | collective-permute-start | bytes 565256 | tf_op jit(solution)/shard_map/ppermute | solution.py:34
  36.2 15.1 %collective-permute-start.6 = (bf16[32,2944]{1,0:T(8,128)(2,1)S(1)}, bf16[32,2944]{1,0:T(8,128)(2,1)S(1)}, u32[]{:S(2)}, u32[]{:S(2)}) collective-permute-start(bf16[32,2944]{1,0:T(8,128)(2,1)S(1)} %pad_maximum_fusion), channel_id=1, source_target_pairs={{384,0},{400,16},{416,32},{432,48},{448,64},{464,80},{480,96},{496... | collective-permute-start | bytes 565256 | tf_op jit(solution)/shard_map/ppermute | solution.py:34
  38.1 24.8 %copy-start.1 = (bf16[192,8192]{1,0:T(8,128)(2,1)S(1)}, bf16[192,8192]{1,0:T(8,128)(2,1)}, u32[]{:S(2)}) copy-start(bf16[192,8192]{1,0:T(8,128)(2,1)} %he_ref.3) | copy-start | bytes 9437188
  38.2 21.2 %copy-start.6 = (s32[128]{0:T(128)S(1)}, s32[128]{0:T(128)}, u32[]{:S(2)}) copy-start(s32[128]{0:T(128)} %param.16) | copy-start | bytes 1540
  38.2 16.3 %collective-permute-start.10 = (bf16[32,2944]{1,0:T(8,128)(2,1)S(1)}, bf16[32,2944]{1,0:T(8,128)(2,1)S(1)}, u32[]{:S(2)}, u32[]{:S(2)}) collective-permute-start(bf16[32,2944]{1,0:T(8,128)(2,1)S(1)} %pad_maximum_fusion.1), channel_id=1, source_target_pairs={{32,0},{48,16},{64,32},{80,48},{96,64},{112,80},{0,96},{16,112},{1... | collective-permute-start | bytes 565256 | tf_op jit(solution)/shard_map/ppermute | solution.py:34
  42.7 12.5 %collective-permute-start.11 = (bf16[32,2944]{1,0:T(8,128)(2,1)S(1)}, bf16[32,2944]{1,0:T(8,128)(2,1)S(1)}, u32[]{:S(2)}, u32[]{:S(2)}) collective-permute-start(bf16[32,2944]{1,0:T(8,128)(2,1)S(1)} %pad_maximum_fusion.1), channel_id=1, source_target_pairs={{64,0},{80,16},{96,32},{112,48},{0,64},{16,80},{32,96},{48,112},{1... | collective-permute-start | bytes 565256 | tf_op jit(solution)/shard_map/ppermute | solution.py:34
  46.7 16.2 %copy-start.5 = (s32[192]{0:T(256)S(1)}, s32[192]{0:T(256)}, u32[]{:S(2)}) copy-start(s32[192]{0:T(256)} %param.15) | copy-start | bytes 2308
  48.0 8.7 %collective-permute-start.12 = (bf16[32,2944]{1,0:T(8,128)(2,1)S(1)}, bf16[32,2944]{1,0:T(8,128)(2,1)S(1)}, u32[]{:S(2)}, u32[]{:S(2)}) collective-permute-start(bf16[32,2944]{1,0:T(8,128)(2,1)S(1)} %pad_maximum_fusion.1), channel_id=1, source_target_pairs={{96,0},{112,16},{0,32},{16,48},{32,64},{48,80},{64,96},{80,112},{2... | collective-permute-start | bytes 565256 | tf_op jit(solution)/shard_map/ppermute | solution.py:34
  57.4 5.5 %collective-permute-start.13 = (bf16[256,2944]{1,0:T(8,128)(2,1)}, bf16[256,2944]{1,0:T(8,128)(2,1)}, u32[]{:S(2)}, u32[]{:S(2)}) collective-permute-start(bf16[256,2944]{1,0:T(8,128)(2,1)} %constant_dynamic-update-slice_fusion.mine_ref), channel_id=1, source_target_pairs={{16,0},{0,16},{48,32},{32,48},{80,64},{64,80},{112,96},{96,112},{1... | collective-permute-start | bytes 4521992 | tf_op jit(solution)/shard_map/ppermute | solution.py:34
  62.9 1.3 copy-start.2
  68.7 15.6 %all-to-all-start = ((f32[32,4,512]{2,1,0:T(4,128)}), f32[32,4,512]{2,1,0:T(4,128)S(1)}, u32[]{:S(2)}, u32[]{:S(2)}) async-start(f32[32,4,512]{2,1,0:T(4,128)} %logits.1), calls=%async_computation | async-start | bytes 524288 | tf_op jit(solution)/shard_map/all_to_all | solution.py:227
  119.1 22.8 %collective-permute-start.14 = (f32[4,128]{1,0:T(4,128)S(1)}, f32[4,128]{1,0:T(4,128)S(1)}, u32[]{:S(2)}, u32[]{:S(2)}) collective-permute-start(f32[4,128]{1,0:T(4,128)S(1)} %get-tuple-element.10), channel_id=1, source_target_pairs={{1,0},{2,1},{3,2},{4,3},{5,4},{6,5},{7,6},{8,7},{9,8},{10,9},{11,1... | collective-permute-start | bytes 6152 | tf_op jit(solution)/shard_map/ppermute | solution.py:252
  123.3 26.3 %collective-permute-start.15 = (f32[4,128]{1,0:T(4,128)S(1)}, f32[4,128]{1,0:T(4,128)S(1)}, u32[]{:S(2)}, u32[]{:S(2)}) collective-permute-start(f32[4,128]{1,0:T(4,128)S(1)} %get-tuple-element.10), channel_id=1, source_target_pairs={{2,0},{3,1},{4,2},{5,3},{6,4},{7,5},{8,6},{9,7},{10,8},{11,9},{12,... | collective-permute-start | bytes 6152 | tf_op jit(solution)/shard_map/ppermute | solution.py:252
  126.6 27.3 %collective-permute-start.16 = (f32[4,128]{1,0:T(4,128)S(1)}, f32[4,128]{1,0:T(4,128)S(1)}, u32[]{:S(2)}, u32[]{:S(2)}) collective-permute-start(f32[4,128]{1,0:T(4,128)S(1)} %get-tuple-element.10), channel_id=1, source_target_pairs={{3,0},{4,1},{5,2},{6,3},{7,4},{8,5},{9,6},{10,7},{11,8},{12,9},{13... | collective-permute-start | bytes 6152 | tf_op jit(solution)/shard_map/ppermute | solution.py:252
  130.7 31.9 %collective-permute-start.17 = (f32[4,128]{1,0:T(4,128)S(1)}, f32[4,128]{1,0:T(4,128)S(1)}, u32[]{:S(2)}, u32[]{:S(2)}) collective-permute-start(f32[4,128]{1,0:T(4,128)S(1)} %get-tuple-element.10), channel_id=1, source_target_pairs={{4,0},{5,1},{6,2},{7,3},{8,4},{9,5},{10,6},{11,7},{12,8},{13,9},{1... | collective-permute-start | bytes 6152 | tf_op jit(solution)/shard_map/ppermute | solution.py:252
  135.9 32.2 %collective-permute-start.18 = (f32[4,128]{1,0:T(4,128)S(1)}, f32[4,128]{1,0:T(4,128)S(1)}, u32[]{:S(2)}, u32[]{:S(2)}) collective-permute-start(f32[4,128]{1,0:T(4,128)S(1)} %get-tuple-element.10), channel_id=1, source_target_pairs={{5,0},{6,1},{7,2},{8,3},{9,4},{10,5},{11,6},{12,7},{13,8},{14,9},{... | collective-permute-start | bytes 6152 | tf_op jit(solution)/shard_map/ppermute | solution.py:252
  142.0 32.6 %collective-permute-start.19 = (f32[4,128]{1,0:T(4,128)S(1)}, f32[4,128]{1,0:T(4,128)S(1)}, u32[]{:S(2)}, u32[]{:S(2)}) collective-permute-start(f32[4,128]{1,0:T(4,128)S(1)} %get-tuple-element.10), channel_id=1, source_target_pairs={{6,0},{7,1},{8,2},{9,3},{10,4},{11,5},{12,6},{13,7},{14,8},{15,9},... | collective-permute-start | bytes 6152 | tf_op jit(solution)/shard_map/ppermute | solution.py:252
  149.6 30.0 %collective-permute-start.20 = (f32[4,128]{1,0:T(4,128)S(1)}, f32[4,128]{1,0:T(4,128)S(1)}, u32[]{:S(2)}, u32[]{:S(2)}) collective-permute-start(f32[4,128]{1,0:T(4,128)S(1)} %get-tuple-element.10), channel_id=1, source_target_pairs={{7,0},{8,1},{9,2},{10,3},{11,4},{12,5},{13,6},{14,7},{15,8},{0,9},... | collective-permute-start | bytes 6152 | tf_op jit(solution)/shard_map/ppermute | solution.py:252
  154.0 29.6 %collective-permute-start.21 = (f32[4,128]{1,0:T(4,128)S(1)}, f32[4,128]{1,0:T(4,128)S(1)}, u32[]{:S(2)}, u32[]{:S(2)}) collective-permute-start(f32[4,128]{1,0:T(4,128)S(1)} %get-tuple-element.10), channel_id=1, source_target_pairs={{8,0},{9,1},{10,2},{11,3},{12,4},{13,5},{14,6},{15,7},{0,8},{1,9},... | collective-permute-start | bytes 6152 | tf_op jit(solution)/shard_map/ppermute | solution.py:252
  162.5 26.3 %collective-permute-start.22 = (f32[4,128]{1,0:T(4,128)S(1)}, f32[4,128]{1,0:T(4,128)S(1)}, u32[]{:S(2)}, u32[]{:S(2)}) collective-permute-start(f32[4,128]{1,0:T(4,128)S(1)} %get-tuple-element.10), channel_id=1, source_target_pairs={{9,0},{10,1},{11,2},{12,3},{13,4},{14,5},{15,6},{0,7},{1,8},{2,9},... | collective-permute-start | bytes 6152 | tf_op jit(solution)/shard_map/ppermute | solution.py:252
  168.2 26.3 %collective-permute-start.23 = (f32[4,128]{1,0:T(4,128)S(1)}, f32[4,128]{1,0:T(4,128)S(1)}, u32[]{:S(2)}, u32[]{:S(2)}) collective-permute-start(f32[4,128]{1,0:T(4,128)S(1)} %get-tuple-element.10), channel_id=1, source_target_pairs={{10,0},{11,1},{12,2},{13,3},{14,4},{15,5},{0,6},{1,7},{2,8},{3,9},... | collective-permute-start | bytes 6152 | tf_op jit(solution)/shard_map/ppermute | solution.py:252
  174.6 22.9 %collective-permute-start.24 = (f32[4,128]{1,0:T(4,128)S(1)}, f32[4,128]{1,0:T(4,128)S(1)}, u32[]{:S(2)}, u32[]{:S(2)}) collective-permute-start(f32[4,128]{1,0:T(4,128)S(1)} %get-tuple-element.10), channel_id=1, source_target_pairs={{11,0},{12,1},{13,2},{14,3},{15,4},{0,5},{1,6},{2,7},{3,8},{4,9},{... | collective-permute-start | bytes 6152 | tf_op jit(solution)/shard_map/ppermute | solution.py:252
  179.6 17.9 %collective-permute-start.25 = (f32[4,128]{1,0:T(4,128)S(1)}, f32[4,128]{1,0:T(4,128)S(1)}, u32[]{:S(2)}, u32[]{:S(2)}) collective-permute-start(f32[4,128]{1,0:T(4,128)S(1)} %get-tuple-element.10), channel_id=1, source_target_pairs={{12,0},{13,1},{14,2},{15,3},{0,4},{1,5},{2,6},{3,7},{4,8},{5,9},{6... | collective-permute-start | bytes 6152 | tf_op jit(solution)/shard_map/ppermute | solution.py:252
  183.7 13.8 %collective-permute-start.26 = (f32[4,128]{1,0:T(4,128)S(1)}, f32[4,128]{1,0:T(4,128)S(1)}, u32[]{:S(2)}, u32[]{:S(2)}) collective-permute-start(f32[4,128]{1,0:T(4,128)S(1)} %get-tuple-element.10), channel_id=1, source_target_pairs={{13,0},{14,1},{15,2},{0,3},{1,4},{2,5},{3,6},{4,7},{5,8},{6,9},{7,... | collective-permute-start | bytes 6152 | tf_op jit(solution)/shard_map/ppermute | solution.py:252
  188.9 8.6 %collective-permute-start.27 = (f32[4,128]{1,0:T(4,128)S(1)}, f32[4,128]{1,0:T(4,128)S(1)}, u32[]{:S(2)}, u32[]{:S(2)}) collective-permute-start(f32[4,128]{1,0:T(4,128)S(1)} %get-tuple-element.10), channel_id=1, source_target_pairs={{14,0},{15,1},{0,2},{1,3},{2,4},{3,5},{4,6},{5,7},{6,8},{7,9},{8,1... | collective-permute-start | bytes 6152 | tf_op jit(solution)/shard_map/ppermute | solution.py:252
  194.5 5.5 %collective-permute-start.28 = (f32[4,128]{1,0:T(4,128)S(1)}, f32[4,128]{1,0:T(4,128)S(1)}, u32[]{:S(2)}, u32[]{:S(2)}) collective-permute-start(f32[4,128]{1,0:T(4,128)S(1)} %get-tuple-element.10), channel_id=1, source_target_pairs={{15,0},{0,1},{1,2},{2,3},{3,4},{4,5},{5,6},{6,7},{7,8},{8,9},{9,10... | collective-permute-start | bytes 6152 | tf_op jit(solution)/shard_map/ppermute | solution.py:252

commit v2 on v1

v2 whole, which is shorter than its diff:
```python
import functools

import jax
import jax.numpy as jnp
from jax import lax
from jax.experimental import pallas as pl
from jax.experimental.pallas import tpu as pltpu
from jax.sharding import PartitionSpec as P

TOP = 4
NC = 2

masked_floor = -1e30
dead_below = -5e29
penalty_slope = 2.0
norm_epsilon = 1e-06

VMEM = pl.BlockSpec(memory_space=pltpu.VMEM)
SMEM = pl.BlockSpec(memory_space=pltpu.SMEM)
PARAMS = pltpu.CompilerParams(vmem_limit_bytes=40 * 1024 * 1024)


def norm_kernel(he_ref, ge_ref, ha_ref, ga_ref, out_ref):
    own, quarters = he_ref.shape[0], []
    for hidden, gains in ((he_ref, ge_ref), (ha_ref, ga_ref)):
        values = hidden[...].astype(jnp.float32)
        gain = gains[...].astype(jnp.float32)
        mean = jnp.mean(values * values, axis=-1, keepdims=True)
        values = values * lax.rsqrt(mean + norm_epsilon)
        chunks = [
            (values[:, 128 * i:128 * i + 128] * gain[i:i + 1, :]).astype(jnp.bfloat16)
            for i in range(values.shape[1] // 128)
        ]
        each = len(chunks) // 4
        quarters.append([chunks[each * q:each * q + each] for q in range(4)])
    for core in range(NC):
        for p in range(2):
            q = 2 * core + p
            for i, chunk in enumerate(quarters[0][q] + quarters[1][q]):
                for dest in range(core, out_ref.shape[0], NC):
                    out_ref[dest, own * p:own * p + own, 128 * i:128 * i + 128] = chunk


def half_logits(core, part_ref, he_ref, ha_ref, model):
    head = (he_ref, ha_ref)[model]
    qe, qa = he_ref.shape[1] // 4, ha_ref.shape[1] // 4
    low, size = ((0, qe), (qe, qa))[model]
    sums = []
    for p in range(2):
        columns = pl.ds(pl.multiple_of((2 * core + p) * size, 128), size)
        sums.append(lax.dot_general(
            part_ref[:, low:low + size], head[:, columns], (((1,), (1,)), ((), ())),
            preferred_element_type=jnp.float32,
        ))
    return sums


def first_kernel(pos_ref, part_ref, he_ref, ha_ref, out_ref):
    for model in range(2):
        for p, total in enumerate(half_logits(pos_ref[0], part_ref, he_ref, ha_ref, model)):
            out_ref[model, p] = total


def second_kernel(pos_ref, part_ref, he_ref, ha_ref, first_ref, live_ref, ids_ref, out_ref, acc_ref):
    width = he_ref.shape[0]
    own = out_ref.shape[1]
    for model in range(2):
        for p, total in enumerate(half_logits(1 - pos_ref[0], part_ref, he_ref, ha_ref, model)):
            acc_ref[model, p] = total + first_ref[model, p]
    live = live_ref[...] == 1
    positions = pos_ref[1] + lax.broadcasted_iota(jnp.int32, (1, width), 1)
    for owner in range(out_ref.shape[0]):
        at = 2 * own * owner
        hits = ids_ref[owner] == positions
        for model in range(2):
            logits = acc_ref[model, 0, at:at + own, :] + acc_ref[model, 1, at + own:at + 2 * own, :]
            pick = jnp.sum(jnp.where(hits, logits, 0.0), axis=1, keepdims=True)
            low = 256 * model
            out_ref[owner, :, low:low + width] = jnp.where(live, logits, masked_floor)
            out_ref[owner, :, low + width:low + 256] = jnp.broadcast_to(pick, (own, 256 - width))


def lanes_of(columns, shape):
    lane = lax.broadcasted_iota(jnp.int32, shape, len(shape) - 1)
    result = jnp.zeros(shape, jnp.float32)
    for i, column in enumerate(columns):
        result = jnp.where(lane == i, column, result)
    return result


def lane_at(values, i):
    lane = lax.broadcasted_iota(jnp.int32, values.shape, values.ndim - 1)
    return jnp.sum(jnp.where(lane == i, values, 0.0), axis=-1, keepdims=True)


def stats_kernel(width, table_ref, out_ref):
    columns = []
    for model in range(2):
        part = table_ref[:, :, 256 * model:256 * model + 256]
        real = lax.broadcasted_iota(jnp.int32, part.shape, 2) < width
        peak = jnp.max(jnp.max(jnp.where(real, part, masked_floor), axis=0), axis=1, keepdims=True)
        total = jnp.sum(jnp.where(real, jnp.exp(part - peak[None]), 0.0), axis=0)
        total = jnp.sum(total, axis=1, keepdims=True)
        pick = lane_at(jnp.sum(part, axis=0), width)
        columns.append((peak, total, pick))
    (pe, te, ce), (pa, ta, ca) = columns
    stats = lanes_of([pe, pa, te, ta, ce, ca], out_ref.shape[1:])
    for plane in range(out_ref.shape[0]):
        out_ref[plane] = stats


def best_of(levels):
    lane = lax.broadcasted_iota(jnp.int32, levels[0].shape, 1)
    found = []
    for _ in range(TOP):
        top = jnp.max(levels[0], axis=1, keepdims=True)
        found.append(top)
        at = jnp.min(jnp.where(levels[0] == top, lane, lane.shape[1]), axis=1, keepdims=True)
        hit = lane == at
        lower = levels[1:] + [jnp.full_like(levels[0], -jnp.inf)]
        levels = [jnp.where(hit, low, level) for level, low in zip(levels, lower)]
    return found


def sorted_levels(parts):
    levels = [jnp.full_like(parts[0], -jnp.inf)] * TOP
    for part in parts:
        for i in range(TOP):
            levels[i], part = jnp.maximum(levels[i], part), jnp.minimum(levels[i], part)
    return levels


def score_kernel(width, table_ref, stats_ref, gap_ref, best_ref, peaks_ref, chosen_ref):
    stats = stats_ref[...]
    peak_e, peak_a, sum_e, sum_a, pick_e, pick_a = [lane_at(stats, i) for i in range(6)]

    def total_of(peaks, sums):
        peak = jnp.max(peaks, axis=0)
        return peak, peak + jnp.log(jnp.sum(sums * jnp.exp(peaks - peak[None]), axis=0))

    peak_e, log_total_e = total_of(peak_e, sum_e)
    peak_a, log_total_a = total_of(peak_a, sum_a)
    cut = peak_e - log_total_e - gap_ref[...].astype(jnp.float32) * 0.1

    def score(logits_e, logits_a):
        logprob_e = logits_e - log_total_e
        logprob_a = logits_a - log_total_a
        return logprob_e - logprob_a - penalty_slope * jnp.maximum(cut - logprob_e, 0.0)

    peaks_ref[...] = lanes_of([peak_e - log_total_e, peak_a - log_total_a], peaks_ref.shape)
    chosen_ref[...] = score(jnp.sum(pick_e, axis=0), jnp.sum(pick_a, axis=0))
    real = lax.broadcasted_iota(jnp.int32, (table_ref.shape[1], 256), 1) < width
    parts = []
    for source in range(table_ref.shape[0]):
        e = table_ref[source, :, 0:256]
        a = table_ref[source, :, 256:512]
        parts.append(jnp.where(real & (e > dead_below), score(e, a), masked_floor))
    best = lanes_of(best_of(sorted_levels(parts)), best_ref.shape[1:])
    for plane in range(best_ref.shape[0]):
        best_ref[plane] = best


def merge_kernel(parts_ref, out_ref):
    shape = parts_ref.shape[1:]
    real = lax.broadcasted_iota(jnp.int32, shape, 1) < TOP
    parts = [jnp.where(real, parts_ref[i], -jnp.inf) for i in range(parts_ref.shape[0])]
    out_ref[...] = lanes_of(best_of(sorted_levels(parts)), out_ref.shape)


def per_device(
    expert_hidden,
    expert_gain,
    expert_head,
    amateur_hidden,
    amateur_gain,
    amateur_head,
    live_mask,
    token_ids,
    plaus_level,
):
    own, depth_e = expert_hidden.shape
    depth_a = amateur_hidden.shape[1]
    width = expert_head.shape[0]
    rows, planes = lax.axis_size("rows"), lax.axis_size("vocab")
    beams = own * rows
    quarter = (depth_e + depth_a) // 4
    row, plane = lax.axis_index("rows"), lax.axis_index("vocab")
    position = jnp.stack([row % NC, (row * planes + plane) * width]).astype(jnp.int32)
    ids = token_ids.reshape(rows, own, 1)
    gap = lax.dynamic_slice_in_dim(plaus_level, row * own, own, 0).reshape(own, 1)

    blocks = pl.pallas_call(
        norm_kernel,
        out_shape=jax.ShapeDtypeStruct((rows, 2 * own, quarter), jnp.bfloat16),
        in_specs=[VMEM] * 4,
        out_specs=VMEM,
        compiler_params=PARAMS,
        name="norms",
    )(expert_hidden, expert_gain.reshape(-1, 128), amateur_hidden, amateur_gain.reshape(-1, 128))
    half = lax.all_to_all(blocks, "rows", 0, 0, tiled=True).reshape(2 * beams, quarter)
    other_half = lax.ppermute(half, "rows", [(r, r ^ 1) for r in range(rows)])
    cost = pl.CostEstimate(
        flops=4 * beams * width * 2 * quarter, bytes_accessed=4 * beams * quarter, transcendentals=0
    )
    first = pl.pallas_call(
        first_kernel,
        out_shape=jax.ShapeDtypeStruct((2, 2, 2 * beams, width), jnp.float32),
        in_specs=[SMEM] + [VMEM] * 3,
        out_specs=VMEM,
        compiler_params=PARAMS,
        cost_estimate=cost,
        name="first_half",
    )(position, half, expert_head, amateur_head)
    table = pl.pallas_call(
        second_kernel,
        out_shape=jax.ShapeDtypeStruct((rows, own, 512), jnp.float32),
        in_specs=[SMEM] + [VMEM] * 6,
        out_specs=VMEM,
        scratch_shapes=[pltpu.VMEM((2, 2, 2 * beams, width), jnp.float32)],
        compiler_params=PARAMS,
        cost_estimate=cost,
        name="second_half",
    )(position, other_half, expert_head, amateur_head, first, live_mask.reshape(1, -1), ids)
    table = lax.all_to_all(table, "rows", 0, 0, tiled=True)

    small = jax.ShapeDtypeStruct((planes, own, 128), jnp.float32)
    stats = pl.pallas_call(
        functools.partial(stats_kernel, width),
        out_shape=small,
        in_specs=[VMEM],
        out_specs=VMEM,
        compiler_params=PARAMS,
        name="stats",
    )(table)
    stats = lax.all_to_all(stats, "vocab", 0, 0, tiled=True)
    best, peaks, chosen = pl.pallas_call(
        functools.partial(score_kernel, width),
        out_shape=(
            small,
            jax.ShapeDtypeStruct((own, 2), jnp.float32),
            jax.ShapeDtypeStruct((own, 1), jnp.float32),
        ),
        in_specs=[VMEM] * 3,
        out_specs=(VMEM,) * 3,
        compiler_params=PARAMS,
        name="scores",
    )(table, stats, gap)
    best = lax.all_to_all(best, "vocab", 0, 0, tiled=True)
    top = pl.pallas_call(
        merge_kernel,
        out_shape=jax.ShapeDtypeStruct((own, TOP), jnp.float32),
        in_specs=[VMEM],
        out_specs=VMEM,
        compiler_params=PARAMS,
        name="merge",
    )(best)
    return top, peaks, chosen.reshape(own)


def solution(mesh):
    in_specs = (
        P("rows", None),
        P(),
        P(("rows", "vocab"), None),
        P("rows", None),
        P(),
        P(("rows", "vocab"), None),
        P(("rows", "vocab")),
        P(),
        P(),
    )
    out_specs = (P("rows", None), P("rows", None), P("rows"))
    return jax.shard_map(
        per_device, mesh=mesh, in_specs=in_specs, out_specs=out_specs, check_vma=False
    )
```

time: 203 us -> 103 us (0.51)
  the two profiles are of different devices: /device:TPU:32 before, /device:TPU:1 now
where the time goes in v2:
time: 103 us; the launch traced here: 102 us
  blocking collectives  44.9 us (44%)
  waiting for transfers between devices  21.4 us (21%)
  starting transfers between devices  18.9 us (18%)
  Pallas kernels  9.55 us (9%)
  local copies, waits for them, and re-layouts  5.43 us (5%)
    all_to_all x1, blocking collectives, per_device(): lax.all_to_all(blocks, 'rows', 0, 0, tiled=True).reshape(2 * beams, quarter)  32.5 us
    all_to_all x1, starting transfers between devices, per_device(): stats = lax.all_to_all(stats, 'vocab', 0, 0, tiled=True)  13.1 us
    all_to_all x1, blocking collectives, per_device(): table = lax.all_to_all(table, 'rows', 0, 0, tiled=True)  12.4 us
    all_to_all x1, waiting for transfers between devices, per_device(): stats = lax.all_to_all(stats, 'vocab', 0, 0, tiled=True)  11.3 us
    all_to_all x1, waiting for transfers between devices, per_device(): best = lax.all_to_all(best, 'vocab', 0, 0, tiled=True)  10.1 us
    unnamed x19, local copies, waits for them, and re-layouts  5.01 us
    all_to_all x1, starting transfers between devices, per_device(): best = lax.all_to_all(best, 'vocab', 0, 0, tiled=True)  3.47 us
    pallas_call x1, Pallas kernels, per_device(): pl.pallas_call(second_kernel, out_shape=jax.ShapeDtypeStruct((rows, own,...  2.58 us
  transfers between devices with their start and end apart: 3, of which 2 were waited for; matrix products, arithmetic and copies ran while one was open for 2% of the time, Pallas kernels for 2%

profile of v2, /device:TPU:1, one launch (start us, length us, event | category | flops | bytes accessed | tf_op | source)
XLA Modules:
  0.0 101.7 jit_solution(9036622435536747910)
XLA Ops:
  0.6 0.0 copy-start
  0.6 0.0 copy-start.3
  0.7 0.8 copy-done.3
  1.5 0.0 copy-start.4
  1.5 0.7 copy-done.4
  2.2 0.0 copy-start.5
  2.2 0.7 copy-done.5
  3.0 0.0 copy-start.6
  3.0 0.7 copy-done.6
  3.7 0.0 copy-start.1
  3.7 0.5 norms.1
  4.2 0.0 copy-start.8
  4.2 32.5 %all_to_all.20 = bf16[32,8,2944]{2,1,0:T(8,128)(2,1)} all-to-all(bf16[32,8,2944]{2,1,0:T(8,128)(2,1)S(1)} %norms.1), channel_id=1, replica_groups=mesh['rows'=32,'vocab'=16] {'rows'}, dimensions={0} | all-to-all | bytes 3014656 | tf_op jit(solution)/shard_map/all_to_all | solution.py:200
  36.8 2.3 %collective-permute-start = (bf16[256,2944]{1,0:T(8,128)(2,1)}, bf16[256,2944]{1,0:T(8,128)(2,1)}, u32[]{:S(2)}, u32[]{:S(2)}) collective-permute-start(bf16[256,2944]{1,0:T(8,128)(2,1)} %bitcast.4.part_ref), channel_id=1, source_target_pairs={{0,16},{16,0},{32,48},{48,32},{64,80},{80,64},{96,112},{112,96},{1... | collective-permute-start | bytes 4521992 | tf_op jit(solution)/shard_map/ppermute | solution.py:201
  39.1 0.0 copy-done.8
  39.1 0.2 reshape.34.ids_ref
  39.4 0.1 pad_add_fusion.pos_ref
  39.4 0.0 copy-done.1
  39.4 0.0 copy-start.2
  39.4 1.3 %copy-done.2 = bf16[192,3584]{1,0:T(8,128)(2,1)S(1)} copy-done((bf16[192,3584]{1,0:T(8,128)(2,1)S(1)}, bf16[192,3584]{1,0:T(8,128)(2,1)}, u32[]{:S(2)}) %copy-start.2) | copy-done | bytes 1376280
  40.8 0.0 copy-start.7
  40.8 2.4 %first_half.1.first_ref = f32[2,2,256,192]{3,2,1,0:T(8,128)S(1)} custom-call(s32[2]{0:T(128)S(1)} %pad_add_fusion.pos_ref, bf16[256,2944]{1,0:T(8,128)(2,1)} %bitcast.4.part_ref, bf16[192,8192]{1,0:T(8,128)(2,1)S(1)} %copy-done.1, bf16[192,3584]{1,0:T(8,128)(2,1)S(1)} %copy-done.2), custom_call_target="tpu_custom_call" | custom-call | flops 578813952 | bytes 1507328 | tf_op jit(solution)/shard_map/first_half/pallas_call | solution.py:205
  43.2 0.0 collective-permute-done.part_ref
  43.2 0.0 copy-done.7
  43.2 2.6 %second_half.1 = f32[32,4,512]{2,1,0:T(4,128)S(1)} custom-call(s32[2]{0:T(128)S(1)} %pad_add_fusion.pos_ref, bf16[256,2944]{1,0:T(8,128)(2,1)} %collective-permute-done.part_ref, bf16[192,8192]{1,0:T(8,128)(2,1)S(1)} %copy-done.1, bf16[192,3584]{1,0:T(8,128)(2,1)S(1)} %copy-done.2, f32[2,2,256,192]{3,2,1,0:T(8,128)S(1)} %first_half.1.first_ref, ...), custom_call_target="tpu_custom_call" | custom-call | flops 578813952 | bytes 1507328 | tf_op jit(solution)/shard_map/second_half/pallas_call | solution.py:214
  45.8 12.4 %all_to_all.21.table_ref = f32[32,4,512]{2,1,0:T(4,128)S(1)} all-to-all(f32[32,4,512]{2,1,0:T(4,128)S(1)} %second_half.1), channel_id=1, replica_groups=mesh['rows'=32,'vocab'=16] {'rows'}, dimensions={0} | all-to-all | bytes 524288 | tf_op jit(solution)/shard_map/all_to_all | solution.py:224
  58.2 0.9 stats.1
  59.1 13.1 %all-to-all-start.2 = ((f32[16,4,128]{2,1,0:T(4,128)}), f32[16,4,128]{2,1,0:T(4,128)S(1)}, u32[]{:S(2)}, u32[]{:S(2)}) async-start(f32[16,4,128]{2,1,0:T(4,128)} %stats.1), calls=%async_computation.2 | async-start | bytes 65536 | tf_op jit(solution)/shard_map/all_to_all | solution.py:235
  72.2 0.0 copy-done
  72.2 0.1 dynamic-slice_bitcast_fusion
  72.3 0.1 copy.16.gap_ref
  72.4 11.3 %all-to-all-done.2.stats_ref = f32[16,4,128]{2,1,0:T(4,128)S(1)} async-done(((f32[16,4,128]{2,1,0:T(4,128)}), f32[16,4,128]{2,1,0:T(4,128)S(1)}, u32[]{:S(2)}, u32[]{:S(2)}) %all-to-all-start.2) | async-done | bytes 32800 | tf_op jit(solution)/shard_map/all_to_all | solution.py:235
  83.7 1.7 %scores.1 = (f32[16,4,128]{2,1,0:T(4,128)}, f32[4,2]{1,0:T(4,128)S(1)}, f32[4,1]{1,0:T(4,128)S(1)}) custom-call(f32[32,4,512]{2,1,0:T(4,128)S(1)} %all_to_all.21.table_ref, f32[16,4,128]{2,1,0:T(4,128)S(1)} %all-to-all-done.2.stats_ref, s32[4,1]{1,0:T(4,128)S(1)} %copy.16.gap_ref), custom_call_target="tpu_custom_call" | custom-call | tf_op jit(solution)/shard_map/scores/pallas_call | solution.py:236
  85.5 3.5 %all-to-all-start.3 = ((f32[16,4,128]{2,1,0:T(4,128)}), f32[16,4,128]{2,1,0:T(4,128)S(1)}, u32[]{:S(2)}, u32[]{:S(2)}) async-start(f32[16,4,128]{2,1,0:T(4,128)} %get-tuple-element.6), calls=%async_computation.3 | async-start | bytes 65536 | tf_op jit(solution)/shard_map/all_to_all | solution.py:248
  88.9 0.6 copy.17
  89.6 0.6 reduce
  90.2 10.1 %all-to-all-done.3.parts_ref = f32[16,4,128]{2,1,0:T(4,128)S(1)} async-done(((f32[16,4,128]{2,1,0:T(4,128)}), f32[16,4,128]{2,1,0:T(4,128)S(1)}, u32[]{:S(2)}, u32[]{:S(2)}) %all-to-all-start.3) | async-done | bytes 32800 | tf_op jit(solution)/shard_map/all_to_all | solution.py:248
  100.3 1.4 %merge.1 = f32[4,4]{1,0:T(4,128)} custom-call(f32[16,4,128]{2,1,0:T(4,128)S(1)} %all-to-all-done.3.parts_ref), custom_call_target="tpu_custom_call" | custom-call | tf_op jit(solution)/shard_map/merge/pallas_call | solution.py:249
Async XLA Ops:
  0.6 71.6 %copy-start = (s32[128]{0:T(128)S(1)}, s32[128]{0:T(128)}, u32[]{:S(2)}) copy-start(s32[128]{0:T(128)} %param.17) | copy-start | bytes 1540
  0.6 0.8 copy-start.3
  1.5 0.7 copy-start.4
  2.2 0.7 copy-start.5
  3.0 0.7 copy-start.6
  3.7 35.8 %copy-start.1 = (bf16[192,8192]{1,0:T(8,128)(2,1)S(1)}, bf16[192,8192]{1,0:T(8,128)(2,1)}, u32[]{:S(2)}) copy-start(bf16[192,8192]{1,0:T(8,128)(2,1)} %he_ref.5) | copy-start | bytes 9437188
  4.2 34.9 %copy-start.8 = (s32[128]{0:T(128)S(1)}, s32[128]{0:T(128)}, u32[]{:S(2)}) copy-start(s32[128]{0:T(128)} %param.16) | copy-start | bytes 1540
  36.8 6.4 %collective-permute-start = (bf16[256,2944]{1,0:T(8,128)(2,1)}, bf16[256,2944]{1,0:T(8,128)(2,1)}, u32[]{:S(2)}, u32[]{:S(2)}) collective-permute-start(bf16[256,2944]{1,0:T(8,128)(2,1)} %bitcast.4.part_ref), channel_id=1, source_target_pairs={{0,16},{16,0},{32,48},{48,32},{64,80},{80,64},{96,112},{112,96},{1... | collective-permute-start | bytes 4521992 | tf_op jit(solution)/shard_map/ppermute | solution.py:201
  39.4 1.3 %copy-start.2 = (bf16[192,3584]{1,0:T(8,128)(2,1)S(1)}, bf16[192,3584]{1,0:T(8,128)(2,1)}, u32[]{:S(2)}) copy-start(bf16[192,3584]{1,0:T(8,128)(2,1)} %ha_ref.5) | copy-start | bytes 4128772
  40.8 2.4 %copy-start.7 = (s32[192]{0:T(256)S(1)}, s32[192]{0:T(256)}, u32[]{:S(2)}) copy-start(s32[192]{0:T(256)} %param.15) | copy-start | bytes 2308
  59.1 24.6 %all-to-all-start.2 = ((f32[16,4,128]{2,1,0:T(4,128)}), f32[16,4,128]{2,1,0:T(4,128)S(1)}, u32[]{:S(2)}, u32[]{:S(2)}) async-start(f32[16,4,128]{2,1,0:T(4,128)} %stats.1), calls=%async_computation.2 | async-start | bytes 65536 | tf_op jit(solution)/shard_map/all_to_all | solution.py:235
  85.5 14.8 %all-to-all-start.3 = ((f32[16,4,128]{2,1,0:T(4,128)}), f32[16,4,128]{2,1,0:T(4,128)S(1)}, u32[]{:S(2)}, u32[]{:S(2)}) async-start(f32[16,4,128]{2,1,0:T(4,128)} %get-tuple-element.6), calls=%async_computation.3 | async-start | bytes 65536 | tf_op jit(solution)/shard_map/all_to_all | solution.py:248

commit v3 on v2

--- a/solution.py
+++ b/solution.py
@@ -8,6 +8,8 @@
 from jax.sharding import PartitionSpec as P
 
 TOP = 4
+NEAR = 16
+FIRST = 16
 NC = 2
 
 masked_floor = -1e30
@@ -93,32 +95,90 @@
     return jnp.sum(jnp.where(lane == i, values, 0.0), axis=-1, keepdims=True)
 
 
-def stats_kernel(width, table_ref, out_ref):
+def total_rows(values):
+    return jnp.sum(values, axis=1, keepdims=True)
+
+
+def insert(levels, entry):
+    for i, level in enumerate(levels):
+        above = entry[0] > level[0]
+        levels[i] = tuple(jnp.where(above, new, old) for new, old in zip(entry, level))
+        entry = tuple(jnp.where(above, old, new) for new, old in zip(entry, level))
+
+
+def remove_top(levels, top):
+    hit = levels[0][0] == top
+    payload = [total_rows(jnp.where(hit, field, 0.0)) for field in levels[0][1:]]
+    count = total_rows(jnp.where(hit, 1.0, 0.0))
+    last = tuple(jnp.full_like(f, masked_floor) for f in levels[0])
+    lower = levels[1:] + [last]
+    return payload, count, [
+        tuple(jnp.where(hit, new, old) for new, old in zip(low, level))
+        for low, level in zip(lower, levels)
+    ]
+
+
+def stats_kernel(width, table_ref, gap_ref, out_ref):
+    sources, own = table_ref.shape[0], table_ref.shape[1]
+    real = lax.broadcasted_iota(jnp.int32, (own, 256), 1) < width
     columns = []
     for model in range(2):
-        part = table_ref[:, :, 256 * model:256 * model + 256]
-        real = lax.broadcasted_iota(jnp.int32, part.shape, 2) < width
-        peak = jnp.max(jnp.max(jnp.where(real, part, masked_floor), axis=0), axis=1, keepdims=True)
-        total = jnp.sum(jnp.where(real, jnp.exp(part - peak[None]), 0.0), axis=0)
-        total = jnp.sum(total, axis=1, keepdims=True)
-        pick = lane_at(jnp.sum(part, axis=0), width)
-        columns.append((peak, total, pick))
+        parts = [table_ref[i, :, 256 * model:256 * model + 256] for i in range(sources)]
+        peak = functools.reduce(jnp.maximum, parts)
+        peak = jnp.max(jnp.where(real, peak, masked_floor), axis=1, keepdims=True)
+        total = functools.reduce(jnp.add, [jnp.exp(part - peak) for part in parts])
+        total = total_rows(jnp.where(real, total, 0.0))
+        columns.append((peak, total, lane_at(functools.reduce(jnp.add, parts), width)))
     (pe, te, ce), (pa, ta, ca) = columns
-    stats = lanes_of([pe, pa, te, ta, ce, ca], out_ref.shape[1:])
+    least = pe - gap_ref[...].astype(jnp.float32) * 0.1
+    floor = jnp.full((own, 256), masked_floor, jnp.float32)
+    near, rest = [(floor,) * 2] * TOP, [(floor,) * 3] * TOP
+    count = jnp.zeros((own, 256), jnp.float32)
+    for i in range(sources):
+        e, a = table_ref[i, :, 0:256], table_ref[i, :, 256:512]
+        live = real & (e > dead_below)
+        is_near = live & (e >= least)
+        count += jnp.where(is_near, 1.0, 0.0)
+        insert(near, (jnp.where(is_near, e, masked_floor), a))
+        insert(rest, (jnp.where(live & (e < least), 3.0 * e - a, masked_floor), e, a))
+    missing = total_rows(count)
+    picked = []
+    for _ in range(NEAR):
+        top = jnp.max(near[0][0], axis=1, keepdims=True)
+        (a,), hits, near = remove_top(near, top)
+        found = top > dead_below
+        picked.append((jnp.where(found, top, masked_floor), a))
+        missing -= jnp.where(found & (hits == 1.0), 1.0, 0.0)
+    for _ in range(TOP):
+        top = jnp.max(rest[0][0], axis=1, keepdims=True)
+        (e, a), hits, rest = remove_top(rest, top)
+        found = top > dead_below
+        picked.append((jnp.where(found, e, masked_floor), a))
+        missing += jnp.where(found & (hits > 1.0), 1.0, 0.0)
+    lanes = [pe, pa, te, ta, ce, ca, missing]
+    lanes += [jnp.zeros_like(pe)] * (FIRST - len(lanes)) + [e for e, _ in picked]
+    lanes += [jnp.zeros_like(pe)] * (64 + FIRST - len(lanes)) + [a for _, a in picked]
+    stats = lanes_of(lanes, out_ref.shape[1:])
     for plane in range(out_ref.shape[0]):
         out_ref[plane] = stats
 
 
 def best_of(levels):
-    lane = lax.broadcasted_iota(jnp.int32, levels[0].shape, 1)
-    found = []
+    tops, counts, seen = [], [], 0.0
     for _ in range(TOP):
         top = jnp.max(levels[0], axis=1, keepdims=True)
-        found.append(top)
-        at = jnp.min(jnp.where(levels[0] == top, lane, lane.shape[1]), axis=1, keepdims=True)
-        hit = lane == at
+        hit = levels[0] == top
+        seen = seen + total_rows(jnp.where(hit, 1.0, 0.0))
+        tops.append(top)
+        counts.append(seen)
         lower = levels[1:] + [jnp.full_like(levels[0], -jnp.inf)]
         levels = [jnp.where(hit, low, level) for level, low in zip(levels, lower)]
+    found = []
+    for i in range(TOP):
+        value = tops[-1]
+        for top, seen in reversed(list(zip(tops, counts))):
+            value = jnp.where(seen > i, top, value)
+        found.append(value)
     return found
 
 
@@ -130,9 +190,9 @@
     return levels
 
 
-def score_kernel(width, table_ref, stats_ref, gap_ref, best_ref, peaks_ref, chosen_ref):
+def totals_of(stats_ref, gap_ref):
     stats = stats_ref[...]
-    peak_e, peak_a, sum_e, sum_a, pick_e, pick_a = [lane_at(stats, i) for i in range(6)]
+    peak_e, peak_a, sum_e, sum_a = [lane_at(stats, i) for i in range(4)]
 
     def total_of(peaks, sums):
         peak = jnp.max(peaks, axis=0)
@@ -147,8 +207,28 @@
         logprob_a = logits_a - log_total_a
         return logprob_e - logprob_a - penalty_slope * jnp.maximum(cut - logprob_e, 0.0)
 
-    peaks_ref[...] = lanes_of([peak_e - log_total_e, peak_a - log_total_a], peaks_ref.shape)
-    chosen_ref[...] = score(jnp.sum(pick_e, axis=0), jnp.sum(pick_a, axis=0))
+    return [peak_e - log_total_e, peak_a - log_total_a], score
+
+
+def finish_kernel(stats_ref, gap_ref, top_ref, peaks_ref, chosen_ref, lacking_ref):
+    peaks, score = totals_of(stats_ref, gap_ref)
+    stats = stats_ref[...]
+    peaks_ref[...] = lanes_of(peaks, peaks_ref.shape)
+    chosen_ref[...] = score(jnp.sum(lane_at(stats, 4), axis=0), jnp.sum(lane_at(stats, 5), axis=0))
+    lane = lax.broadcasted_iota(jnp.int32, stats.shape[1:], 1)
+    is_candidate = (lane >= FIRST) & (lane < FIRST + NEAR + TOP)
+    parts, lacking = [], jnp.zeros(stats.shape[1:], jnp.float32)
+    for plane in range(stats.shape[0]):
+        e, a = stats[plane], pltpu.roll(stats[plane], 64, 1)
+        value = jnp.where(e > dead_below, score(e, a), masked_floor)
+        parts.append(jnp.where(is_candidate, value, -jnp.inf))
+        lacking = jnp.maximum(lacking, jnp.where(lane == 6, e, 0.0))
+    top_ref[...] = lanes_of(best_of(sorted_levels(parts)), top_ref.shape)
+    lacking_ref[0] = jnp.where(jnp.max(lacking) > 0.0, 1, 0).astype(jnp.int32)
+
+
+def score_kernel(width, table_ref, stats_ref, gap_ref, best_ref):
+    _, score = totals_of(stats_ref, gap_ref)
     real = lax.broadcasted_iota(jnp.int32, (table_ref.shape[1], 256), 1) < width
     parts = []
     for source in range(table_ref.shape[0]):
@@ -224,36 +304,50 @@
     table = lax.all_to_all(table, "rows", 0, 0, tiled=True)
 
     small = jax.ShapeDtypeStruct((planes, own, 128), jnp.float32)
+    best_shape = jax.ShapeDtypeStruct((own, TOP), jnp.float32)
     stats = pl.pallas_call(
         functools.partial(stats_kernel, width),
         out_shape=small,
-        in_specs=[VMEM],
+        in_specs=[VMEM] * 2,
         out_specs=VMEM,
         compiler_params=PARAMS,
         name="stats",
-    )(table)
+    )(table, gap)
     stats = lax.all_to_all(stats, "vocab", 0, 0, tiled=True)
-    best, peaks, chosen = pl.pallas_call(
-        functools.partial(score_kernel, width),
+    top, peaks, chosen, lacking = pl.pallas_call(
+        finish_kernel,
         out_shape=(
-            small,
+            best_shape,
             jax.ShapeDtypeStruct((own, 2), jnp.float32),
             jax.ShapeDtypeStruct((own, 1), jnp.float32),
+            jax.ShapeDtypeStruct((1,), jnp.int32),
         ),
-        in_specs=[VMEM] * 3,
-        out_specs=(VMEM,) * 3,
-        compiler_params=PARAMS,
-        name="scores",
-    )(table, stats, gap)
-    best = lax.all_to_all(best, "vocab", 0, 0, tiled=True)
-    top = pl.pallas_call(
-        merge_kernel,
-        out_shape=jax.ShapeDtypeStruct((own, TOP), jnp.float32),
-        in_specs=[VMEM],
-        out_specs=VMEM,
-        compiler_params=PARAMS,
-        name="merge",
-    )(best)
+        in_specs=[VMEM] * 2,
+        out_specs=(VMEM, VMEM, VMEM, SMEM),
+        compiler_params=PARAMS,
+        name="finish",
+    )(stats, gap)
+
+    def with_every_entry(table, stats, gap, _):
+        best = pl.pallas_call(
+            functools.partial(score_kernel, width),
+            out_shape=small,
+            in_specs=[VMEM] * 3,
+            out_specs=VMEM,
+            compiler_params=PARAMS,
+            name="scores",
+        )(table, stats, gap)
+        best = lax.all_to_all(best, "vocab", 0, 0, tiled=True)
+        return pl.pallas_call(
+            merge_kernel,
+            out_shape=best_shape,
+            in_specs=[VMEM],
+            out_specs=VMEM,
+            compiler_params=PARAMS,
+            name="merge",
+        )(best)
+
+    top = lax.cond(lacking[0] > 0, with_every_entry, lambda *args: args[-1], table, stats, gap, top)
     return top, peaks, chosen.reshape(own)
 
 

time: 103 us -> 104 us (level)
  the two profiles are of different devices: /device:TPU:1 before, /device:TPU:4 now
where the time goes in v3:
time: 104 us; the launch traced here: 103 us
  blocking collectives  70.5 us (68%)
  Pallas kernels  10.2 us (10%)
  starting transfers between devices  7.85 us (8%)
  waiting for transfers between devices  6.67 us (6%)
  local copies, waits for them, and re-layouts  6.1 us (6%)
  between operations  1.42 us (1%)
    all_to_all x1, blocking collectives, per_device(): lax.all_to_all(blocks, 'rows', 0, 0, tiled=True).reshape(2 * beams, quarter)  29.7 us
    all_to_all x1, blocking collectives, per_device(): stats = lax.all_to_all(stats, 'vocab', 0, 0, tiled=True)  25.7 us
    all_to_all x1, blocking collectives, with_every_entry(): best = lax.all_to_all(best, 'vocab', 0, 0, tiled=True)  15.2 us
    all_to_all x1, waiting for transfers between devices, per_device(): table = lax.all_to_all(table, 'rows', 0, 0, tiled=True)  6.66 us
    all_to_all x1, starting transfers between devices, per_device(): table = lax.all_to_all(table, 'rows', 0, 0, tiled=True)  5.88 us
    unnamed x21, local copies, waits for them, and re-layouts  5.59 us
    pallas_call x1, Pallas kernels, per_device(): pl.pallas_call(second_kernel, out_shape=jax.ShapeDtypeStruct((rows, own,...  3.28 us
    pallas_call x1, Pallas kernels, per_device(): pl.pallas_call(first_kernel, out_shape=jax.ShapeDtypeStruct((2, 2, 2 * be...  2.41 us
  transfers between devices with their start and end apart: 2, of which 1 were waited for; matrix products, arithmetic and copies ran while one was open for 0% of the time, Pallas kernels for 2%

profile of v3, /device:TPU:4, one launch (start us, length us, event | category | flops | bytes accessed | tf_op | source)
XLA Modules:
  0.0 103.5 jit_solution(17037546006466028358)
XLA Ops:
  0.6 0.0 copy-start
  0.6 0.0 copy-start.3
  0.7 0.8 copy-done.3
  1.5 0.0 copy-start.4
  1.5 0.7 copy-done.4
  2.2 0.0 copy-start.5
  2.2 0.7 copy-done.5
  3.0 0.0 copy-start.6
  3.0 0.7 copy-done.6
  3.7 0.0 copy-start.1
  3.7 0.5 norms.1
  4.2 0.0 copy-start.8
  4.2 29.7 %all_to_all.20 = bf16[32,8,2944]{2,1,0:T(8,128)(2,1)} all-to-all(bf16[32,8,2944]{2,1,0:T(8,128)(2,1)S(1)} %norms.1), channel_id=1, replica_groups=mesh['rows'=32,'vocab'=16] {'rows'}, dimensions={0} | all-to-all | bytes 3014656 | tf_op jit(solution)/shard_map/all_to_all | solution.py:280
  33.9 2.0 %collective-permute-start = (bf16[256,2944]{1,0:T(8,128)(2,1)}, bf16[256,2944]{1,0:T(8,128)(2,1)}, u32[]{:S(2)}, u32[]{:S(2)}) collective-permute-start(bf16[256,2944]{1,0:T(8,128)(2,1)} %bitcast.4.part_ref), channel_id=1, source_target_pairs={{0,16},{16,0},{32,48},{48,32},{64,80},{80,64},{96,112},{112,96},{1... | collective-permute-start | bytes 4521992 | tf_op jit(solution)/shard_map/ppermute | solution.py:281
  35.9 0.0 copy-done.8
  35.9 0.2 reshape.39.ids_ref
  36.1 0.1 pad_add_fusion.pos_ref
  36.2 0.0 copy-done.1
  36.2 0.0 copy-start.2
  36.2 1.3 %copy-done.2 = bf16[192,3584]{1,0:T(8,128)(2,1)S(1)} copy-done((bf16[192,3584]{1,0:T(8,128)(2,1)S(1)}, bf16[192,3584]{1,0:T(8,128)(2,1)}, u32[]{:S(2)}) %copy-start.2) | copy-done | bytes 1376280
  37.6 0.0 copy-start.7
  37.6 2.4 %first_half.1.first_ref = f32[2,2,256,192]{3,2,1,0:T(8,128)S(1)} custom-call(s32[2]{0:T(128)S(1)} %pad_add_fusion.pos_ref, bf16[256,2944]{1,0:T(8,128)(2,1)} %bitcast.4.part_ref, bf16[192,8192]{1,0:T(8,128)(2,1)S(1)} %copy-done.1, bf16[192,3584]{1,0:T(8,128)(2,1)S(1)} %copy-done.2), custom_call_target="tpu_custom_call" | custom-call | flops 578813952 | bytes 1507328 | tf_op jit(solution)/shard_map/first_half/pallas_call | solution.py:285
  40.0 0.0 collective-permute-done.part_ref
  40.0 0.0 copy-done.7
  40.0 3.3 %second_half.1 = f32[32,4,512]{2,1,0:T(4,128)} custom-call(s32[2]{0:T(128)S(1)} %pad_add_fusion.pos_ref, bf16[256,2944]{1,0:T(8,128)(2,1)} %collective-permute-done.part_ref, bf16[192,8192]{1,0:T(8,128)(2,1)S(1)} %copy-done.1, bf16[192,3584]{1,0:T(8,128)(2,1)S(1)} %copy-done.2, f32[2,2,256,192]{3,2,1,0:T(8,128)S(1)} %first_half.1.first_ref, ...), custom_call_target="tpu_custom_call" | custom-call | flops 578813952 | bytes 1507328 | tf_op jit(solution)/shard_map/second_half/pallas_call | solution.py:294
  43.3 5.9 %all-to-all-start.2 = ((f32[32,4,512]{2,1,0:T(4,128)}), f32[32,4,512]{2,1,0:T(4,128)S(1)}, u32[]{:S(2)}, u32[]{:S(2)}) async-start(f32[32,4,512]{2,1,0:T(4,128)} %second_half.1), calls=%async_computation.2 | async-start | bytes 524288 | tf_op jit(solution)/shard_map/all_to_all | solution.py:304
  49.2 0.0 copy-done
  49.2 0.1 dynamic-slice_bitcast_fusion
  49.3 0.1 copy.18.gap_ref
  49.4 6.7 %all-to-all-done.2.table_ref = f32[32,4,512]{2,1,0:T(4,128)S(1)} async-done(((f32[32,4,512]{2,1,0:T(4,128)}), f32[32,4,512]{2,1,0:T(4,128)S(1)}, u32[]{:S(2)}, u32[]{:S(2)}) %all-to-all-start.2) | async-done | bytes 262176 | tf_op jit(solution)/shard_map/all_to_all | solution.py:304
  56.0 1.9 %stats.1 = f32[16,4,128]{2,1,0:T(4,128)S(1)} custom-call(f32[32,4,512]{2,1,0:T(4,128)S(1)} %all-to-all-done.2.table_ref, s32[4,1]{1,0:T(4,128)S(1)} %copy.18.gap_ref), custom_call_target="tpu_custom_call" | custom-call | tf_op jit(solution)/shard_map/stats/pallas_call | solution.py:308
  58.0 25.7 %all_to_all.21.stats_ref = f32[16,4,128]{2,1,0:T(4,128)S(1)} all-to-all(f32[16,4,128]{2,1,0:T(4,128)S(1)} %stats.1), channel_id=1, replica_groups=mesh['rows'=32,'vocab'=16] {'vocab'}, dimensions={0} | all-to-all | bytes 65536 | tf_op jit(solution)/shard_map/all_to_all | solution.py:316
  83.7 1.0 %finish.1 = (f32[4,4]{1,0:T(4,128)S(1)}, f32[4,2]{1,0:T(4,128)S(1)}, f32[4,1]{1,0:T(4,128)S(1)}, s32[1]{0:T(128)}) custom-call(f32[16,4,128]{2,1,0:T(4,128)S(1)} %all_to_all.21.stats_ref, s32[4,1]{1,0:T(4,128)S(1)} %copy.18.gap_ref), custom_call_target="tpu_custom_call" | custom-call | tf_op jit(solution)/shard_map/finish/pallas_call | solution.py:317
  85.4 0.6 copy.21
  86.0 0.6 reduce
  86.7 16.2 %conditional.1 = (f32[4,4]{1,0:T(4,128)S(1)}) conditional(s32[]{:T(128)} %bitcast.7, f32[4,4]{1,0:T(4,128)S(1)} %get-tuple-element.21, (f32[32,4,512]{2,1,0:T(4,128)S(1)}, f32[16,4,128]{2,1,0:T(4,128)S(1)}, s32[4,1]{0,1:T(1,128)S(1)}) %tuple.14), branch_computations={%region_0.1_spmd, %region_1.2_spmd} | conditional | bytes 65576 | solution.py:350
  86.7 0.1 copy.20.gap_ref
  86.7 0.6 scores.1
  87.4 15.2 %all_to_all.19.parts_ref = f32[16,4,128]{2,1,0:T(4,128)S(1)} all-to-all(f32[16,4,128]{2,1,0:T(4,128)S(1)} %scores.1), channel_id=1, replica_groups=mesh['rows'=32,'vocab'=16] {'vocab'}, dimensions={0} | all-to-all | bytes 65536 | tf_op jit(solution)/shard_map/cond/branch_1_fun/all_to_all | solution.py:340
  102.6 0.3 merge.1
  102.9 0.0 copy-start.9
  102.9 0.6 copy-done.9
Async XLA Ops:
  0.6 48.5 %copy-start = (s32[128]{0:T(128)S(1)}, s32[128]{0:T(128)}, u32[]{:S(2)}) copy-start(s32[128]{0:T(128)} %param.19) | copy-start | bytes 1540
  0.6 0.8 copy-start.3
  1.5 0.7 copy-start.4
  2.2 0.7 copy-start.5
  3.0 0.7 copy-start.6
  3.7 32.6 %copy-start.1 = (bf16[192,8192]{1,0:T(8,128)(2,1)S(1)}, bf16[192,8192]{1,0:T(8,128)(2,1)}, u32[]{:S(2)}) copy-start(bf16[192,8192]{1,0:T(8,128)(2,1)} %he_ref.5) | copy-start | bytes 9437188
  4.2 31.7 %copy-start.8 = (s32[128]{0:T(128)S(1)}, s32[128]{0:T(128)}, u32[]{:S(2)}) copy-start(s32[128]{0:T(128)} %param.18) | copy-start | bytes 1540
  33.9 6.1 %collective-permute-start = (bf16[256,2944]{1,0:T(8,128)(2,1)}, bf16[256,2944]{1,0:T(8,128)(2,1)}, u32[]{:S(2)}, u32[]{:S(2)}) collective-permute-start(bf16[256,2944]{1,0:T(8,128)(2,1)} %bitcast.4.part_ref), channel_id=1, source_target_pairs={{0,16},{16,0},{32,48},{48,32},{64,80},{80,64},{96,112},{112,96},{1... | collective-permute-start | bytes 4521992 | tf_op jit(solution)/shard_map/ppermute | solution.py:281
  36.2 1.3 %copy-start.2 = (bf16[192,3584]{1,0:T(8,128)(2,1)S(1)}, bf16[192,3584]{1,0:T(8,128)(2,1)}, u32[]{:S(2)}) copy-start(bf16[192,3584]{1,0:T(8,128)(2,1)} %ha_ref.5) | copy-start | bytes 4128772
  37.6 2.4 %copy-start.7 = (s32[192]{0:T(256)S(1)}, s32[192]{0:T(256)}, u32[]{:S(2)}) copy-start(s32[192]{0:T(256)} %param.17) | copy-start | bytes 2308
  43.3 12.7 %all-to-all-start.2 = ((f32[32,4,512]{2,1,0:T(4,128)}), f32[32,4,512]{2,1,0:T(4,128)S(1)}, u32[]{:S(2)}, u32[]{:S(2)}) async-start(f32[32,4,512]{2,1,0:T(4,128)} %second_half.1), calls=%async_computation.2 | async-start | bytes 524288 | tf_op jit(solution)/shard_map/all_to_all | solution.py:304
  102.9 0.6 copy-start.9

commit v4 on v3

--- a/solution.py
+++ b/solution.py
@@ -8,7 +8,7 @@
 from jax.sharding import PartitionSpec as P
 
 TOP = 4
-NEAR = 16
+NEAR = 40
 FIRST = 16
 NC = 2
 
@@ -19,12 +19,19 @@
 
 VMEM = pl.BlockSpec(memory_space=pltpu.VMEM)
 SMEM = pl.BlockSpec(memory_space=pltpu.SMEM)
-PARAMS = pltpu.CompilerParams(vmem_limit_bytes=40 * 1024 * 1024)
-
-
-def norm_kernel(he_ref, ge_ref, ha_ref, ga_ref, out_ref):
-    own, quarters = he_ref.shape[0], []
-    for hidden, gains in ((he_ref, ge_ref), (ha_ref, ga_ref)):
+PARAMS = pltpu.CompilerParams(vmem_limit_bytes=16 * 1024 * 1024)
+WIDE_PARAMS = pltpu.CompilerParams(vmem_limit_bytes=60 * 1024 * 1024)
+
+
+def norm_kernel(*refs):
+    inputs, out_ref, held, sems = refs[:4], refs[4], refs[5:9], refs[9]
+    copies = [pltpu.make_async_copy(inputs[i], held[i], sems.at[i]) for i in range(4)]
+    for copy in copies:
+        copy.start()
+    for copy in copies:
+        copy.wait()
+    own, quarters = held[0].shape[0], []
+    for hidden, gains in ((held[0], held[1]), (held[2], held[3])):
         values = hidden[...].astype(jnp.float32)
         gain = gains[...].astype(jnp.float32)
         mean = jnp.mean(values * values, axis=-1, keepdims=True)
@@ -190,6 +197,12 @@
     return levels
 
 
+def row_from(column):
+    shape = (column.shape[0], column.shape[0])
+    here = lax.broadcasted_iota(jnp.int32, shape, 0) == lax.broadcasted_iota(jnp.int32, shape, 1)
+    return jnp.sum(jnp.where(here, column, 0.0), axis=0, keepdims=True)
+
+
 def totals_of(stats_ref, gap_ref):
     stats = stats_ref[...]
     peak_e, peak_a, sum_e, sum_a = [lane_at(stats, i) for i in range(4)]
@@ -213,8 +226,10 @@
 def finish_kernel(stats_ref, gap_ref, top_ref, peaks_ref, chosen_ref, lacking_ref):
     peaks, score = totals_of(stats_ref, gap_ref)
     stats = stats_ref[...]
-    peaks_ref[...] = lanes_of(peaks, peaks_ref.shape)
-    chosen_ref[...] = score(jnp.sum(lane_at(stats, 4), axis=0), jnp.sum(lane_at(stats, 5), axis=0))
+    for i, peak in enumerate(peaks):
+        peaks_ref[i:i + 1, :] = row_from(peak)
+    picks = [jnp.sum(lane_at(stats, i), axis=0) for i in (4, 5)]
+    chosen_ref[...] = row_from(score(*picks))
     lane = lax.broadcasted_iota(jnp.int32, stats.shape[1:], 1)
     is_candidate = (lane >= FIRST) & (lane < FIRST + NEAR + TOP)
     parts, lacking = [], jnp.zeros(stats.shape[1:], jnp.float32)
@@ -269,14 +284,19 @@
     ids = token_ids.reshape(rows, own, 1)
     gap = lax.dynamic_slice_in_dim(plaus_level, row * own, own, 0).reshape(own, 1)
 
+    norm_inputs = (
+        expert_hidden, expert_gain.reshape(-1, 128), amateur_hidden, amateur_gain.reshape(-1, 128)
+    )
     blocks = pl.pallas_call(
         norm_kernel,
         out_shape=jax.ShapeDtypeStruct((rows, 2 * own, quarter), jnp.bfloat16),
-        in_specs=[VMEM] * 4,
+        in_specs=[pl.BlockSpec(memory_space=pl.ANY)] * 4,
         out_specs=VMEM,
-        compiler_params=PARAMS,
+        scratch_shapes=[pltpu.VMEM(x.shape, x.dtype) for x in norm_inputs]
+        + [pltpu.SemaphoreType.DMA((4,))],
+        compiler_params=WIDE_PARAMS,
         name="norms",
-    )(expert_hidden, expert_gain.reshape(-1, 128), amateur_hidden, amateur_gain.reshape(-1, 128))
+    )(*norm_inputs)
     half = lax.all_to_all(blocks, "rows", 0, 0, tiled=True).reshape(2 * beams, quarter)
     other_half = lax.ppermute(half, "rows", [(r, r ^ 1) for r in range(rows)])
     cost = pl.CostEstimate(
@@ -318,8 +338,8 @@
         finish_kernel,
         out_shape=(
             best_shape,
-            jax.ShapeDtypeStruct((own, 2), jnp.float32),
-            jax.ShapeDtypeStruct((own, 1), jnp.float32),
+            jax.ShapeDtypeStruct((2, own), jnp.float32),
+            jax.ShapeDtypeStruct((1, own), jnp.float32),
             jax.ShapeDtypeStruct((1,), jnp.int32),
         ),
         in_specs=[VMEM] * 2,
@@ -348,7 +368,7 @@
         )(best)
 
     top = lax.cond(lacking[0] > 0, with_every_entry, lambda *args: args[-1], table, stats, gap, top)
-    return top, peaks, chosen.reshape(own)
+    return top, peaks.T, chosen.reshape(own)
 
 
 def solution(mesh):

time: 104 us -> 89.3 us (0.86)
  the two profiles are of different devices: /device:TPU:4 before, /device:TPU:1 now
where the time goes in v4:
time: 89.3 us; the launch traced here: 88.9 us
  blocking collectives  57 us (64%)
  Pallas kernels  13.3 us (15%)
  waiting for transfers between devices  8.79 us (10%)
  starting transfers between devices  5.96 us (7%)
  local copies, waits for them, and re-layouts  2.36 us (3%)
  between operations  1.44 us (2%)
    all_to_all x1, blocking collectives, per_device(): lax.all_to_all(blocks, 'rows', 0, 0, tiled=True).reshape(2 * beams, quarter)  33.4 us
    all_to_all x1, blocking collectives, per_device(): stats = lax.all_to_all(stats, 'vocab', 0, 0, tiled=True)  23.6 us
    all_to_all x1, waiting for transfers between devices, per_device(): table = lax.all_to_all(table, 'rows', 0, 0, tiled=True)  8.79 us
    pallas_call x1, Pallas kernels, per_device(): pl.pallas_call(functools.partial(stats_kernel, width), out_shape=small, i...  3.81 us
    all_to_all x1, starting transfers between devices, per_device(): table = lax.all_to_all(table, 'rows', 0, 0, tiled=True)  3.67 us
    pallas_call x1, Pallas kernels, per_device(): pl.pallas_call(second_kernel, out_shape=jax.ShapeDtypeStruct((rows, own,...  3.28 us
    pallas_call x1, Pallas kernels, per_device(): pl.pallas_call(norm_kernel, out_shape=jax.ShapeDtypeStruct((rows, 2 * own...  2.72 us
    pallas_call x1, Pallas kernels, per_device(): pl.pallas_call(first_kernel, out_shape=jax.ShapeDtypeStruct((2, 2, 2 * be...  2.41 us
  transfers between devices with their start and end apart: 2, of which 1 were waited for; matrix products, arithmetic and copies ran while one was open for 1% of the time, Pallas kernels for 3%

profile of v4, /device:TPU:1, one launch (start us, length us, event | category | flops | bytes accessed | tf_op | source)
XLA Modules:
  0.0 88.9 jit_solution(12036255959100667661)
XLA Ops:
  0.6 0.0 copy-start
  0.6 0.0 copy-start.1
  0.7 2.7 %norms.1 = bf16[32,8,2944]{2,1,0:T(8,128)(2,1)} custom-call(bf16[4,8192]{1,0:T(4,128)(2,1)} %refs_0_.1, bf16[64,128]{1,0:T(8,128)(2,1)} %bitcast.12, bf16[4,3584]{1,0:T(4,128)(2,1)} %refs_2_.1, bf16[28,128]{1,0:T(8,128)(2,1)} %bitcast.13), custom_call_target="tpu_custom_call" | custom-call | tf_op jit(solution)/shard_map/norms/pallas_call | solution.py:290
  3.4 0.0 copy-start.4
  3.4 33.4 %all_to_all.20 = bf16[32,8,2944]{2,1,0:T(8,128)(2,1)} all-to-all(bf16[32,8,2944]{2,1,0:T(8,128)(2,1)} %norms.1), channel_id=1, replica_groups=mesh['rows'=32,'vocab'=16] {'rows'}, dimensions={0} | all-to-all | bytes 3014656 | tf_op jit(solution)/shard_map/all_to_all | solution.py:300
  36.8 2.3 %collective-permute-start = (bf16[256,2944]{1,0:T(8,128)(2,1)}, bf16[256,2944]{1,0:T(8,128)(2,1)}, u32[]{:S(2)}, u32[]{:S(2)}) collective-permute-start(bf16[256,2944]{1,0:T(8,128)(2,1)} %bitcast.4.part_ref), channel_id=1, source_target_pairs={{0,16},{16,0},{32,48},{48,32},{64,80},{80,64},{96,112},{112,96},{1... | collective-permute-start | bytes 4521992 | tf_op jit(solution)/shard_map/ppermute | solution.py:301
  39.1 0.0 copy-done.4
  39.1 0.2 reshape.39.ids_ref
  39.4 0.1 pad_add_fusion.pos_ref
  39.5 0.0 copy-done.1
  39.5 0.0 copy-start.2
  39.5 1.3 %copy-done.2 = bf16[192,3584]{1,0:T(8,128)(2,1)S(1)} copy-done((bf16[192,3584]{1,0:T(8,128)(2,1)S(1)}, bf16[192,3584]{1,0:T(8,128)(2,1)}, u32[]{:S(2)}) %copy-start.2) | copy-done | bytes 1376280
  40.8 0.0 copy-start.3
  40.8 2.4 %first_half.1.first_ref = f32[2,2,256,192]{3,2,1,0:T(8,128)S(1)} custom-call(s32[2]{0:T(128)S(1)} %pad_add_fusion.pos_ref, bf16[256,2944]{1,0:T(8,128)(2,1)} %bitcast.4.part_ref, bf16[192,8192]{1,0:T(8,128)(2,1)S(1)} %copy-done.1, bf16[192,3584]{1,0:T(8,128)(2,1)S(1)} %copy-done.2), custom_call_target="tpu_custom_call" | custom-call | flops 578813952 | bytes 1507328 | tf_op jit(solution)/shard_map/first_half/pallas_call | solution.py:305
  43.2 0.0 collective-permute-done.part_ref
  43.3 0.0 copy-done.3
  43.3 3.3 %second_half.1 = f32[32,4,512]{2,1,0:T(4,128)} custom-call(s32[2]{0:T(128)S(1)} %pad_add_fusion.pos_ref, bf16[256,2944]{1,0:T(8,128)(2,1)} %collective-permute-done.part_ref, bf16[192,8192]{1,0:T(8,128)(2,1)S(1)} %copy-done.1, bf16[192,3584]{1,0:T(8,128)(2,1)S(1)} %copy-done.2, f32[2,2,256,192]{3,2,1,0:T(8,128)S(1)} %first_half.1.first_ref, ...), custom_call_target="tpu_custom_call" | custom-call | flops 578813952 | bytes 1507328 | tf_op jit(solution)/shard_map/second_half/pallas_call | solution.py:314
  46.5 3.7 %all-to-all-start.2 = ((f32[32,4,512]{2,1,0:T(4,128)}), f32[32,4,512]{2,1,0:T(4,128)S(1)}, u32[]{:S(2)}, u32[]{:S(2)}) async-start(f32[32,4,512]{2,1,0:T(4,128)} %second_half.1), calls=%async_computation.2 | async-start | bytes 524288 | tf_op jit(solution)/shard_map/all_to_all | solution.py:324
  50.2 0.0 copy-done
  50.2 0.1 dynamic-slice_bitcast_fusion
  50.3 0.1 copy.17.gap_ref
  50.4 8.8 %all-to-all-done.2.table_ref = f32[32,4,512]{2,1,0:T(4,128)S(1)} async-done(((f32[32,4,512]{2,1,0:T(4,128)}), f32[32,4,512]{2,1,0:T(4,128)S(1)}, u32[]{:S(2)}, u32[]{:S(2)}) %all-to-all-start.2) | async-done | bytes 262176 | tf_op jit(solution)/shard_map/all_to_all | solution.py:324
  59.2 3.8 %stats.1 = f32[16,4,128]{2,1,0:T(4,128)S(1)} custom-call(f32[32,4,512]{2,1,0:T(4,128)S(1)} %all-to-all-done.2.table_ref, s32[4,1]{1,0:T(4,128)S(1)} %copy.17.gap_ref), custom_call_target="tpu_custom_call" | custom-call | tf_op jit(solution)/shard_map/stats/pallas_call | solution.py:328
  63.0 23.6 %all_to_all.21.stats_ref = f32[16,4,128]{2,1,0:T(4,128)S(1)} all-to-all(f32[16,4,128]{2,1,0:T(4,128)S(1)} %stats.1), channel_id=1, replica_groups=mesh['rows'=32,'vocab'=16] {'vocab'}, dimensions={0} | all-to-all | bytes 65536 | tf_op jit(solution)/shard_map/all_to_all | solution.py:336
  86.6 1.0 %finish.1 = (f32[4,4]{1,0:T(4,128)S(1)}, f32[2,4]{1,0:T(2,128)}, f32[1,4]{1,0:T(1,128)}, s32[1]{0:T(128)}) custom-call(f32[16,4,128]{2,1,0:T(4,128)S(1)} %all_to_all.21.stats_ref, s32[4,1]{1,0:T(4,128)S(1)} %copy.17.gap_ref), custom_call_target="tpu_custom_call" | custom-call | tf_op jit(solution)/shard_map/finish/pallas_call | solution.py:337
  88.3 0.0 copy-start.5
  88.3 0.6 copy-done.5
  (1 shorter events, 0.0 us)
Async XLA Ops:
  0.6 49.6 %copy-start = (s32[128]{0:T(128)S(1)}, s32[128]{0:T(128)}, u32[]{:S(2)}) copy-start(s32[128]{0:T(128)} %param.19) | copy-start | bytes 1540
  0.6 38.8 %copy-start.1 = (bf16[192,8192]{1,0:T(8,128)(2,1)S(1)}, bf16[192,8192]{1,0:T(8,128)(2,1)}, u32[]{:S(2)}) copy-start(bf16[192,8192]{1,0:T(8,128)(2,1)} %he_ref.3) | copy-start | bytes 9437188
  3.4 35.7 %copy-start.4 = (s32[128]{0:T(128)S(1)}, s32[128]{0:T(128)}, u32[]{:S(2)}) copy-start(s32[128]{0:T(128)} %param.18) | copy-start | bytes 1540
  36.8 6.4 %collective-permute-start = (bf16[256,2944]{1,0:T(8,128)(2,1)}, bf16[256,2944]{1,0:T(8,128)(2,1)}, u32[]{:S(2)}, u32[]{:S(2)}) collective-permute-start(bf16[256,2944]{1,0:T(8,128)(2,1)} %bitcast.4.part_ref), channel_id=1, source_target_pairs={{0,16},{16,0},{32,48},{48,32},{64,80},{80,64},{96,112},{112,96},{1... | collective-permute-start | bytes 4521992 | tf_op jit(solution)/shard_map/ppermute | solution.py:301
  39.5 1.3 %copy-start.2 = (bf16[192,3584]{1,0:T(8,128)(2,1)S(1)}, bf16[192,3584]{1,0:T(8,128)(2,1)}, u32[]{:S(2)}) copy-start(bf16[192,3584]{1,0:T(8,128)(2,1)} %ha_ref.3) | copy-start | bytes 4128772
  40.8 2.4 %copy-start.3 = (s32[192]{0:T(256)S(1)}, s32[192]{0:T(256)}, u32[]{:S(2)}) copy-start(s32[192]{0:T(256)} %param.17) | copy-start | bytes 2308
  46.5 12.7 %all-to-all-start.2 = ((f32[32,4,512]{2,1,0:T(4,128)}), f32[32,4,512]{2,1,0:T(4,128)S(1)}, u32[]{:S(2)}, u32[]{:S(2)}) async-start(f32[32,4,512]{2,1,0:T(4,128)} %second_half.1), calls=%async_computation.2 | async-start | bytes 524288 | tf_op jit(solution)/shard_map/all_to_all | solution.py:324
  88.3 0.6 copy-start.5

commit v5 on v4

--- a/solution.py
+++ b/solution.py
@@ -8,7 +8,7 @@
 from jax.sharding import PartitionSpec as P
 
 TOP = 4
-NEAR = 40
+NEAR = 20
 FIRST = 16
 NC = 2
 
@@ -18,8 +18,10 @@
 norm_epsilon = 1e-06
 
 VMEM = pl.BlockSpec(memory_space=pltpu.VMEM)
+ANY = pl.BlockSpec(memory_space=pl.ANY)
 SMEM = pl.BlockSpec(memory_space=pltpu.SMEM)
 PARAMS = pltpu.CompilerParams(vmem_limit_bytes=16 * 1024 * 1024)
+PRODUCT_PARAMS = pltpu.CompilerParams(vmem_limit_bytes=54 * 1024 * 1024)
 WIDE_PARAMS = pltpu.CompilerParams(vmem_limit_bytes=60 * 1024 * 1024)
 
 
@@ -50,43 +52,79 @@
                     out_ref[dest, own * p:own * p + own, 128 * i:128 * i + 128] = chunk
 
 
-def half_logits(core, part_ref, he_ref, ha_ref, model):
-    head = (he_ref, ha_ref)[model]
-    qe, qa = he_ref.shape[1] // 4, ha_ref.shape[1] // 4
-    low, size = ((0, qe), (qe, qa))[model]
-    sums = []
-    for p in range(2):
-        columns = pl.ds(pl.multiple_of((2 * core + p) * size, 128), size)
-        sums.append(lax.dot_general(
-            part_ref[:, low:low + size], head[:, columns], (((1,), (1,)), ((), ())),
-            preferred_element_type=jnp.float32,
-        ))
-    return sums
-
-
-def first_kernel(pos_ref, part_ref, he_ref, ha_ref, out_ref):
+def chunked(core, part_ref, head_refs, held, sems):
+    part_buf, head_bufs = held
+    columns = part_ref.shape[1]
+    quarter_e = head_refs[0].shape[1] // 4
+    chunks = [(0, 0, quarter_e // 2), (0, quarter_e // 2, quarter_e // 2), (1, quarter_e, columns - quarter_e)]
+    copies = []
+    for i, (model, low, size) in enumerate(chunks):
+        here = pl.ds(low, size)
+        own = [pltpu.make_async_copy(part_ref.at[:, here], part_buf.at[:, here], sems.at[i, 2])]
+        quarter = head_refs[model].shape[1] // 4
+        inside = low - (quarter_e if model else 0)
+        for p in range(2):
+            source = pl.ds(pl.multiple_of((2 * core + p) * quarter + inside, 128), size)
+            own.append(pltpu.make_async_copy(
+                head_refs[model].at[:, source], head_bufs.at[p, :, here], sems.at[i, p]
+            ))
+        for copy in own:
+            copy.start()
+        copies.append(own)
+    for (model, low, size), own in zip(chunks, copies):
+        for copy in own:
+            copy.wait()
+        yield model, [
+            lax.dot_general(
+                part_buf[:, low:low + size], head_bufs[p, :, low:low + size],
+                (((1,), (1,)), ((), ())), preferred_element_type=jnp.float32,
+            )
+            for p in range(2)
+        ]
+
+
+def half_sums(core, part_ref, head_refs, held, sems, acc_ref):
+    started = set()
+    for model, sums in chunked(core, part_ref, head_refs, held, sems):
+        for p, total in enumerate(sums):
+            acc_ref[model, p] = acc_ref[model, p] + total if model in started else total
+        started.add(model)
+
+
+def quarters_joined(acc_ref, model, owner, own):
+    at = 2 * own * owner
+    return acc_ref[model, 0, at:at + own, :] + acc_ref[model, 1, at + own:at + 2 * own, :]
+
+
+def first_kernel(pos_ref, part_ref, he_ref, ha_ref, out_ref, part_buf, head_bufs, sems, acc_ref):
+    half_sums(pos_ref[0], part_ref, (he_ref, ha_ref), (part_buf, head_bufs), sems, acc_ref)
     for model in range(2):
-        for p, total in enumerate(half_logits(pos_ref[0], part_ref, he_ref, ha_ref, model)):
-            out_ref[model, p] = total
-
-
-def second_kernel(pos_ref, part_ref, he_ref, ha_ref, first_ref, live_ref, ids_ref, out_ref, acc_ref):
+        for owner in range(out_ref.shape[1]):
+            out_ref[model, owner] = quarters_joined(acc_ref, model, owner, out_ref.shape[2])
+
+
+def second_kernel(
+    pos_ref, part_ref, he_ref, ha_ref, first_ref, live_ref, ids_ref, out_ref,
+    part_buf, head_bufs, sems, acc_ref,
+):
     width = he_ref.shape[0]
-    own = out_ref.shape[1]
-    for model in range(2):
-        for p, total in enumerate(half_logits(1 - pos_ref[0], part_ref, he_ref, ha_ref, model)):
-            acc_ref[model, p] = total + first_ref[model, p]
+    own = ids_ref.shape[1]
+    half_sums(1 - pos_ref[0], part_ref, (he_ref, ha_ref), (part_buf, head_bufs), sems, acc_ref)
     live = live_ref[...] == 1
     positions = pos_ref[1] + lax.broadcasted_iota(jnp.int32, (1, width), 1)
+    half = width // 2
     for owner in range(out_ref.shape[0]):
-        at = 2 * own * owner
         hits = ids_ref[owner] == positions
         for model in range(2):
-            logits = acc_ref[model, 0, at:at + own, :] + acc_ref[model, 1, at + own:at + 2 * own, :]
+            logits = first_ref[model, owner] + quarters_joined(acc_ref, model, owner, own)
             pick = jnp.sum(jnp.where(hits, logits, 0.0), axis=1, keepdims=True)
-            low = 256 * model
-            out_ref[owner, :, low:low + width] = jnp.where(live, logits, masked_floor)
-            out_ref[owner, :, low + width:low + 256] = jnp.broadcast_to(pick, (own, 256 - width))
+            pick = jnp.broadcast_to(pick, (own, 128 - half))
+            held = jnp.where(live, logits, masked_floor)
+            low = 128 * model
+            for side in range(2):
+                rows = slice(own * side, own * side + own)
+                out_ref[owner, rows, low:low + half] = held[:, half * side:half * side + half]
+                out_ref[owner, rows, low + half:low + 128] = pick
 
 
 def lanes_of(columns, shape):
@@ -126,23 +164,28 @@
 
 
 def stats_kernel(width, table_ref, gap_ref, out_ref):
-    sources, own = table_ref.shape[0], table_ref.shape[1]
-    real = lax.broadcasted_iota(jnp.int32, (own, 256), 1) < width
+    sources, own = table_ref.shape[0], table_ref.shape[1] // 2
+    shape = (2 * own, 128)
+    real = lax.broadcasted_iota(jnp.int32, shape, 1) < width // 2
     columns = []
     for model in range(2):
-        parts = [table_ref[i, :, 256 * model:256 * model + 256] for i in range(sources)]
+        parts = [table_ref[i, :, 128 * model:128 * model + 128] for i in range(sources)]
         peak = functools.reduce(jnp.maximum, parts)
         peak = jnp.max(jnp.where(real, peak, masked_floor), axis=1, keepdims=True)
-        total = functools.reduce(jnp.add, [jnp.exp(part - peak) for part in parts])
+        peak = jnp.maximum(peak[:own], peak[own:])
+        both = jnp.concatenate([peak, peak])
+        total = functools.reduce(jnp.add, [jnp.exp(part - both) for part in parts])
         total = total_rows(jnp.where(real, total, 0.0))
-        columns.append((peak, total, lane_at(functools.reduce(jnp.add, parts), width)))
+        pick = lane_at(functools.reduce(jnp.add, parts), width // 2)
+        columns.append((peak, total[:own] + total[own:], pick[:own]))
     (pe, te, ce), (pa, ta, ca) = columns
     least = pe - gap_ref[...].astype(jnp.float32) * 0.1
-    floor = jnp.full((own, 256), masked_floor, jnp.float32)
+    least = jnp.concatenate([least, least])
+    floor = jnp.full(shape, masked_floor, jnp.float32)
     near, rest = [(floor,) * 2] * TOP, [(floor,) * 3] * TOP
-    count = jnp.zeros((own, 256), jnp.float32)
+    count = jnp.zeros(shape, jnp.float32)
     for i in range(sources):
-        e, a = table_ref[i, :, 0:256], table_ref[i, :, 256:512]
+        e, a = table_ref[i, :, 0:128], table_ref[i, :, 128:256]
         live = real & (e > dead_below)
         is_near = live & (e >= least)
         count += jnp.where(is_near, 1.0, 0.0)
@@ -162,10 +205,12 @@
         found = top > dead_below
         picked.append((jnp.where(found, e, masked_floor), a))
         missing += jnp.where(found & (hits > 1.0), 1.0, 0.0)
-    lanes = [pe, pa, te, ta, ce, ca, missing]
-    lanes += [jnp.zeros_like(pe)] * (FIRST - len(lanes)) + [e for e, _ in picked]
-    lanes += [jnp.zeros_like(pe)] * (64 + FIRST - len(lanes)) + [a for _, a in picked]
-    stats = lanes_of(lanes, out_ref.shape[1:])
+    zeros = [jnp.zeros_like(missing)]
+    lanes = zeros * FIRST + [e for e, _ in picked]
+    lanes += zeros * (64 + FIRST - len(lanes)) + [a for _, a in picked]
+    lanes = lanes_of(lanes, shape)
+    stats = lanes_of([pe, pa, te, ta, ce, ca, missing[:own] + missing[own:]], (own, 128))
+    stats += lanes[:own] + pltpu.roll(lanes, len(picked), 1)[own:]
     for plane in range(out_ref.shape[0]):
         out_ref[plane] = stats
 
@@ -203,7 +248,7 @@
     return jnp.sum(jnp.where(here, column, 0.0), axis=0, keepdims=True)
 
 
-def totals_of(stats_ref, gap_ref):
+def totals_of(stats_ref, gap_ref, copies=1):
     stats = stats_ref[...]
     peak_e, peak_a, sum_e, sum_a = [lane_at(stats, i) for i in range(4)]
 
@@ -214,11 +259,14 @@
     peak_e, log_total_e = total_of(peak_e, sum_e)
     peak_a, log_total_a = total_of(peak_a, sum_a)
     cut = peak_e - log_total_e - gap_ref[...].astype(jnp.float32) * 0.1
+    shift_e, shift_a, cuts = [
+        jnp.concatenate([x] * copies) if copies > 1 else x for x in (log_total_e, log_total_a, cut)
+    ]
 
     def score(logits_e, logits_a):
-        logprob_e = logits_e - log_total_e
-        logprob_a = logits_a - log_total_a
-        return logprob_e - logprob_a - penalty_slope * jnp.maximum(cut - logprob_e, 0.0)
+        logprob_e = logits_e - shift_e
+        logprob_a = logits_a - shift_a
+        return logprob_e - logprob_a - penalty_slope * jnp.maximum(cuts - logprob_e, 0.0)
 
     return [peak_e - log_total_e, peak_a - log_total_a], score
 
@@ -231,7 +279,7 @@
     picks = [jnp.sum(lane_at(stats, i), axis=0) for i in (4, 5)]
     chosen_ref[...] = row_from(score(*picks))
     lane = lax.broadcasted_iota(jnp.int32, stats.shape[1:], 1)
-    is_candidate = (lane >= FIRST) & (lane < FIRST + NEAR + TOP)
+    is_candidate = (lane >= FIRST) & (lane < FIRST + 2 * (NEAR + TOP))
     parts, lacking = [], jnp.zeros(stats.shape[1:], jnp.float32)
     for plane in range(stats.shape[0]):
         e, a = stats[plane], pltpu.roll(stats[plane], 64, 1)
@@ -243,21 +291,23 @@
 
 
 def score_kernel(width, table_ref, stats_ref, gap_ref, best_ref):
-    _, score = totals_of(stats_ref, gap_ref)
-    real = lax.broadcasted_iota(jnp.int32, (table_ref.shape[1], 256), 1) < width
+    _, score = totals_of(stats_ref, gap_ref, 2)
+    own = table_ref.shape[1] // 2
+    real = lax.broadcasted_iota(jnp.int32, (2 * own, 128), 1) < width // 2
     parts = []
     for source in range(table_ref.shape[0]):
-        e = table_ref[source, :, 0:256]
-        a = table_ref[source, :, 256:512]
+        e, a = table_ref[source, :, 0:128], table_ref[source, :, 128:256]
         parts.append(jnp.where(real & (e > dead_below), score(e, a), masked_floor))
-    best = lanes_of(best_of(sorted_levels(parts)), best_ref.shape[1:])
+    found = best_of(sorted_levels(parts))
+    found = [value[:own] for value in found] + [value[own:] for value in found]
+    best = lanes_of(found, best_ref.shape[1:])
     for plane in range(best_ref.shape[0]):
         best_ref[plane] = best
 
 
 def merge_kernel(parts_ref, out_ref):
     shape = parts_ref.shape[1:]
-    real = lax.broadcasted_iota(jnp.int32, shape, 1) < TOP
+    real = lax.broadcasted_iota(jnp.int32, shape, 1) < 2 * TOP
     parts = [jnp.where(real, parts_ref[i], -jnp.inf) for i in range(parts_ref.shape[0])]
     out_ref[...] = lanes_of(best_of(sorted_levels(parts)), out_ref.shape)
 
@@ -290,7 +340,7 @@
     blocks = pl.pallas_call(
         norm_kernel,
         out_shape=jax.ShapeDtypeStruct((rows, 2 * own, quarter), jnp.bfloat16),
-        in_specs=[pl.BlockSpec(memory_space=pl.ANY)] * 4,
+        in_specs=[ANY] * 4,
         out_specs=VMEM,
         scratch_shapes=[pltpu.VMEM(x.shape, x.dtype) for x in norm_inputs]
         + [pltpu.SemaphoreType.DMA((4,))],
@@ -302,22 +352,29 @@
     cost = pl.CostEstimate(
         flops=4 * beams * width * 2 * quarter, bytes_accessed=4 * beams * quarter, transcendentals=0
     )
+    buffers = [
+        pltpu.VMEM((2 * beams, quarter), jnp.bfloat16),
+        pltpu.VMEM((2, width, quarter), jnp.bfloat16),
+        pltpu.SemaphoreType.DMA((3, 3)),
+        pltpu.VMEM((2, 2, 2 * beams, width), jnp.float32),
+    ]
     first = pl.pallas_call(
         first_kernel,
-        out_shape=jax.ShapeDtypeStruct((2, 2, 2 * beams, width), jnp.float32),
-        in_specs=[SMEM] + [VMEM] * 3,
+        out_shape=jax.ShapeDtypeStruct((2, rows, own, width), jnp.float32),
+        in_specs=[SMEM] + [ANY] * 3,
         out_specs=VMEM,
-        compiler_params=PARAMS,
+        scratch_shapes=buffers,
+        compiler_params=PRODUCT_PARAMS,
         cost_estimate=cost,
         name="first_half",
     )(position, half, expert_head, amateur_head)
     table = pl.pallas_call(
         second_kernel,
-        out_shape=jax.ShapeDtypeStruct((rows, own, 512), jnp.float32),
-        in_specs=[SMEM] + [VMEM] * 6,
+        out_shape=jax.ShapeDtypeStruct((rows, 2 * own, 256), jnp.float32),
+        in_specs=[SMEM] + [ANY] * 3 + [VMEM] * 3,
         out_specs=VMEM,
-        scratch_shapes=[pltpu.VMEM((2, 2, 2 * beams, width), jnp.float32)],
-        compiler_params=PARAMS,
+        scratch_shapes=buffers,
+        compiler_params=PRODUCT_PARAMS,
         cost_estimate=cost,
         name="second_half",
     )(position, other_half, expert_head, amateur_head, first, live_mask.reshape(1, -1), ids)

time: 89.3 us -> 92.8 us (1.039)
  Pallas kernels: 13.3 us -> 15.9 us
    pallas_call x2, Pallas kernels: 5.7 us -> 10.3 us  [the longest x1 6.2 us: per_device(): pl.pallas_call(second_kernel, out_shape=jax.ShapeDtypeStruct((rows, 2 * o...]
    pallas_call x1, Pallas kernels: 3.81 us -> 2.02 us  [per_device(): pl.pallas_call(functools.partial(stats_kernel, width), out_shape=small, i...]
    unnamed x12 -> x10, local copies, waits for them, and re-layouts: 1.94 us -> 1.72 us
  transfers between devices with their start and end apart: 2 -> 2, of which waited for: 1 -> 1; matrix products, arithmetic and copies ran while one was open for 1% -> 2% of each run, Pallas kernels for 3% -> 4%
where the time goes in v5:
time: 92.8 us; the launch traced here: 92.4 us
  blocking collectives  56.9 us (61%)
  Pallas kernels  15.9 us (17%)
  waiting for transfers between devices  8.8 us (9%)
  starting transfers between devices  5.97 us (6%)
  local copies, waits for them, and re-layouts  2.77 us (3%)
  between operations  1.41 us (2%)
    all_to_all x1, blocking collectives, per_device(): lax.all_to_all(blocks, 'rows', 0, 0, tiled=True).reshape(2 * beams, quarter)  32.7 us
    all_to_all x1, blocking collectives, per_device(): stats = lax.all_to_all(stats, 'vocab', 0, 0, tiled=True)  24.2 us
    all_to_all x1, waiting for transfers between devices, per_device(): table = lax.all_to_all(table, 'rows', 0, 0, tiled=True)  8.8 us
    pallas_call x1, Pallas kernels, per_device(): pl.pallas_call(second_kernel, out_shape=jax.ShapeDtypeStruct((rows, 2 * o...  6.2 us
    pallas_call x1, Pallas kernels, per_device(): pl.pallas_call(first_kernel, out_shape=jax.ShapeDtypeStruct((2, rows, own...  4.11 us
    all_to_all x1, starting transfers between devices, per_device(): table = lax.all_to_all(table, 'rows', 0, 0, tiled=True)  3.68 us
    pallas_call x1, Pallas kernels, per_device(): pl.pallas_call(norm_kernel, out_shape=jax.ShapeDtypeStruct((rows, 2 * own...  2.56 us
    ppermute x1, starting transfers between devices, per_device(): other_half = lax.ppermute(half, 'rows', [(r, r ^ 1) for r in range(rows)])  2.29 us
  transfers between devices with their start and end apart: 2, of which 1 were waited for; matrix products, arithmetic and copies ran while one was open for 2% of the time, Pallas kernels for 4%

profile of v5, /device:TPU:1, one launch (start us, length us, event | category | flops | bytes accessed | tf_op | source)
XLA Modules:
  0.0 92.4 jit_solution(5331784522182964847)
XLA Ops:
  0.6 0.0 copy-start
  0.6 2.6 %norms.1 = bf16[32,8,2944]{2,1,0:T(8,128)(2,1)} custom-call(bf16[4,8192]{1,0:T(4,128)(2,1)} %refs_0_.1, bf16[64,128]{1,0:T(8,128)(2,1)} %bitcast.13, bf16[4,3584]{1,0:T(4,128)(2,1)} %refs_2_.1, bf16[28,128]{1,0:T(8,128)(2,1)} %bitcast.14), custom_call_target="tpu_custom_call" | custom-call | tf_op jit(solution)/shard_map/norms/pallas_call | solution.py:340
  3.2 0.0 copy-start.3
  3.2 32.7 %all_to_all.20 = bf16[32,8,2944]{2,1,0:T(8,128)(2,1)S(1)} all-to-all(bf16[32,8,2944]{2,1,0:T(8,128)(2,1)} %norms.1), channel_id=1, replica_groups=mesh['rows'=32,'vocab'=16] {'rows'}, dimensions={0} | all-to-all | bytes 3014656 | tf_op jit(solution)/shard_map/all_to_all | solution.py:350
  35.9 0.0 copy-start.1
  35.9 2.3 %collective-permute-start = (bf16[256,2944]{1,0:T(8,128)(2,1)S(1)}, bf16[256,2944]{1,0:T(8,128)(2,1)S(1)}, u32[]{:S(2)}, u32[]{:S(2)}) collective-permute-start(bf16[256,2944]{1,0:T(8,128)(2,1)S(1)} %bitcast.11), channel_id=1, source_target_pairs={{0,16},{16,0},{32,48},{48,32},{64,80},{80,64},{96,112},{112,96},{1... | collective-permute-start | bytes 4521992 | tf_op jit(solution)/shard_map/ppermute | solution.py:351
  38.2 0.0 copy-done.3
  38.3 0.9 reshape.39.ids_ref
  39.1 0.6 pad_add_fusion.pos_ref
  39.7 0.0 copy-done.1
  39.7 4.1 %first_half.1.first_ref = f32[2,32,4,192]{3,2,1,0:T(4,128)} custom-call(s32[2]{0:T(128)} %pad_add_fusion.pos_ref, bf16[256,2944]{1,0:T(8,128)(2,1)} %bitcast.12, bf16[192,8192]{1,0:T(8,128)(2,1)} %he_ref.3, bf16[192,3584]{1,0:T(8,128)(2,1)} %ha_ref.3), custom_call_target="tpu_custom_call" | custom-call | flops 578813952 | bytes 1507328 | tf_op jit(solution)/shard_map/first_half/pallas_call | solution.py:361
  43.8 0.0 collective-permute-done.part_ref
  43.9 0.0 copy-start.2
  43.9 1.1 %copy-done.2 = bf16[256,2944]{1,0:T(8,128)(2,1)} copy-done((bf16[256,2944]{1,0:T(8,128)(2,1)}, bf16[256,2944]{1,0:T(8,128)(2,1)S(1)}, u32[]{:S(2)}) %copy-start.2) | copy-done | bytes 1507352
  45.0 6.2 %second_half.1 = f32[32,8,256]{2,1,0:T(8,128)} custom-call(s32[2]{0:T(128)} %pad_add_fusion.pos_ref, bf16[256,2944]{1,0:T(8,128)(2,1)} %copy-done.2, bf16[192,8192]{1,0:T(8,128)(2,1)} %he_ref.3, bf16[192,3584]{1,0:T(8,128)(2,1)} %ha_ref.3, f32[2,32,4,192]{3,2,1,0:T(4,128)} %first_half.1.first_ref, s32[1,192]{1,0:T(1,128)} %bitcast.15, ...), custom_call_target="tpu_custom_call" | custom-call | flops 578813952 | bytes 1507328 | tf_op jit(solution)/shard_map/second_half/pallas_call | solution.py:371
  51.2 3.7 %all-to-all-start.2 = ((f32[32,8,256]{2,1,0:T(8,128)}), f32[32,8,256]{2,1,0:T(8,128)S(1)}, u32[]{:S(2)}, u32[]{:S(2)}) async-start(f32[32,8,256]{2,1,0:T(8,128)} %second_half.1), calls=%async_computation.2 | async-start | bytes 524288 | tf_op jit(solution)/shard_map/all_to_all | solution.py:381
  54.9 0.0 copy-done
  54.9 0.1 dynamic-slice_bitcast_fusion
  55.0 0.1 copy.17.gap_ref
  55.1 8.8 %all-to-all-done.2.table_ref = f32[32,8,256]{2,1,0:T(8,128)S(1)} async-done(((f32[32,8,256]{2,1,0:T(8,128)}), f32[32,8,256]{2,1,0:T(8,128)S(1)}, u32[]{:S(2)}, u32[]{:S(2)}) %all-to-all-start.2) | async-done | bytes 262176 | tf_op jit(solution)/shard_map/all_to_all | solution.py:381
  63.9 2.0 %stats.1 = f32[16,4,128]{2,1,0:T(4,128)S(1)} custom-call(f32[32,8,256]{2,1,0:T(8,128)S(1)} %all-to-all-done.2.table_ref, s32[4,1]{1,0:T(4,128)S(1)} %copy.17.gap_ref), custom_call_target="tpu_custom_call" | custom-call | tf_op jit(solution)/shard_map/stats/pallas_call | solution.py:385
  65.9 24.2 %all_to_all.21.stats_ref = f32[16,4,128]{2,1,0:T(4,128)S(1)} all-to-all(f32[16,4,128]{2,1,0:T(4,128)S(1)} %stats.1), channel_id=1, replica_groups=mesh['rows'=32,'vocab'=16] {'vocab'}, dimensions={0} | all-to-all | bytes 65536 | tf_op jit(solution)/shard_map/all_to_all | solution.py:393
  90.1 1.0 %finish.1 = (f32[4,4]{1,0:T(4,128)S(1)}, f32[2,4]{1,0:T(2,128)}, f32[1,4]{1,0:T(1,128)}, s32[1]{0:T(128)}) custom-call(f32[16,4,128]{2,1,0:T(4,128)S(1)} %all_to_all.21.stats_ref, s32[4,1]{1,0:T(4,128)S(1)} %copy.17.gap_ref), custom_call_target="tpu_custom_call" | custom-call | tf_op jit(solution)/shard_map/finish/pallas_call | solution.py:394
  91.8 0.0 copy-start.4
  91.8 0.6 copy-done.4
  (1 shorter events, 0.0 us)
Async XLA Ops:
  0.6 54.3 %copy-start = (s32[128]{0:T(128)S(1)}, s32[128]{0:T(128)}, u32[]{:S(2)}) copy-start(s32[128]{0:T(128)} %param.19) | copy-start | bytes 1540
  3.2 35.0 %copy-start.3 = (s32[128]{0:T(128)S(1)}, s32[128]{0:T(128)}, u32[]{:S(2)}) copy-start(s32[128]{0:T(128)} %param.18) | copy-start | bytes 1540
  35.9 3.8 %copy-start.1 = (bf16[32,8,2944]{2,1,0:T(8,128)(2,1)}, bf16[32,8,2944]{2,1,0:T(8,128)(2,1)S(1)}, u32[]{:S(2)}) copy-start(bf16[32,8,2944]{2,1,0:T(8,128)(2,1)S(1)} %all_to_all.20) | copy-start | bytes 4521988
  35.9 7.9 %collective-permute-start = (bf16[256,2944]{1,0:T(8,128)(2,1)S(1)}, bf16[256,2944]{1,0:T(8,128)(2,1)S(1)}, u32[]{:S(2)}, u32[]{:S(2)}) collective-permute-start(bf16[256,2944]{1,0:T(8,128)(2,1)S(1)} %bitcast.11), channel_id=1, source_target_pairs={{0,16},{16,0},{32,48},{48,32},{64,80},{80,64},{96,112},{112,96},{1... | collective-permute-start | bytes 4521992 | tf_op jit(solution)/shard_map/ppermute | solution.py:351
  43.9 1.1 %copy-start.2 = (bf16[256,2944]{1,0:T(8,128)(2,1)}, bf16[256,2944]{1,0:T(8,128)(2,1)S(1)}, u32[]{:S(2)}) copy-start(bf16[256,2944]{1,0:T(8,128)(2,1)S(1)} %collective-permute-done.part_ref) | copy-start | bytes 4521988
  51.2 12.7 %all-to-all-start.2 = ((f32[32,8,256]{2,1,0:T(8,128)}), f32[32,8,256]{2,1,0:T(8,128)S(1)}, u32[]{:S(2)}, u32[]{:S(2)}) async-start(f32[32,8,256]{2,1,0:T(8,128)} %second_half.1), calls=%async_computation.2 | async-start | bytes 524288 | tf_op jit(solution)/shard_map/all_to_all | solution.py:381
  91.8 0.6 copy-start.4

commit v6 on v5

--- a/solution.py
+++ b/solution.py
@@ -18,11 +18,10 @@
 norm_epsilon = 1e-06
 
 VMEM = pl.BlockSpec(memory_space=pltpu.VMEM)
-ANY = pl.BlockSpec(memory_space=pl.ANY)
+HBM = pl.BlockSpec(memory_space=pltpu.HBM)
 SMEM = pl.BlockSpec(memory_space=pltpu.SMEM)
+WIDE_PARAMS = pltpu.CompilerParams(vmem_limit_bytes=60 * 1024 * 1024)
 PARAMS = pltpu.CompilerParams(vmem_limit_bytes=16 * 1024 * 1024)
-PRODUCT_PARAMS = pltpu.CompilerParams(vmem_limit_bytes=54 * 1024 * 1024)
-WIDE_PARAMS = pltpu.CompilerParams(vmem_limit_bytes=60 * 1024 * 1024)
 
 
 def norm_kernel(*refs):
@@ -52,43 +51,17 @@
                     out_ref[dest, own * p:own * p + own, 128 * i:128 * i + 128] = chunk
 
 
-def chunked(core, part_ref, head_refs, held, sems):
-    part_buf, head_bufs = held
-    columns = part_ref.shape[1]
-    quarter_e = head_refs[0].shape[1] // 4
-    chunks = [(0, 0, quarter_e // 2), (0, quarter_e // 2, quarter_e // 2), (1, quarter_e, columns - quarter_e)]
-    copies = []
-    for i, (model, low, size) in enumerate(chunks):
-        here = pl.ds(low, size)
-        own = [pltpu.make_async_copy(part_ref.at[:, here], part_buf.at[:, here], sems.at[i, 2])]
-        quarter = head_refs[model].shape[1] // 4
-        inside = low - (quarter_e if model else 0)
+def half_sums(core, part_ref, head_refs, acc_ref):
+    low = 0
+    for model, head in enumerate(head_refs):
+        size = head.shape[1] // 4
         for p in range(2):
-            source = pl.ds(pl.multiple_of((2 * core + p) * quarter + inside, 128), size)
-            own.append(pltpu.make_async_copy(
-                head_refs[model].at[:, source], head_bufs.at[p, :, here], sems.at[i, p]
-            ))
-        for copy in own:
-            copy.start()
-        copies.append(own)
-    for (model, low, size), own in zip(chunks, copies):
-        for copy in own:
-            copy.wait()
-        yield model, [
-            lax.dot_general(
-                part_buf[:, low:low + size], head_bufs[p, :, low:low + size],
-                (((1,), (1,)), ((), ())), preferred_element_type=jnp.float32,
+            columns = pl.ds(pl.multiple_of((2 * core + p) * size, 128), size)
+            acc_ref[model, p] = lax.dot_general(
+                part_ref[:, low:low + size], head[:, columns], (((1,), (1,)), ((), ())),
+                preferred_element_type=jnp.float32,
             )
-            for p in range(2)
-        ]
-
-
-def half_sums(core, part_ref, head_refs, held, sems, acc_ref):
-    started = set()
-    for model, sums in chunked(core, part_ref, head_refs, held, sems):
-        for p, total in enumerate(sums):
-            acc_ref[model, p] = acc_ref[model, p] + total if model in started else total
-        started.add(model)
+        low += size
 
 
 def quarters_joined(acc_ref, model, owner, own):
@@ -96,20 +69,19 @@
     return acc_ref[model, 0, at:at + own, :] + acc_ref[model, 1, at + own:at + 2 * own, :]
 
 
-def first_kernel(pos_ref, part_ref, he_ref, ha_ref, out_ref, part_buf, head_bufs, sems, acc_ref):
-    half_sums(pos_ref[0], part_ref, (he_ref, ha_ref), (part_buf, head_bufs), sems, acc_ref)
+def first_kernel(pos_ref, part_ref, he_ref, ha_ref, out_ref, acc_ref):
+    half_sums(pos_ref[0], part_ref, (he_ref, ha_ref), acc_ref)
     for model in range(2):
         for owner in range(out_ref.shape[1]):
             out_ref[model, owner] = quarters_joined(acc_ref, model, owner, out_ref.shape[2])
 
 
 def second_kernel(
-    pos_ref, part_ref, he_ref, ha_ref, first_ref, live_ref, ids_ref, out_ref,
-    part_buf, head_bufs, sems, acc_ref,
+    pos_ref, part_ref, he_ref, ha_ref, first_ref, live_ref, ids_ref, out_ref, acc_ref
 ):
     width = he_ref.shape[0]
     own = ids_ref.shape[1]
-    half_sums(1 - pos_ref[0], part_ref, (he_ref, ha_ref), (part_buf, head_bufs), sems, acc_ref)
+    half_sums(1 - pos_ref[0], part_ref, (he_ref, ha_ref), acc_ref)
     live = live_ref[...] == 1
     positions = pos_ref[1] + lax.broadcasted_iota(jnp.int32, (1, width), 1)
     half = width // 2
@@ -340,7 +312,7 @@
     blocks = pl.pallas_call(
         norm_kernel,
         out_shape=jax.ShapeDtypeStruct((rows, 2 * own, quarter), jnp.bfloat16),
-        in_specs=[ANY] * 4,
+        in_specs=[HBM] * 4,
         out_specs=VMEM,
         scratch_shapes=[pltpu.VMEM(x.shape, x.dtype) for x in norm_inputs]
         + [pltpu.SemaphoreType.DMA((4,))],
@@ -352,29 +324,24 @@
     cost = pl.CostEstimate(
         flops=4 * beams * width * 2 * quarter, bytes_accessed=4 * beams * quarter, transcendentals=0
     )
-    buffers = [
-        pltpu.VMEM((2 * beams, quarter), jnp.bfloat16),
-        pltpu.VMEM((2, width, quarter), jnp.bfloat16),
-        pltpu.SemaphoreType.DMA((3, 3)),
-        pltpu.VMEM((2, 2, 2 * beams, width), jnp.float32),
-    ]
+    buffers = [pltpu.VMEM((2, 2, 2 * beams, width), jnp.float32)]
     first = pl.pallas_call(
         first_kernel,
         out_shape=jax.ShapeDtypeStruct((2, rows, own, width), jnp.float32),
-        in_specs=[SMEM] + [ANY] * 3,
+        in_specs=[SMEM] + [VMEM] * 3,
         out_specs=VMEM,
         scratch_shapes=buffers,
-        compiler_params=PRODUCT_PARAMS,
+        compiler_params=PARAMS,
         cost_estimate=cost,
         name="first_half",
     )(position, half, expert_head, amateur_head)
     table = pl.pallas_call(
         second_kernel,
         out_shape=jax.ShapeDtypeStruct((rows, 2 * own, 256), jnp.float32),
-        in_specs=[SMEM] + [ANY] * 3 + [VMEM] * 3,
+        in_specs=[SMEM] + [VMEM] * 6,
         out_specs=VMEM,
         scratch_shapes=buffers,
-        compiler_params=PRODUCT_PARAMS,
+        compiler_params=PARAMS,
         cost_estimate=cost,
         name="second_half",
     )(position, other_half, expert_head, amateur_head, first, live_mask.reshape(1, -1), ids)

time: 92.8 us -> 87.8 us (0.946)
  Pallas kernels: 15.9 us -> 11.8 us
    pallas_call x1, Pallas kernels: 6.2 us -> 3.53 us  [per_device(): pl.pallas_call(second_kernel, out_shape=jax.ShapeDtypeStruct((rows, 2 * o...]
    pallas_call x1, Pallas kernels: 4.11 us -> 2.48 us  [per_device(): pl.pallas_call(first_kernel, out_shape=jax.ShapeDtypeStruct((2, rows, own...]
    unnamed x10 -> x12, local copies, waits for them, and re-layouts: 1.72 us -> 1.94 us
  transfers between devices with their start and end apart: 2 -> 2, of which waited for: 1 -> 1; matrix products, arithmetic and copies ran while one was open for 2% -> 1% of each run, Pallas kernels for 4% -> 3%
where the time goes in v6:
time: 87.8 us; the launch traced here: 87.4 us
  blocking collectives  57 us (65%)
  Pallas kernels  11.8 us (13%)
  waiting for transfers between devices  8.79 us (10%)
  starting transfers between devices  5.96 us (7%)
  local copies, waits for them, and re-layouts  2.36 us (3%)
  between operations  1.43 us (2%)
    all_to_all x1, blocking collectives, per_device(): lax.all_to_all(blocks, 'rows', 0, 0, tiled=True).reshape(2 * beams, quarter)  33.4 us
    all_to_all x1, blocking collectives, per_device(): stats = lax.all_to_all(stats, 'vocab', 0, 0, tiled=True)  23.6 us
    all_to_all x1, waiting for transfers between devices, per_device(): table = lax.all_to_all(table, 'rows', 0, 0, tiled=True)  8.79 us
    all_to_all x1, starting transfers between devices, per_device(): table = lax.all_to_all(table, 'rows', 0, 0, tiled=True)  3.66 us
    pallas_call x1, Pallas kernels, per_device(): pl.pallas_call(second_kernel, out_shape=jax.ShapeDtypeStruct((rows, 2 * o...  3.53 us
    pallas_call x1, Pallas kernels, per_device(): pl.pallas_call(norm_kernel, out_shape=jax.ShapeDtypeStruct((rows, 2 * own...  2.72 us
    pallas_call x1, Pallas kernels, per_device(): pl.pallas_call(first_kernel, out_shape=jax.ShapeDtypeStruct((2, rows, own...  2.48 us
    ppermute x1, starting transfers between devices, per_device(): other_half = lax.ppermute(half, 'rows', [(r, r ^ 1) for r in range(rows)])  2.29 us
  transfers between devices with their start and end apart: 2, of which 1 were waited for; matrix products, arithmetic and copies ran while one was open for 1% of the time, Pallas kernels for 3%

profile of v6, /device:TPU:1, one launch (start us, length us, event | category | flops | bytes accessed | tf_op | source)
XLA Modules:
  0.0 87.4 jit_solution(16427128720089403803)
XLA Ops:
  0.6 0.0 copy-start
  0.6 0.0 copy-start.1
  0.7 2.7 %norms.1 = bf16[32,8,2944]{2,1,0:T(8,128)(2,1)} custom-call(bf16[4,8192]{1,0:T(4,128)(2,1)} %refs_0_.1, bf16[64,128]{1,0:T(8,128)(2,1)} %bitcast.12, bf16[4,3584]{1,0:T(4,128)(2,1)} %refs_2_.1, bf16[28,128]{1,0:T(8,128)(2,1)} %bitcast.13), custom_call_target="tpu_custom_call" | custom-call | tf_op jit(solution)/shard_map/norms/pallas_call | solution.py:312
  3.4 0.0 copy-start.4
  3.4 33.4 %all_to_all.20 = bf16[32,8,2944]{2,1,0:T(8,128)(2,1)} all-to-all(bf16[32,8,2944]{2,1,0:T(8,128)(2,1)} %norms.1), channel_id=1, replica_groups=mesh['rows'=32,'vocab'=16] {'rows'}, dimensions={0} | all-to-all | bytes 3014656 | tf_op jit(solution)/shard_map/all_to_all | solution.py:322
  36.8 2.3 %collective-permute-start = (bf16[256,2944]{1,0:T(8,128)(2,1)}, bf16[256,2944]{1,0:T(8,128)(2,1)}, u32[]{:S(2)}, u32[]{:S(2)}) collective-permute-start(bf16[256,2944]{1,0:T(8,128)(2,1)} %bitcast.4.part_ref), channel_id=1, source_target_pairs={{0,16},{16,0},{32,48},{48,32},{64,80},{80,64},{96,112},{112,96},{1... | collective-permute-start | bytes 4521992 | tf_op jit(solution)/shard_map/ppermute | solution.py:323
  39.1 0.0 copy-done.4
  39.1 0.2 reshape.39.ids_ref
  39.4 0.1 pad_add_fusion.pos_ref
  39.5 0.0 copy-done.1
  39.5 0.0 copy-start.2
  39.5 1.3 %copy-done.2 = bf16[192,3584]{1,0:T(8,128)(2,1)S(1)} copy-done((bf16[192,3584]{1,0:T(8,128)(2,1)S(1)}, bf16[192,3584]{1,0:T(8,128)(2,1)}, u32[]{:S(2)}) %copy-start.2) | copy-done | bytes 1376280
  40.8 0.0 copy-start.3
  40.8 2.5 %first_half.1.first_ref = f32[2,32,4,192]{3,2,1,0:T(4,128)S(1)} custom-call(s32[2]{0:T(128)S(1)} %pad_add_fusion.pos_ref, bf16[256,2944]{1,0:T(8,128)(2,1)} %bitcast.4.part_ref, bf16[192,8192]{1,0:T(8,128)(2,1)S(1)} %copy-done.1, bf16[192,3584]{1,0:T(8,128)(2,1)S(1)} %copy-done.2), custom_call_target="tpu_custom_call" | custom-call | flops 578813952 | bytes 1507328 | tf_op jit(solution)/shard_map/first_half/pallas_call | solution.py:328
  43.3 0.0 collective-permute-done.part_ref
  43.3 0.0 copy-done.3
  43.3 3.5 %second_half.1 = f32[32,8,256]{2,1,0:T(8,128)} custom-call(s32[2]{0:T(128)S(1)} %pad_add_fusion.pos_ref, bf16[256,2944]{1,0:T(8,128)(2,1)} %collective-permute-done.part_ref, bf16[192,8192]{1,0:T(8,128)(2,1)S(1)} %copy-done.1, bf16[192,3584]{1,0:T(8,128)(2,1)S(1)} %copy-done.2, f32[2,32,4,192]{3,2,1,0:T(4,128)S(1)} %first_half.1.first_ref, ...), custom_call_target="tpu_custom_call" | custom-call | flops 578813952 | bytes 1507328 | tf_op jit(solution)/shard_map/second_half/pallas_call | solution.py:338
  46.9 3.7 %all-to-all-start.2 = ((f32[32,8,256]{2,1,0:T(8,128)}), f32[32,8,256]{2,1,0:T(8,128)S(1)}, u32[]{:S(2)}, u32[]{:S(2)}) async-start(f32[32,8,256]{2,1,0:T(8,128)} %second_half.1), calls=%async_computation.2 | async-start | bytes 524288 | tf_op jit(solution)/shard_map/all_to_all | solution.py:348
  50.5 0.0 copy-done
  50.5 0.1 dynamic-slice_bitcast_fusion
  50.6 0.1 copy.17.gap_ref
  50.7 8.8 %all-to-all-done.2.table_ref = f32[32,8,256]{2,1,0:T(8,128)S(1)} async-done(((f32[32,8,256]{2,1,0:T(8,128)}), f32[32,8,256]{2,1,0:T(8,128)S(1)}, u32[]{:S(2)}, u32[]{:S(2)}) %all-to-all-start.2) | async-done | bytes 262176 | tf_op jit(solution)/shard_map/all_to_all | solution.py:348
  59.5 2.0 %stats.1 = f32[16,4,128]{2,1,0:T(4,128)S(1)} custom-call(f32[32,8,256]{2,1,0:T(8,128)S(1)} %all-to-all-done.2.table_ref, s32[4,1]{1,0:T(4,128)S(1)} %copy.17.gap_ref), custom_call_target="tpu_custom_call" | custom-call | tf_op jit(solution)/shard_map/stats/pallas_call | solution.py:352
  61.5 23.6 %all_to_all.21.stats_ref = f32[16,4,128]{2,1,0:T(4,128)S(1)} all-to-all(f32[16,4,128]{2,1,0:T(4,128)S(1)} %stats.1), channel_id=1, replica_groups=mesh['rows'=32,'vocab'=16] {'vocab'}, dimensions={0} | all-to-all | bytes 65536 | tf_op jit(solution)/shard_map/all_to_all | solution.py:360
  85.1 1.0 %finish.1 = (f32[4,4]{1,0:T(4,128)S(1)}, f32[2,4]{1,0:T(2,128)}, f32[1,4]{1,0:T(1,128)}, s32[1]{0:T(128)}) custom-call(f32[16,4,128]{2,1,0:T(4,128)S(1)} %all_to_all.21.stats_ref, s32[4,1]{1,0:T(4,128)S(1)} %copy.17.gap_ref), custom_call_target="tpu_custom_call" | custom-call | tf_op jit(solution)/shard_map/finish/pallas_call | solution.py:361
  86.8 0.0 copy-start.5
  86.8 0.6 copy-done.5
  (1 shorter events, 0.0 us)
Async XLA Ops:
  0.6 49.9 %copy-start = (s32[128]{0:T(128)S(1)}, s32[128]{0:T(128)}, u32[]{:S(2)}) copy-start(s32[128]{0:T(128)} %param.19) | copy-start | bytes 1540
  0.6 38.8 %copy-start.1 = (bf16[192,8192]{1,0:T(8,128)(2,1)S(1)}, bf16[192,8192]{1,0:T(8,128)(2,1)}, u32[]{:S(2)}) copy-start(bf16[192,8192]{1,0:T(8,128)(2,1)} %he_ref.3) | copy-start | bytes 9437188
  3.4 35.7 %copy-start.4 = (s32[128]{0:T(128)S(1)}, s32[128]{0:T(128)}, u32[]{:S(2)}) copy-start(s32[128]{0:T(128)} %param.18) | copy-start | bytes 1540
  36.8 6.5 %collective-permute-start = (bf16[256,2944]{1,0:T(8,128)(2,1)}, bf16[256,2944]{1,0:T(8,128)(2,1)}, u32[]{:S(2)}, u32[]{:S(2)}) collective-permute-start(bf16[256,2944]{1,0:T(8,128)(2,1)} %bitcast.4.part_ref), channel_id=1, source_target_pairs={{0,16},{16,0},{32,48},{48,32},{64,80},{80,64},{96,112},{112,96},{1... | collective-permute-start | bytes 4521992 | tf_op jit(solution)/shard_map/ppermute | solution.py:323
  39.5 1.3 %copy-start.2 = (bf16[192,3584]{1,0:T(8,128)(2,1)S(1)}, bf16[192,3584]{1,0:T(8,128)(2,1)}, u32[]{:S(2)}) copy-start(bf16[192,3584]{1,0:T(8,128)(2,1)} %ha_ref.3) | copy-start | bytes 4128772
  40.8 2.5 %copy-start.3 = (s32[192]{0:T(256)S(1)}, s32[192]{0:T(256)}, u32[]{:S(2)}) copy-start(s32[192]{0:T(256)} %param.17) | copy-start | bytes 2308
  46.9 12.6 %all-to-all-start.2 = ((f32[32,8,256]{2,1,0:T(8,128)}), f32[32,8,256]{2,1,0:T(8,128)S(1)}, u32[]{:S(2)}, u32[]{:S(2)}) async-start(f32[32,8,256]{2,1,0:T(8,128)} %second_half.1), calls=%async_computation.2 | async-start | bytes 524288 | tf_op jit(solution)/shard_map/all_to_all | solution.py:348
  86.8 0.6 copy-start.5

commit v7 on v6

--- a/solution.py
+++ b/solution.py
@@ -25,30 +25,33 @@
 
 
 def norm_kernel(*refs):
-    inputs, out_ref, held, sems = refs[:4], refs[4], refs[5:9], refs[9]
+    inputs, out_ref, held, block_ref, sems, out_sems = refs[:4], refs[4], refs[5:9], *refs[9:]
     copies = [pltpu.make_async_copy(inputs[i], held[i], sems.at[i]) for i in range(4)]
     for copy in copies:
         copy.start()
-    for copy in copies:
-        copy.wait()
-    own, quarters = held[0].shape[0], []
-    for hidden, gains in ((held[0], held[1]), (held[2], held[3])):
-        values = hidden[...].astype(jnp.float32)
-        gain = gains[...].astype(jnp.float32)
+    quarters = []
+    for model in range(2):
+        copies[2 * model].wait()
+        copies[2 * model + 1].wait()
+        values = held[2 * model][...].astype(jnp.float32)
+        gain = held[2 * model + 1][...].astype(jnp.float32)
         mean = jnp.mean(values * values, axis=-1, keepdims=True)
         values = values * lax.rsqrt(mean + norm_epsilon)
         chunks = [
-            (values[:, 128 * i:128 * i + 128] * gain[i:i + 1, :]).astype(jnp.bfloat16)
-            for i in range(values.shape[1] // 128)
+            values[:, 128 * i:128 * i + 128] * gain[i:i + 1, :] for i in range(values.shape[1] // 128)
         ]
         each = len(chunks) // 4
         quarters.append([chunks[each * q:each * q + each] for q in range(4)])
+    sent = []
     for core in range(NC):
-        for p in range(2):
-            q = 2 * core + p
-            for i, chunk in enumerate(quarters[0][q] + quarters[1][q]):
-                for dest in range(core, out_ref.shape[0], NC):
-                    out_ref[dest, own * p:own * p + own, 128 * i:128 * i + 128] = chunk
+        rows = [quarters[0][2 * core + p] + quarters[1][2 * core + p] for p in range(2)]
+        for i, pair in enumerate(zip(*rows)):
+            block_ref[core, :, 128 * i:128 * i + 128] = jnp.concatenate(pair).astype(jnp.bfloat16)
+        for dest in range(core, out_ref.shape[0], NC):
+            sent.append(pltpu.make_async_copy(block_ref.at[core], out_ref.at[dest], out_sems.at[dest]))
+            sent[-1].start()
+    for copy in sent:
+        copy.wait()
 
 
 def half_sums(core, part_ref, head_refs, acc_ref):
@@ -313,9 +316,12 @@
         norm_kernel,
         out_shape=jax.ShapeDtypeStruct((rows, 2 * own, quarter), jnp.bfloat16),
         in_specs=[HBM] * 4,
-        out_specs=VMEM,
-        scratch_shapes=[pltpu.VMEM(x.shape, x.dtype) for x in norm_inputs]
-        + [pltpu.SemaphoreType.DMA((4,))],
+        out_specs=HBM,
+        scratch_shapes=[pltpu.VMEM(x.shape, x.dtype) for x in norm_inputs] + [
+            pltpu.VMEM((NC, 2 * own, quarter), jnp.bfloat16),
+            pltpu.SemaphoreType.DMA((4,)),
+            pltpu.SemaphoreType.DMA((rows,)),
+        ],
         compiler_params=WIDE_PARAMS,
         name="norms",
     )(*norm_inputs)

time: 87.8 us -> 87.9 us (level)
  no operation moved by 1% of the time
where the time goes in v7:
time: 87.9 us; the launch traced here: 87.4 us
  blocking collectives  57 us (65%)
  Pallas kernels  11.8 us (13%)
  waiting for transfers between devices  8.79 us (10%)
  starting transfers between devices  5.96 us (7%)
  local copies, waits for them, and re-layouts  2.36 us (3%)
  between operations  1.43 us (2%)
    all_to_all x1, blocking collectives, per_device(): lax.all_to_all(blocks, 'rows', 0, 0, tiled=True).reshape(2 * beams, quarter)  33.4 us
    all_to_all x1, blocking collectives, per_device(): stats = lax.all_to_all(stats, 'vocab', 0, 0, tiled=True)  23.6 us
    all_to_all x1, waiting for transfers between devices, per_device(): table = lax.all_to_all(table, 'rows', 0, 0, tiled=True)  8.79 us
    all_to_all x1, starting transfers between devices, per_device(): table = lax.all_to_all(table, 'rows', 0, 0, tiled=True)  3.67 us
    pallas_call x1, Pallas kernels, per_device(): pl.pallas_call(second_kernel, out_shape=jax.ShapeDtypeStruct((rows, 2 * o...  3.53 us
    pallas_call x1, Pallas kernels, per_device(): pl.pallas_call(norm_kernel, out_shape=jax.ShapeDtypeStruct((rows, 2 * own...  2.75 us
    pallas_call x1, Pallas kernels, per_device(): pl.pallas_call(first_kernel, out_shape=jax.ShapeDtypeStruct((2, rows, own...  2.48 us
    ppermute x1, starting transfers between devices, per_device(): other_half = lax.ppermute(half, 'rows', [(r, r ^ 1) for r in range(rows)])  2.29 us
  transfers between devices with their start and end apart: 2, of which 1 were waited for; matrix products, arithmetic and copies ran while one was open for 1% of the time, Pallas kernels for 3%

profile of v7, /device:TPU:1, one launch (start us, length us, event | category | flops | bytes accessed | tf_op | source)
XLA Modules:
  0.0 87.4 jit_solution(9738596128952614192)
XLA Ops:
  0.6 0.0 copy-start
  0.6 0.0 copy-start.1
  0.7 2.8 %norms.1 = bf16[32,8,2944]{2,1,0:T(8,128)(2,1)} custom-call(bf16[4,8192]{1,0:T(4,128)(2,1)} %refs_0_.1, bf16[64,128]{1,0:T(8,128)(2,1)} %bitcast.12, bf16[4,3584]{1,0:T(4,128)(2,1)} %refs_2_.1, bf16[28,128]{1,0:T(8,128)(2,1)} %bitcast.13), custom_call_target="tpu_custom_call" | custom-call | tf_op jit(solution)/shard_map/norms/pallas_call | solution.py:315
  3.4 0.0 copy-start.4
  3.4 33.4 %all_to_all.20 = bf16[32,8,2944]{2,1,0:T(8,128)(2,1)} all-to-all(bf16[32,8,2944]{2,1,0:T(8,128)(2,1)} %norms.1), channel_id=1, replica_groups=mesh['rows'=32,'vocab'=16] {'rows'}, dimensions={0} | all-to-all | bytes 3014656 | tf_op jit(solution)/shard_map/all_to_all | solution.py:328
  36.9 2.3 %collective-permute-start = (bf16[256,2944]{1,0:T(8,128)(2,1)}, bf16[256,2944]{1,0:T(8,128)(2,1)}, u32[]{:S(2)}, u32[]{:S(2)}) collective-permute-start(bf16[256,2944]{1,0:T(8,128)(2,1)} %bitcast.4.part_ref), channel_id=1, source_target_pairs={{0,16},{16,0},{32,48},{48,32},{64,80},{80,64},{96,112},{112,96},{1... | collective-permute-start | bytes 4521992 | tf_op jit(solution)/shard_map/ppermute | solution.py:329
  39.2 0.0 copy-done.4
  39.2 0.2 reshape.39.ids_ref
  39.4 0.1 pad_add_fusion.pos_ref
  39.5 0.0 copy-done.1
  39.5 0.0 copy-start.2
  39.5 1.3 %copy-done.2 = bf16[192,3584]{1,0:T(8,128)(2,1)S(1)} copy-done((bf16[192,3584]{1,0:T(8,128)(2,1)S(1)}, bf16[192,3584]{1,0:T(8,128)(2,1)}, u32[]{:S(2)}) %copy-start.2) | copy-done | bytes 1376280
  40.9 0.0 copy-start.3
  40.9 2.5 %first_half.1.first_ref = f32[2,32,4,192]{3,2,1,0:T(4,128)S(1)} custom-call(s32[2]{0:T(128)S(1)} %pad_add_fusion.pos_ref, bf16[256,2944]{1,0:T(8,128)(2,1)} %bitcast.4.part_ref, bf16[192,8192]{1,0:T(8,128)(2,1)S(1)} %copy-done.1, bf16[192,3584]{1,0:T(8,128)(2,1)S(1)} %copy-done.2), custom_call_target="tpu_custom_call" | custom-call | flops 578813952 | bytes 1507328 | tf_op jit(solution)/shard_map/first_half/pallas_call | solution.py:334
  43.3 0.0 collective-permute-done.part_ref
  43.4 0.0 copy-done.3
  43.4 3.5 %second_half.1 = f32[32,8,256]{2,1,0:T(8,128)} custom-call(s32[2]{0:T(128)S(1)} %pad_add_fusion.pos_ref, bf16[256,2944]{1,0:T(8,128)(2,1)} %collective-permute-done.part_ref, bf16[192,8192]{1,0:T(8,128)(2,1)S(1)} %copy-done.1, bf16[192,3584]{1,0:T(8,128)(2,1)S(1)} %copy-done.2, f32[2,32,4,192]{3,2,1,0:T(4,128)S(1)} %first_half.1.first_ref, ...), custom_call_target="tpu_custom_call" | custom-call | flops 578813952 | bytes 1507328 | tf_op jit(solution)/shard_map/second_half/pallas_call | solution.py:344
  46.9 3.7 %all-to-all-start.2 = ((f32[32,8,256]{2,1,0:T(8,128)}), f32[32,8,256]{2,1,0:T(8,128)S(1)}, u32[]{:S(2)}, u32[]{:S(2)}) async-start(f32[32,8,256]{2,1,0:T(8,128)} %second_half.1), calls=%async_computation.2 | async-start | bytes 524288 | tf_op jit(solution)/shard_map/all_to_all | solution.py:354
  50.6 0.0 copy-done
  50.6 0.1 dynamic-slice_bitcast_fusion
  50.7 0.1 copy.17.gap_ref
  50.8 8.8 %all-to-all-done.2.table_ref = f32[32,8,256]{2,1,0:T(8,128)S(1)} async-done(((f32[32,8,256]{2,1,0:T(8,128)}), f32[32,8,256]{2,1,0:T(8,128)S(1)}, u32[]{:S(2)}, u32[]{:S(2)}) %all-to-all-start.2) | async-done | bytes 262176 | tf_op jit(solution)/shard_map/all_to_all | solution.py:354
  59.5 2.0 %stats.1 = f32[16,4,128]{2,1,0:T(4,128)S(1)} custom-call(f32[32,8,256]{2,1,0:T(8,128)S(1)} %all-to-all-done.2.table_ref, s32[4,1]{1,0:T(4,128)S(1)} %copy.17.gap_ref), custom_call_target="tpu_custom_call" | custom-call | tf_op jit(solution)/shard_map/stats/pallas_call | solution.py:358
  61.6 23.6 %all_to_all.21.stats_ref = f32[16,4,128]{2,1,0:T(4,128)S(1)} all-to-all(f32[16,4,128]{2,1,0:T(4,128)S(1)} %stats.1), channel_id=1, replica_groups=mesh['rows'=32,'vocab'=16] {'vocab'}, dimensions={0} | all-to-all | bytes 65536 | tf_op jit(solution)/shard_map/all_to_all | solution.py:366
  85.1 1.0 %finish.1 = (f32[4,4]{1,0:T(4,128)S(1)}, f32[2,4]{1,0:T(2,128)}, f32[1,4]{1,0:T(1,128)}, s32[1]{0:T(128)}) custom-call(f32[16,4,128]{2,1,0:T(4,128)S(1)} %all_to_all.21.stats_ref, s32[4,1]{1,0:T(4,128)S(1)} %copy.17.gap_ref), custom_call_target="tpu_custom_call" | custom-call | tf_op jit(solution)/shard_map/finish/pallas_call | solution.py:367
  86.9 0.0 copy-start.5
  86.9 0.6 copy-done.5
  (1 shorter events, 0.0 us)
Async XLA Ops:
  0.6 49.9 %copy-start = (s32[128]{0:T(128)S(1)}, s32[128]{0:T(128)}, u32[]{:S(2)}) copy-start(s32[128]{0:T(128)} %param.19) | copy-start | bytes 1540
  0.6 38.9 %copy-start.1 = (bf16[192,8192]{1,0:T(8,128)(2,1)S(1)}, bf16[192,8192]{1,0:T(8,128)(2,1)}, u32[]{:S(2)}) copy-start(bf16[192,8192]{1,0:T(8,128)(2,1)} %he_ref.3) | copy-start | bytes 9437188
  3.4 35.7 %copy-start.4 = (s32[128]{0:T(128)S(1)}, s32[128]{0:T(128)}, u32[]{:S(2)}) copy-start(s32[128]{0:T(128)} %param.18) | copy-start | bytes 1540
  36.9 6.5 %collective-permute-start = (bf16[256,2944]{1,0:T(8,128)(2,1)}, bf16[256,2944]{1,0:T(8,128)(2,1)}, u32[]{:S(2)}, u32[]{:S(2)}) collective-permute-start(bf16[256,2944]{1,0:T(8,128)(2,1)} %bitcast.4.part_ref), channel_id=1, source_target_pairs={{0,16},{16,0},{32,48},{48,32},{64,80},{80,64},{96,112},{112,96},{1... | collective-permute-start | bytes 4521992 | tf_op jit(solution)/shard_map/ppermute | solution.py:329
  39.5 1.3 %copy-start.2 = (bf16[192,3584]{1,0:T(8,128)(2,1)S(1)}, bf16[192,3584]{1,0:T(8,128)(2,1)}, u32[]{:S(2)}) copy-start(bf16[192,3584]{1,0:T(8,128)(2,1)} %ha_ref.3) | copy-start | bytes 4128772
  40.9 2.5 %copy-start.3 = (s32[192]{0:T(256)S(1)}, s32[192]{0:T(256)}, u32[]{:S(2)}) copy-start(s32[192]{0:T(256)} %param.17) | copy-start | bytes 2308
  46.9 12.7 %all-to-all-start.2 = ((f32[32,8,256]{2,1,0:T(8,128)}), f32[32,8,256]{2,1,0:T(8,128)S(1)}, u32[]{:S(2)}, u32[]{:S(2)}) async-start(f32[32,8,256]{2,1,0:T(8,128)} %second_half.1), calls=%async_computation.2 | async-start | bytes 524288 | tf_op jit(solution)/shard_map/all_to_all | solution.py:354
  86.9 0.6 copy-start.5

commit v8 on v7

--- a/solution.py
+++ b/solution.py
@@ -54,29 +54,41 @@
         copy.wait()
 
 
+def quarters_apart(part):
+    groups = part.reshape(part.shape[0] // 32, 2, 16, part.shape[1])
+    even, odd = groups[:, 0], groups[:, 1]
+    first = lax.broadcasted_iota(jnp.int32, even.shape, 1) % 8 < 4
+    down = pltpu.roll(odd, 4, 1)
+    up = pltpu.roll(even, 12, 1)
+    apart = jnp.where(first, even, down), jnp.where(first, up, odd)
+    return [x.reshape(part.shape[0] // 2, part.shape[1]) for x in apart]
+
+
 def half_sums(core, part_ref, head_refs, acc_ref):
     low = 0
     for model, head in enumerate(head_refs):
         size = head.shape[1] // 4
-        for p in range(2):
+        total = None
+        for p, rows in enumerate(quarters_apart(part_ref[:, low:low + size])):
             columns = pl.ds(pl.multiple_of((2 * core + p) * size, 128), size)
-            acc_ref[model, p] = lax.dot_general(
-                part_ref[:, low:low + size], head[:, columns], (((1,), (1,)), ((), ())),
-                preferred_element_type=jnp.float32,
+            product = lax.dot_general(
+                rows, head[:, columns], (((1,), (1,)), ((), ())), preferred_element_type=jnp.float32
             )
+            total = product if total is None else total + product
+        acc_ref[model] = total
         low += size
 
 
-def quarters_joined(acc_ref, model, owner, own):
-    at = 2 * own * owner
-    return acc_ref[model, 0, at:at + own, :] + acc_ref[model, 1, at + own:at + 2 * own, :]
+def sums_of(acc_ref, model, owner, own):
+    at = 4 * own * (owner // 4) + own * (0, 2, 1, 3)[owner % 4]
+    return acc_ref[model, at:at + own, :]
 
 
 def first_kernel(pos_ref, part_ref, he_ref, ha_ref, out_ref, acc_ref):
     half_sums(pos_ref[0], part_ref, (he_ref, ha_ref), acc_ref)
     for model in range(2):
         for owner in range(out_ref.shape[1]):
-            out_ref[model, owner] = quarters_joined(acc_ref, model, owner, out_ref.shape[2])
+            out_ref[model, owner] = sums_of(acc_ref, model, owner, out_ref.shape[2])
 
 
 def second_kernel(
@@ -91,7 +103,7 @@
     for owner in range(out_ref.shape[0]):
         hits = ids_ref[owner] == positions
         for model in range(2):
-            logits = first_ref[model, owner] + quarters_joined(acc_ref, model, owner, own)
+            logits = first_ref[model, owner] + sums_of(acc_ref, model, owner, own)
             pick = jnp.sum(jnp.where(hits, logits, 0.0), axis=1, keepdims=True)
             pick = jnp.broadcast_to(pick, (own, 128 - half))
             held = jnp.where(live, logits, masked_floor)
@@ -330,7 +342,7 @@
     cost = pl.CostEstimate(
         flops=4 * beams * width * 2 * quarter, bytes_accessed=4 * beams * quarter, transcendentals=0
     )
-    buffers = [pltpu.VMEM((2, 2, 2 * beams, width), jnp.float32)]
+    buffers = [pltpu.VMEM((2, beams, width), jnp.float32)]
     first = pl.pallas_call(
         first_kernel,
         out_shape=jax.ShapeDtypeStruct((2, rows, own, width), jnp.float32),

time: 87.9 us -> 88.2 us (level)
  no operation moved by 1% of the time
where the time goes in v8:
time: 88.2 us; the launch traced here: 87.7 us
  blocking collectives  57 us (65%)
  Pallas kernels  12.1 us (14%)
  waiting for transfers between devices  8.78 us (10%)
  starting transfers between devices  5.97 us (7%)
  local copies, waits for them, and re-layouts  2.36 us (3%)
  between operations  1.43 us (2%)
    all_to_all x1, blocking collectives, per_device(): lax.all_to_all(blocks, 'rows', 0, 0, tiled=True).reshape(2 * beams, quarter)  33.4 us
    all_to_all x1, blocking collectives, per_device(): stats = lax.all_to_all(stats, 'vocab', 0, 0, tiled=True)  23.6 us
    all_to_all x1, waiting for transfers between devices, per_device(): table = lax.all_to_all(table, 'rows', 0, 0, tiled=True)  8.78 us
    pallas_call x1, Pallas kernels, per_device(): pl.pallas_call(second_kernel, out_shape=jax.ShapeDtypeStruct((rows, 2 * o...  3.91 us
    all_to_all x1, starting transfers between devices, per_device(): table = lax.all_to_all(table, 'rows', 0, 0, tiled=True)  3.67 us
    pallas_call x1, Pallas kernels, per_device(): pl.pallas_call(norm_kernel, out_shape=jax.ShapeDtypeStruct((rows, 2 * own...  2.75 us
    pallas_call x1, Pallas kernels, per_device(): pl.pallas_call(first_kernel, out_shape=jax.ShapeDtypeStruct((2, rows, own...  2.41 us
    ppermute x1, starting transfers between devices, per_device(): other_half = lax.ppermute(half, 'rows', [(r, r ^ 1) for r in range(rows)])  2.29 us
  transfers between devices with their start and end apart: 2, of which 1 were waited for; matrix products, arithmetic and copies ran while one was open for 1% of the time, Pallas kernels for 3%

profile of v8, /device:TPU:1, one launch (start us, length us, event | category | flops | bytes accessed | tf_op | source)
XLA Modules:
  0.0 87.7 jit_solution(13891360526830069161)
XLA Ops:
  0.6 0.0 copy-start
  0.6 0.0 copy-start.1
  0.7 2.8 %norms.1 = bf16[32,8,2944]{2,1,0:T(8,128)(2,1)} custom-call(bf16[4,8192]{1,0:T(4,128)(2,1)} %refs_0_.1, bf16[64,128]{1,0:T(8,128)(2,1)} %bitcast.12, bf16[4,3584]{1,0:T(4,128)(2,1)} %refs_2_.1, bf16[28,128]{1,0:T(8,128)(2,1)} %bitcast.13), custom_call_target="tpu_custom_call" | custom-call | tf_op jit(solution)/shard_map/norms/pallas_call | solution.py:327
  3.4 0.0 copy-start.4
  3.4 33.4 %all_to_all.20 = bf16[32,8,2944]{2,1,0:T(8,128)(2,1)} all-to-all(bf16[32,8,2944]{2,1,0:T(8,128)(2,1)} %norms.1), channel_id=1, replica_groups=mesh['rows'=32,'vocab'=16] {'rows'}, dimensions={0} | all-to-all | bytes 3014656 | tf_op jit(solution)/shard_map/all_to_all | solution.py:340
  36.9 2.3 %collective-permute-start = (bf16[256,2944]{1,0:T(8,128)(2,1)}, bf16[256,2944]{1,0:T(8,128)(2,1)}, u32[]{:S(2)}, u32[]{:S(2)}) collective-permute-start(bf16[256,2944]{1,0:T(8,128)(2,1)} %bitcast.4.part_ref), channel_id=1, source_target_pairs={{0,16},{16,0},{32,48},{48,32},{64,80},{80,64},{96,112},{112,96},{1... | collective-permute-start | bytes 4521992 | tf_op jit(solution)/shard_map/ppermute | solution.py:341
  39.2 0.0 copy-done.4
  39.2 0.2 reshape.39.ids_ref
  39.4 0.1 pad_add_fusion.pos_ref
  39.5 0.0 copy-done.1
  39.5 0.0 copy-start.2
  39.5 1.3 %copy-done.2 = bf16[192,3584]{1,0:T(8,128)(2,1)S(1)} copy-done((bf16[192,3584]{1,0:T(8,128)(2,1)S(1)}, bf16[192,3584]{1,0:T(8,128)(2,1)}, u32[]{:S(2)}) %copy-start.2) | copy-done | bytes 1376280
  40.9 0.0 copy-start.3
  40.9 2.4 %first_half.1.first_ref = f32[2,32,4,192]{3,2,1,0:T(4,128)S(1)} custom-call(s32[2]{0:T(128)S(1)} %pad_add_fusion.pos_ref, bf16[256,2944]{1,0:T(8,128)(2,1)} %bitcast.4.part_ref, bf16[192,8192]{1,0:T(8,128)(2,1)S(1)} %copy-done.1, bf16[192,3584]{1,0:T(8,128)(2,1)S(1)} %copy-done.2), custom_call_target="tpu_custom_call" | custom-call | flops 578813952 | bytes 1507328 | tf_op jit(solution)/shard_map/first_half/pallas_call | solution.py:346
  43.3 0.0 collective-permute-done.part_ref
  43.3 0.0 copy-done.3
  43.3 3.9 %second_half.1 = f32[32,8,256]{2,1,0:T(8,128)} custom-call(s32[2]{0:T(128)S(1)} %pad_add_fusion.pos_ref, bf16[256,2944]{1,0:T(8,128)(2,1)} %collective-permute-done.part_ref, bf16[192,8192]{1,0:T(8,128)(2,1)S(1)} %copy-done.1, bf16[192,3584]{1,0:T(8,128)(2,1)S(1)} %copy-done.2, f32[2,32,4,192]{3,2,1,0:T(4,128)S(1)} %first_half.1.first_ref, ...), custom_call_target="tpu_custom_call" | custom-call | flops 578813952 | bytes 1507328 | tf_op jit(solution)/shard_map/second_half/pallas_call | solution.py:356
  47.2 3.7 %all-to-all-start.2 = ((f32[32,8,256]{2,1,0:T(8,128)}), f32[32,8,256]{2,1,0:T(8,128)S(1)}, u32[]{:S(2)}, u32[]{:S(2)}) async-start(f32[32,8,256]{2,1,0:T(8,128)} %second_half.1), calls=%async_computation.2 | async-start | bytes 524288 | tf_op jit(solution)/shard_map/all_to_all | solution.py:366
  50.9 0.0 copy-done
  50.9 0.1 dynamic-slice_bitcast_fusion
  51.0 0.1 copy.17.gap_ref
  51.1 8.8 %all-to-all-done.2.table_ref = f32[32,8,256]{2,1,0:T(8,128)S(1)} async-done(((f32[32,8,256]{2,1,0:T(8,128)}), f32[32,8,256]{2,1,0:T(8,128)S(1)}, u32[]{:S(2)}, u32[]{:S(2)}) %all-to-all-start.2) | async-done | bytes 262176 | tf_op jit(solution)/shard_map/all_to_all | solution.py:366
  59.9 2.0 %stats.1 = f32[16,4,128]{2,1,0:T(4,128)S(1)} custom-call(f32[32,8,256]{2,1,0:T(8,128)S(1)} %all-to-all-done.2.table_ref, s32[4,1]{1,0:T(4,128)S(1)} %copy.17.gap_ref), custom_call_target="tpu_custom_call" | custom-call | tf_op jit(solution)/shard_map/stats/pallas_call | solution.py:370
  61.9 23.6 %all_to_all.21.stats_ref = f32[16,4,128]{2,1,0:T(4,128)S(1)} all-to-all(f32[16,4,128]{2,1,0:T(4,128)S(1)} %stats.1), channel_id=1, replica_groups=mesh['rows'=32,'vocab'=16] {'vocab'}, dimensions={0} | all-to-all | bytes 65536 | tf_op jit(solution)/shard_map/all_to_all | solution.py:378
  85.5 1.0 %finish.1 = (f32[4,4]{1,0:T(4,128)S(1)}, f32[2,4]{1,0:T(2,128)}, f32[1,4]{1,0:T(1,128)}, s32[1]{0:T(128)}) custom-call(f32[16,4,128]{2,1,0:T(4,128)S(1)} %all_to_all.21.stats_ref, s32[4,1]{1,0:T(4,128)S(1)} %copy.17.gap_ref), custom_call_target="tpu_custom_call" | custom-call | tf_op jit(solution)/shard_map/finish/pallas_call | solution.py:379
  87.2 0.0 copy-start.5
  87.2 0.6 copy-done.5
  (1 shorter events, 0.0 us)
Async XLA Ops:
  0.6 50.3 %copy-start = (s32[128]{0:T(128)S(1)}, s32[128]{0:T(128)}, u32[]{:S(2)}) copy-start(s32[128]{0:T(128)} %param.19) | copy-start | bytes 1540
  0.6 38.9 %copy-start.1 = (bf16[192,8192]{1,0:T(8,128)(2,1)S(1)}, bf16[192,8192]{1,0:T(8,128)(2,1)}, u32[]{:S(2)}) copy-start(bf16[192,8192]{1,0:T(8,128)(2,1)} %he_ref.3) | copy-start | bytes 9437188
  3.4 35.7 %copy-start.4 = (s32[128]{0:T(128)S(1)}, s32[128]{0:T(128)}, u32[]{:S(2)}) copy-start(s32[128]{0:T(128)} %param.18) | copy-start | bytes 1540
  36.9 6.4 %collective-permute-start = (bf16[256,2944]{1,0:T(8,128)(2,1)}, bf16[256,2944]{1,0:T(8,128)(2,1)}, u32[]{:S(2)}, u32[]{:S(2)}) collective-permute-start(bf16[256,2944]{1,0:T(8,128)(2,1)} %bitcast.4.part_ref), channel_id=1, source_target_pairs={{0,16},{16,0},{32,48},{48,32},{64,80},{80,64},{96,112},{112,96},{1... | collective-permute-start | bytes 4521992 | tf_op jit(solution)/shard_map/ppermute | solution.py:341
  39.5 1.3 %copy-start.2 = (bf16[192,3584]{1,0:T(8,128)(2,1)S(1)}, bf16[192,3584]{1,0:T(8,128)(2,1)}, u32[]{:S(2)}) copy-start(bf16[192,3584]{1,0:T(8,128)(2,1)} %ha_ref.3) | copy-start | bytes 4128772
  40.9 2.4 %copy-start.3 = (s32[192]{0:T(256)S(1)}, s32[192]{0:T(256)}, u32[]{:S(2)}) copy-start(s32[192]{0:T(256)} %param.17) | copy-start | bytes 2308
  47.2 12.6 %all-to-all-start.2 = ((f32[32,8,256]{2,1,0:T(8,128)}), f32[32,8,256]{2,1,0:T(8,128)S(1)}, u32[]{:S(2)}, u32[]{:S(2)}) async-start(f32[32,8,256]{2,1,0:T(8,128)} %second_half.1), calls=%async_computation.2 | async-start | bytes 524288 | tf_op jit(solution)/shard_map/all_to_all | solution.py:366
  87.2 0.6 copy-start.5

commit v9 on v8

--- a/solution.py
+++ b/solution.py
@@ -79,39 +79,34 @@
         low += size
 
 
-def sums_of(acc_ref, model, owner, own):
-    at = 4 * own * (owner // 4) + own * (0, 2, 1, 3)[owner % 4]
-    return acc_ref[model, at:at + own, :]
-
-
-def first_kernel(pos_ref, part_ref, he_ref, ha_ref, out_ref, acc_ref):
-    half_sums(pos_ref[0], part_ref, (he_ref, ha_ref), acc_ref)
-    for model in range(2):
-        for owner in range(out_ref.shape[1]):
-            out_ref[model, owner] = sums_of(acc_ref, model, owner, out_ref.shape[2])
+def first_kernel(pos_ref, part_ref, he_ref, ha_ref, out_ref):
+    half_sums(pos_ref[0], part_ref, (he_ref, ha_ref), out_ref)
 
 
 def second_kernel(
     pos_ref, part_ref, he_ref, ha_ref, first_ref, live_ref, ids_ref, out_ref, acc_ref
 ):
-    width = he_ref.shape[0]
-    own = ids_ref.shape[1]
+    beams, width = ids_ref.shape[0], he_ref.shape[0]
     half_sums(1 - pos_ref[0], part_ref, (he_ref, ha_ref), acc_ref)
+    hits = ids_ref[...] == pos_ref[1] + lax.broadcasted_iota(jnp.int32, (1, width), 1)
     live = live_ref[...] == 1
-    positions = pos_ref[1] + lax.broadcasted_iota(jnp.int32, (1, width), 1)
     half = width // 2
-    for owner in range(out_ref.shape[0]):
-        hits = ids_ref[owner] == positions
-        for model in range(2):
-            logits = first_ref[model, owner] + sums_of(acc_ref, model, owner, own)
-            pick = jnp.sum(jnp.where(hits, logits, 0.0), axis=1, keepdims=True)
-            pick = jnp.broadcast_to(pick, (own, 128 - half))
-            held = jnp.where(live, logits, masked_floor)
-            low = 128 * model
-            for side in range(2):
-                rows = slice(own * side, own * side + own)
-                out_ref[owner, rows, low:low + half] = held[:, half * side:half * side + half]
-                out_ref[owner, rows, low + half:low + 128] = pick
+    tiles = (beams // 8, 8, 128)
+    upper = lax.broadcasted_iota(jnp.int32, tiles, 1) < 4
+    for model in range(2):
+        logits = first_ref[model] + acc_ref[model]
+        pick = jnp.sum(jnp.where(hits, logits, 0.0), axis=1, keepdims=True)
+        pick = jnp.broadcast_to(pick, (beams, 128 - half))
+        held = jnp.where(live, logits, masked_floor)
+        left = jnp.concatenate([held[:, :half], pick], axis=1).reshape(tiles)
+        right = jnp.concatenate([held[:, half:], pick], axis=1).reshape(tiles)
+        low_owner = jnp.where(upper, left, pltpu.roll(right, 4, 1))
+        high_owner = jnp.where(upper, pltpu.roll(left, 4, 1), right)
+        lanes = slice(128 * model, 128 * model + 128)
+        for tile in range(tiles[0]):
+            owner = 4 * (tile // 2) + tile % 2
+            out_ref[owner, :, lanes] = low_owner[tile]
+            out_ref[owner + 2, :, lanes] = high_owner[tile]
 
 
 def lanes_of(columns, shape):
@@ -318,7 +313,7 @@
     quarter = (depth_e + depth_a) // 4
     row, plane = lax.axis_index("rows"), lax.axis_index("vocab")
     position = jnp.stack([row % NC, (row * planes + plane) * width]).astype(jnp.int32)
-    ids = token_ids.reshape(rows, own, 1)
+    ids = token_ids.reshape(rows // 4, 2, 2, own).swapaxes(1, 2).reshape(beams, 1)
     gap = lax.dynamic_slice_in_dim(plaus_level, row * own, own, 0).reshape(own, 1)
 
     norm_inputs = (
@@ -342,13 +337,11 @@
     cost = pl.CostEstimate(
         flops=4 * beams * width * 2 * quarter, bytes_accessed=4 * beams * quarter, transcendentals=0
     )
-    buffers = [pltpu.VMEM((2, beams, width), jnp.float32)]
     first = pl.pallas_call(
         first_kernel,
-        out_shape=jax.ShapeDtypeStruct((2, rows, own, width), jnp.float32),
+        out_shape=jax.ShapeDtypeStruct((2, beams, width), jnp.float32),
         in_specs=[SMEM] + [VMEM] * 3,
         out_specs=VMEM,
-        scratch_shapes=buffers,
         compiler_params=PARAMS,
         cost_estimate=cost,
         name="first_half",
@@ -358,7 +351,7 @@
         out_shape=jax.ShapeDtypeStruct((rows, 2 * own, 256), jnp.float32),
         in_specs=[SMEM] + [VMEM] * 6,
         out_specs=VMEM,
-        scratch_shapes=buffers,
+        scratch_shapes=[pltpu.VMEM((2, beams, width), jnp.float32)],
         compiler_params=PARAMS,
         cost_estimate=cost,
         name="second_half",

time: 88.2 us -> 88 us (level)
  no operation moved by 1% of the time
where the time goes in v9:
time: 88 us; the launch traced here: 87.5 us
  blocking collectives  57.3 us (65%)
  Pallas kernels  11.6 us (13%)
  waiting for transfers between devices  8.79 us (10%)
  starting transfers between devices  5.97 us (7%)
  local copies, waits for them, and re-layouts  2.32 us (3%)
  between operations  1.44 us (2%)
    all_to_all x1, blocking collectives, per_device(): lax.all_to_all(blocks, 'rows', 0, 0, tiled=True).reshape(2 * beams, quarter)  33.7 us
    all_to_all x1, blocking collectives, per_device(): stats = lax.all_to_all(stats, 'vocab', 0, 0, tiled=True)  23.6 us
    all_to_all x1, waiting for transfers between devices, per_device(): table = lax.all_to_all(table, 'rows', 0, 0, tiled=True)  8.79 us
    all_to_all x1, starting transfers between devices, per_device(): table = lax.all_to_all(table, 'rows', 0, 0, tiled=True)  3.67 us
    pallas_call x1, Pallas kernels, per_device(): pl.pallas_call(second_kernel, out_shape=jax.ShapeDtypeStruct((rows, 2 * o...  3.56 us
    pallas_call x1, Pallas kernels, per_device(): pl.pallas_call(norm_kernel, out_shape=jax.ShapeDtypeStruct((rows, 2 * own...  2.61 us
    pallas_call x1, Pallas kernels, per_device(): pl.pallas_call(first_kernel, out_shape=jax.ShapeDtypeStruct((2, beams, wi...  2.39 us
    ppermute x1, starting transfers between devices, per_device(): other_half = lax.ppermute(half, 'rows', [(r, r ^ 1) for r in range(rows)])  2.29 us
  transfers between devices with their start and end apart: 2, of which 1 were waited for; matrix products, arithmetic and copies ran while one was open for 1% of the time, Pallas kernels for 3%

profile of v9, /device:TPU:1, one launch (start us, length us, event | category | flops | bytes accessed | tf_op | source)
XLA Modules:
  0.0 87.5 jit_solution(7744003604270720150)
XLA Ops:
  0.6 0.0 copy-start
  0.6 0.0 copy-start.4
  0.7 2.6 %norms.1 = bf16[32,8,2944]{2,1,0:T(8,128)(2,1)} custom-call(bf16[4,8192]{1,0:T(4,128)(2,1)} %refs_0_.1, bf16[64,128]{1,0:T(8,128)(2,1)} %bitcast.14, bf16[4,3584]{1,0:T(4,128)(2,1)} %refs_2_.1, bf16[28,128]{1,0:T(8,128)(2,1)} %bitcast.15), custom_call_target="tpu_custom_call" | custom-call | tf_op jit(solution)/shard_map/norms/pallas_call | solution.py:322
  3.3 0.0 copy-start.1
  3.3 33.7 %all_to_all.20 = bf16[32,8,2944]{2,1,0:T(8,128)(2,1)} all-to-all(bf16[32,8,2944]{2,1,0:T(8,128)(2,1)} %norms.1), channel_id=1, replica_groups=mesh['rows'=32,'vocab'=16] {'rows'}, dimensions={0} | all-to-all | bytes 3014656 | tf_op jit(solution)/shard_map/all_to_all | solution.py:335
  37.0 2.3 %collective-permute-start = (bf16[256,2944]{1,0:T(8,128)(2,1)}, bf16[256,2944]{1,0:T(8,128)(2,1)}, u32[]{:S(2)}, u32[]{:S(2)}) collective-permute-start(bf16[256,2944]{1,0:T(8,128)(2,1)} %bitcast.4.part_ref), channel_id=1, source_target_pairs={{0,16},{16,0},{32,48},{48,32},{64,80},{80,64},{96,112},{112,96},{1... | collective-permute-start | bytes 4521992 | tf_op jit(solution)/shard_map/ppermute | solution.py:336
  39.3 0.0 copy-done.4
  39.3 0.1 reshape.38
  39.4 0.1 reshape.43.ids_ref
  39.5 0.1 pad_add_fusion.pos_ref
  39.6 0.0 copy-done.1
  39.6 0.0 copy-start.2
  39.6 1.3 %copy-done.2 = bf16[192,3584]{1,0:T(8,128)(2,1)S(1)} copy-done((bf16[192,3584]{1,0:T(8,128)(2,1)S(1)}, bf16[192,3584]{1,0:T(8,128)(2,1)}, u32[]{:S(2)}) %copy-start.2) | copy-done | bytes 1376280
  41.0 0.0 copy-start.3
  41.0 2.4 %first_half.1.first_ref = f32[2,128,192]{2,1,0:T(8,128)S(1)} custom-call(s32[2]{0:T(128)S(1)} %pad_add_fusion.pos_ref, bf16[256,2944]{1,0:T(8,128)(2,1)} %bitcast.4.part_ref, bf16[192,8192]{1,0:T(8,128)(2,1)S(1)} %copy-done.1, bf16[192,3584]{1,0:T(8,128)(2,1)S(1)} %copy-done.2), custom_call_target="tpu_custom_call" | custom-call | flops 578813952 | bytes 1507328 | tf_op jit(solution)/shard_map/first_half/pallas_call | solution.py:340
  43.4 0.0 collective-permute-done.part_ref
  43.4 0.0 copy-done.3
  43.4 3.6 %second_half.1 = f32[32,8,256]{2,1,0:T(8,128)} custom-call(s32[2]{0:T(128)S(1)} %pad_add_fusion.pos_ref, bf16[256,2944]{1,0:T(8,128)(2,1)} %collective-permute-done.part_ref, bf16[192,8192]{1,0:T(8,128)(2,1)S(1)} %copy-done.1, bf16[192,3584]{1,0:T(8,128)(2,1)S(1)} %copy-done.2, f32[2,128,192]{2,1,0:T(8,128)S(1)} %first_half.1.first_ref, ...), custom_call_target="tpu_custom_call" | custom-call | flops 578813952 | bytes 1507328 | tf_op jit(solution)/shard_map/second_half/pallas_call | solution.py:349
  46.9 3.7 %all-to-all-start.2 = ((f32[32,8,256]{2,1,0:T(8,128)}), f32[32,8,256]{2,1,0:T(8,128)S(1)}, u32[]{:S(2)}, u32[]{:S(2)}) async-start(f32[32,8,256]{2,1,0:T(8,128)} %second_half.1), calls=%async_computation.2 | async-start | bytes 524288 | tf_op jit(solution)/shard_map/all_to_all | solution.py:359
  50.6 0.0 copy-done
  50.6 0.1 dynamic-slice_bitcast_fusion
  50.7 0.1 copy.19.gap_ref
  50.8 8.8 %all-to-all-done.2.table_ref = f32[32,8,256]{2,1,0:T(8,128)S(1)} async-done(((f32[32,8,256]{2,1,0:T(8,128)}), f32[32,8,256]{2,1,0:T(8,128)S(1)}, u32[]{:S(2)}, u32[]{:S(2)}) %all-to-all-start.2) | async-done | bytes 262176 | tf_op jit(solution)/shard_map/all_to_all | solution.py:359
  59.6 2.0 %stats.1 = f32[16,4,128]{2,1,0:T(4,128)S(1)} custom-call(f32[32,8,256]{2,1,0:T(8,128)S(1)} %all-to-all-done.2.table_ref, s32[4,1]{1,0:T(4,128)S(1)} %copy.19.gap_ref), custom_call_target="tpu_custom_call" | custom-call | tf_op jit(solution)/shard_map/stats/pallas_call | solution.py:363
  61.6 23.6 %all_to_all.21.stats_ref = f32[16,4,128]{2,1,0:T(4,128)S(1)} all-to-all(f32[16,4,128]{2,1,0:T(4,128)S(1)} %stats.1), channel_id=1, replica_groups=mesh['rows'=32,'vocab'=16] {'vocab'}, dimensions={0} | all-to-all | bytes 65536 | tf_op jit(solution)/shard_map/all_to_all | solution.py:371
  85.2 1.0 %finish.1 = (f32[4,4]{1,0:T(4,128)S(1)}, f32[2,4]{1,0:T(2,128)}, f32[1,4]{1,0:T(1,128)}, s32[1]{0:T(128)}) custom-call(f32[16,4,128]{2,1,0:T(4,128)S(1)} %all_to_all.21.stats_ref, s32[4,1]{1,0:T(4,128)S(1)} %copy.19.gap_ref), custom_call_target="tpu_custom_call" | custom-call | tf_op jit(solution)/shard_map/finish/pallas_call | solution.py:372
  86.9 0.0 copy-start.5
  86.9 0.6 copy-done.5
  (2 shorter events, 0.0 us)
Async XLA Ops:
  0.6 50.0 %copy-start = (s32[128]{0:T(128)S(1)}, s32[128]{0:T(128)}, u32[]{:S(2)}) copy-start(s32[128]{0:T(128)} %param.19) | copy-start | bytes 1540
  0.6 38.6 %copy-start.4 = (s32[128]{0:T(128)S(1)}, s32[128]{0:T(128)}, u32[]{:S(2)}) copy-start(s32[128]{0:T(128)} %param.18) | copy-start | bytes 1540
  3.3 36.3 %copy-start.1 = (bf16[192,8192]{1,0:T(8,128)(2,1)S(1)}, bf16[192,8192]{1,0:T(8,128)(2,1)}, u32[]{:S(2)}) copy-start(bf16[192,8192]{1,0:T(8,128)(2,1)} %he_ref.3) | copy-start | bytes 9437188
  37.0 6.4 %collective-permute-start = (bf16[256,2944]{1,0:T(8,128)(2,1)}, bf16[256,2944]{1,0:T(8,128)(2,1)}, u32[]{:S(2)}, u32[]{:S(2)}) collective-permute-start(bf16[256,2944]{1,0:T(8,128)(2,1)} %bitcast.4.part_ref), channel_id=1, source_target_pairs={{0,16},{16,0},{32,48},{48,32},{64,80},{80,64},{96,112},{112,96},{1... | collective-permute-start | bytes 4521992 | tf_op jit(solution)/shard_map/ppermute | solution.py:336
  39.6 1.3 %copy-start.2 = (bf16[192,3584]{1,0:T(8,128)(2,1)S(1)}, bf16[192,3584]{1,0:T(8,128)(2,1)}, u32[]{:S(2)}) copy-start(bf16[192,3584]{1,0:T(8,128)(2,1)} %ha_ref.3) | copy-start | bytes 4128772
  41.0 2.4 %copy-start.3 = (s32[192]{0:T(256)S(1)}, s32[192]{0:T(256)}, u32[]{:S(2)}) copy-start(s32[192]{0:T(256)} %param.17) | copy-start | bytes 2308
  46.9 12.7 %all-to-all-start.2 = ((f32[32,8,256]{2,1,0:T(8,128)}), f32[32,8,256]{2,1,0:T(8,128)S(1)}, u32[]{:S(2)}, u32[]{:S(2)}) async-start(f32[32,8,256]{2,1,0:T(8,128)} %second_half.1), calls=%async_computation.2 | async-start | bytes 524288 | tf_op jit(solution)/shard_map/all_to_all | solution.py:359
  86.9 0.6 copy-start.5

commit v10 on v9

--- a/solution.py
+++ b/solution.py
@@ -145,7 +145,15 @@
     ]
 
 
-def stats_kernel(width, table_ref, gap_ref, out_ref):
+def gap_column(pos_ref, level_ref, shape):
+    row = lax.broadcasted_iota(jnp.int32, shape, 0)
+    levels = jnp.zeros(shape, jnp.int32)
+    for i in range(shape[0]):
+        levels = jnp.where(row == i, level_ref[pos_ref[2] + i], levels)
+    return levels.astype(jnp.float32) * 0.1
+
+
+def stats_kernel(width, pos_ref, level_ref, table_ref, out_ref):
     sources, own = table_ref.shape[0], table_ref.shape[1] // 2
     shape = (2 * own, 128)
     real = lax.broadcasted_iota(jnp.int32, shape, 1) < width // 2
@@ -161,7 +169,7 @@
         pick = lane_at(functools.reduce(jnp.add, parts), width // 2)
         columns.append((peak, total[:own] + total[own:], pick[:own]))
     (pe, te, ce), (pa, ta, ca) = columns
-    least = pe - gap_ref[...].astype(jnp.float32) * 0.1
+    least = pe - gap_column(pos_ref, level_ref, pe.shape)
     least = jnp.concatenate([least, least])
     floor = jnp.full(shape, masked_floor, jnp.float32)
     near, rest = [(floor,) * 2] * TOP, [(floor,) * 3] * TOP
@@ -230,7 +238,7 @@
     return jnp.sum(jnp.where(here, column, 0.0), axis=0, keepdims=True)
 
 
-def totals_of(stats_ref, gap_ref, copies=1):
+def totals_of(stats_ref, pos_ref, level_ref, copies=1):
     stats = stats_ref[...]
     peak_e, peak_a, sum_e, sum_a = [lane_at(stats, i) for i in range(4)]
 
@@ -240,7 +248,7 @@
 
     peak_e, log_total_e = total_of(peak_e, sum_e)
     peak_a, log_total_a = total_of(peak_a, sum_a)
-    cut = peak_e - log_total_e - gap_ref[...].astype(jnp.float32) * 0.1
+    cut = peak_e - log_total_e - gap_column(pos_ref, level_ref, peak_e.shape)
     shift_e, shift_a, cuts = [
         jnp.concatenate([x] * copies) if copies > 1 else x for x in (log_total_e, log_total_a, cut)
     ]
@@ -253,8 +261,8 @@
     return [peak_e - log_total_e, peak_a - log_total_a], score
 
 
-def finish_kernel(stats_ref, gap_ref, top_ref, peaks_ref, chosen_ref, lacking_ref):
-    peaks, score = totals_of(stats_ref, gap_ref)
+def finish_kernel(pos_ref, level_ref, stats_ref, top_ref, peaks_ref, chosen_ref, lacking_ref):
+    peaks, score = totals_of(stats_ref, pos_ref, level_ref)
     stats = stats_ref[...]
     for i, peak in enumerate(peaks):
         peaks_ref[i:i + 1, :] = row_from(peak)
@@ -272,8 +280,8 @@
     lacking_ref[0] = jnp.where(jnp.max(lacking) > 0.0, 1, 0).astype(jnp.int32)
 
 
-def score_kernel(width, table_ref, stats_ref, gap_ref, best_ref):
-    _, score = totals_of(stats_ref, gap_ref, 2)
+def score_kernel(width, pos_ref, level_ref, table_ref, stats_ref, best_ref):
+    _, score = totals_of(stats_ref, pos_ref, level_ref, 2)
     own = table_ref.shape[1] // 2
     real = lax.broadcasted_iota(jnp.int32, (2 * own, 128), 1) < width // 2
     parts = []
@@ -312,9 +320,8 @@
     beams = own * rows
     quarter = (depth_e + depth_a) // 4
     row, plane = lax.axis_index("rows"), lax.axis_index("vocab")
-    position = jnp.stack([row % NC, (row * planes + plane) * width]).astype(jnp.int32)
+    position = jnp.stack([row % NC, (row * planes + plane) * width, row * own]).astype(jnp.int32)
     ids = token_ids.reshape(rows // 4, 2, 2, own).swapaxes(1, 2).reshape(beams, 1)
-    gap = lax.dynamic_slice_in_dim(plaus_level, row * own, own, 0).reshape(own, 1)
 
     norm_inputs = (
         expert_hidden, expert_gain.reshape(-1, 128), amateur_hidden, amateur_gain.reshape(-1, 128)
@@ -363,11 +370,11 @@
     stats = pl.pallas_call(
         functools.partial(stats_kernel, width),
         out_shape=small,
-        in_specs=[VMEM] * 2,
+        in_specs=[SMEM, SMEM, VMEM],
         out_specs=VMEM,
         compiler_params=PARAMS,
         name="stats",
-    )(table, gap)
+    )(position, plaus_level, table)
     stats = lax.all_to_all(stats, "vocab", 0, 0, tiled=True)
     top, peaks, chosen, lacking = pl.pallas_call(
         finish_kernel,
@@ -377,21 +384,21 @@
             jax.ShapeDtypeStruct((1, own), jnp.float32),
             jax.ShapeDtypeStruct((1,), jnp.int32),
         ),
-        in_specs=[VMEM] * 2,
+        in_specs=[SMEM, SMEM, VMEM],
         out_specs=(VMEM, VMEM, VMEM, SMEM),
         compiler_params=PARAMS,
         name="finish",
-    )(stats, gap)
-
-    def with_every_entry(table, stats, gap, _):
+    )(position, plaus_level, stats)
+
+    def with_every_entry(position, level, table, stats, _):
         best = pl.pallas_call(
             functools.partial(score_kernel, width),
             out_shape=small,
-            in_specs=[VMEM] * 3,
+            in_specs=[SMEM, SMEM, VMEM, VMEM],
             out_specs=VMEM,
             compiler_params=PARAMS,
             name="scores",
-        )(table, stats, gap)
+        )(position, level, table, stats)
         best = lax.all_to_all(best, "vocab", 0, 0, tiled=True)
         return pl.pallas_call(
             merge_kernel,
@@ -402,7 +409,8 @@
             name="merge",
         )(best)
 
-    top = lax.cond(lacking[0] > 0, with_every_entry, lambda *args: args[-1], table, stats, gap, top)
+    operands = (position, plaus_level, table, stats, top)
+    top = lax.cond(lacking[0] > 0, with_every_entry, lambda *args: args[-1], *operands)
     return top, peaks.T, chosen.reshape(own)
 
 

time: 88 us -> 87.9 us (level)
  blocking collectives: 57.3 us -> 69.7 us
  waiting for transfers between devices: 8.79 us -> 0.01 us
  starting transfers between devices: 5.97 us -> 2.29 us
    all_to_all x0 -> x1, blocking collectives: none -> 12.4 us  [per_device(): table = lax.all_to_all(table, 'rows', 0, 0, tiled=True)]
    all_to_all x1 -> x0, waiting for transfers between devices: 8.79 us -> none  [per_device(): table = lax.all_to_all(table, 'rows', 0, 0, tiled=True)]
    all_to_all x1 -> x0, starting transfers between devices: 3.67 us -> none  [per_device(): table = lax.all_to_all(table, 'rows', 0, 0, tiled=True)]
  transfers between devices with their start and end apart: 2 -> 1, of which waited for: 1 -> 0; matrix products, arithmetic and copies ran while one was open for 1% -> 0% of each run, Pallas kernels for 3% -> 3%
where the time goes in v10:
time: 87.9 us; the launch traced here: 87.5 us
  blocking collectives  69.7 us (79%)
  Pallas kernels  11.9 us (14%)
  starting transfers between devices  2.29 us (3%)
  local copies, waits for them, and re-layouts  2.15 us (2%)
  between operations  1.43 us (2%)
    all_to_all x1, blocking collectives, per_device(): lax.all_to_all(blocks, 'rows', 0, 0, tiled=True).reshape(2 * beams, quarter)  33.7 us
    all_to_all x1, blocking collectives, per_device(): stats = lax.all_to_all(stats, 'vocab', 0, 0, tiled=True)  23.6 us
    all_to_all x1, blocking collectives, per_device(): table = lax.all_to_all(table, 'rows', 0, 0, tiled=True)  12.4 us
    pallas_call x1, Pallas kernels, per_device(): pl.pallas_call(second_kernel, out_shape=jax.ShapeDtypeStruct((rows, 2 * o...  2.78 us
    pallas_call x1, Pallas kernels, per_device(): pl.pallas_call(norm_kernel, out_shape=jax.ShapeDtypeStruct((rows, 2 * own...  2.62 us
    pallas_call x1, Pallas kernels, per_device(): pl.pallas_call(functools.partial(stats_kernel, width), out_shape=small, i...  2.55 us
    pallas_call x1, Pallas kernels, per_device(): pl.pallas_call(first_kernel, out_shape=jax.ShapeDtypeStruct((2, beams, wi...  2.37 us
    ppermute x1, starting transfers between devices, per_device(): other_half = lax.ppermute(half, 'rows', [(r, r ^ 1) for r in range(rows)])  2.29 us
  transfers between devices with their start and end apart: 1, of which 0 were waited for; matrix products, arithmetic and copies ran while one was open for 0% of the time, Pallas kernels for 3%

profile of v10, /device:TPU:1, one launch (start us, length us, event | category | flops | bytes accessed | tf_op | source)
XLA Modules:
  0.0 87.5 jit_solution(14435633258633711276)
XLA Ops:
  0.6 0.0 copy-start.4
  0.6 2.6 %norms.1 = bf16[32,8,2944]{2,1,0:T(8,128)(2,1)} custom-call(bf16[4,8192]{1,0:T(4,128)(2,1)} %refs_0_.1, bf16[64,128]{1,0:T(8,128)(2,1)} %bitcast.13, bf16[4,3584]{1,0:T(4,128)(2,1)} %refs_2_.1, bf16[28,128]{1,0:T(8,128)(2,1)} %bitcast.14), custom_call_target="tpu_custom_call" | custom-call | tf_op jit(solution)/shard_map/norms/pallas_call | solution.py:329
  3.3 0.0 copy-start
  3.3 33.7 %all_to_all.20 = bf16[32,8,2944]{2,1,0:T(8,128)(2,1)} all-to-all(bf16[32,8,2944]{2,1,0:T(8,128)(2,1)} %norms.1), channel_id=1, replica_groups=mesh['rows'=32,'vocab'=16] {'rows'}, dimensions={0} | all-to-all | bytes 3014656 | tf_op jit(solution)/shard_map/all_to_all | solution.py:342
  37.0 2.3 %collective-permute-start = (bf16[256,2944]{1,0:T(8,128)(2,1)}, bf16[256,2944]{1,0:T(8,128)(2,1)}, u32[]{:S(2)}, u32[]{:S(2)}) collective-permute-start(bf16[256,2944]{1,0:T(8,128)(2,1)} %bitcast.5.part_ref), channel_id=1, source_target_pairs={{0,16},{16,0},{32,48},{48,32},{64,80},{80,64},{96,112},{112,96},{1... | collective-permute-start | bytes 4521992 | tf_op jit(solution)/shard_map/ppermute | solution.py:343
  39.3 0.0 copy-done.4
  39.3 0.1 reshape.35
  39.4 0.1 reshape.39.ids_ref
  39.5 0.1 pad_add_fusion.pos_ref
  39.6 0.0 copy-done
  39.6 0.0 copy-start.1
  39.6 1.3 %copy-done.1 = bf16[192,3584]{1,0:T(8,128)(2,1)S(1)} copy-done((bf16[192,3584]{1,0:T(8,128)(2,1)S(1)}, bf16[192,3584]{1,0:T(8,128)(2,1)}, u32[]{:S(2)}) %copy-start.1) | copy-done | bytes 1376280
  41.0 0.0 copy-start.2
  41.0 2.4 %first_half.1.first_ref = f32[2,128,192]{2,1,0:T(8,128)S(1)} custom-call(s32[3]{0:T(128)S(1)} %pad_add_fusion.pos_ref, bf16[256,2944]{1,0:T(8,128)(2,1)} %bitcast.5.part_ref, bf16[192,8192]{1,0:T(8,128)(2,1)S(1)} %copy-done, bf16[192,3584]{1,0:T(8,128)(2,1)S(1)} %copy-done.1), custom_call_target="tpu_custom_call" | custom-call | flops 578813952 | bytes 1507328 | tf_op jit(solution)/shard_map/first_half/pallas_call | solution.py:347
  43.3 0.0 collective-permute-done.part_ref
  43.4 0.0 copy-done.2
  43.4 0.0 copy-start.3
  43.4 2.8 %second_half.1 = f32[32,8,256]{2,1,0:T(8,128)S(1)} custom-call(s32[3]{0:T(128)S(1)} %pad_add_fusion.pos_ref, bf16[256,2944]{1,0:T(8,128)(2,1)} %collective-permute-done.part_ref, bf16[192,8192]{1,0:T(8,128)(2,1)S(1)} %copy-done, bf16[192,3584]{1,0:T(8,128)(2,1)S(1)} %copy-done.1, f32[2,128,192]{2,1,0:T(8,128)S(1)} %first_half.1.first_ref, ...), custom_call_target="tpu_custom_call" | custom-call | flops 578813952 | bytes 1507328 | tf_op jit(solution)/shard_map/second_half/pallas_call | solution.py:356
  46.2 12.4 %all_to_all.21.table_ref = f32[32,8,256]{2,1,0:T(8,128)S(1)} all-to-all(f32[32,8,256]{2,1,0:T(8,128)S(1)} %second_half.1), channel_id=1, replica_groups=mesh['rows'=32,'vocab'=16] {'rows'}, dimensions={0} | all-to-all | bytes 524288 | tf_op jit(solution)/shard_map/all_to_all | solution.py:366
  58.6 0.0 copy-done.3
  58.6 2.5 %stats.1 = f32[16,4,128]{2,1,0:T(4,128)S(1)} custom-call(s32[3]{0:T(128)S(1)} %pad_add_fusion.pos_ref, s32[128]{0:T(128)S(1)} %copy-done.3, f32[32,8,256]{2,1,0:T(8,128)S(1)} %all_to_all.21.table_ref), custom_call_target="tpu_custom_call" | custom-call | tf_op jit(solution)/shard_map/stats/pallas_call | solution.py:370
  61.1 23.6 %all_to_all.22.stats_ref = f32[16,4,128]{2,1,0:T(4,128)S(1)} all-to-all(f32[16,4,128]{2,1,0:T(4,128)S(1)} %stats.1), channel_id=1, replica_groups=mesh['rows'=32,'vocab'=16] {'vocab'}, dimensions={0} | all-to-all | bytes 65536 | tf_op jit(solution)/shard_map/all_to_all | solution.py:378
  84.7 1.5 %finish.1 = (f32[4,4]{1,0:T(4,128)S(1)}, f32[2,4]{1,0:T(2,128)}, f32[1,4]{1,0:T(1,128)}, s32[1]{0:T(128)}) custom-call(s32[3]{0:T(128)S(1)} %pad_add_fusion.pos_ref, s32[128]{0:T(128)S(1)} %copy-done.3, f32[16,4,128]{2,1,0:T(4,128)S(1)} %all_to_all.22.stats_ref), custom_call_target="tpu_custom_call" | custom-call | tf_op jit(solution)/shard_map/finish/pallas_call | solution.py:379
  86.9 0.0 copy-start.5
  86.9 0.6 copy-done.5
  (2 shorter events, 0.0 us)
Async XLA Ops:
  0.6 38.7 %copy-start.4 = (s32[128]{0:T(128)S(1)}, s32[128]{0:T(128)}, u32[]{:S(2)}) copy-start(s32[128]{0:T(128)} %param.18) | copy-start | bytes 1540
  3.3 36.3 %copy-start = (bf16[192,8192]{1,0:T(8,128)(2,1)S(1)}, bf16[192,8192]{1,0:T(8,128)(2,1)}, u32[]{:S(2)}) copy-start(bf16[192,8192]{1,0:T(8,128)(2,1)} %he_ref.3) | copy-start | bytes 9437188
  37.0 6.4 %collective-permute-start = (bf16[256,2944]{1,0:T(8,128)(2,1)}, bf16[256,2944]{1,0:T(8,128)(2,1)}, u32[]{:S(2)}, u32[]{:S(2)}) collective-permute-start(bf16[256,2944]{1,0:T(8,128)(2,1)} %bitcast.5.part_ref), channel_id=1, source_target_pairs={{0,16},{16,0},{32,48},{48,32},{64,80},{80,64},{96,112},{112,96},{1... | collective-permute-start | bytes 4521992 | tf_op jit(solution)/shard_map/ppermute | solution.py:343
  39.6 1.3 %copy-start.1 = (bf16[192,3584]{1,0:T(8,128)(2,1)S(1)}, bf16[192,3584]{1,0:T(8,128)(2,1)}, u32[]{:S(2)}) copy-start(bf16[192,3584]{1,0:T(8,128)(2,1)} %ha_ref.3) | copy-start | bytes 4128772
  41.0 2.4 %copy-start.2 = (s32[192]{0:T(256)S(1)}, s32[192]{0:T(256)}, u32[]{:S(2)}) copy-start(s32[192]{0:T(256)} %param.17) | copy-start | bytes 2308
  43.4 15.2 %copy-start.3 = (s32[128]{0:T(128)S(1)}, s32[128]{0:T(128)}, u32[]{:S(2)}) copy-start(s32[128]{0:T(128)} %level_ref.3) | copy-start | bytes 1540
  86.9 0.6 copy-start.5

commit v11 on v9

--- a/solution.py
+++ b/solution.py
@@ -84,7 +84,7 @@
 
 
 def second_kernel(
-    pos_ref, part_ref, he_ref, ha_ref, first_ref, live_ref, ids_ref, out_ref, acc_ref
+    pos_ref, part_ref, he_ref, ha_ref, first_ref, live_ref, ids_ref, _, out_ref, acc_ref
 ):
     beams, width = ids_ref.shape[0], he_ref.shape[0]
     half_sums(1 - pos_ref[0], part_ref, (he_ref, ha_ref), acc_ref)
@@ -349,13 +349,13 @@
     table = pl.pallas_call(
         second_kernel,
         out_shape=jax.ShapeDtypeStruct((rows, 2 * own, 256), jnp.float32),
-        in_specs=[SMEM] + [VMEM] * 6,
+        in_specs=[SMEM] + [VMEM] * 7,
         out_specs=VMEM,
         scratch_shapes=[pltpu.VMEM((2, beams, width), jnp.float32)],
         compiler_params=PARAMS,
         cost_estimate=cost,
         name="second_half",
-    )(position, other_half, expert_head, amateur_head, first, live_mask.reshape(1, -1), ids)
+    )(position, other_half, expert_head, amateur_head, first, live_mask.reshape(1, -1), ids, gap)
     table = lax.all_to_all(table, "rows", 0, 0, tiled=True)
 
     small = jax.ShapeDtypeStruct((planes, own, 128), jnp.float32)

time: 88 us -> 87.1 us (0.990)
  blocking collectives: 57.3 us -> 69.7 us
  waiting for transfers between devices: 8.79 us -> 0.01 us
  starting transfers between devices: 5.97 us -> 2.29 us
    all_to_all x0 -> x1, blocking collectives: none -> 12.4 us  [per_device(): table = lax.all_to_all(table, 'rows', 0, 0, tiled=True)]
    all_to_all x1 -> x0, waiting for transfers between devices: 8.79 us -> none  [per_device(): table = lax.all_to_all(table, 'rows', 0, 0, tiled=True)]
    all_to_all x1 -> x0, starting transfers between devices: 3.67 us -> none  [per_device(): table = lax.all_to_all(table, 'rows', 0, 0, tiled=True)]
  transfers between devices with their start and end apart: 2 -> 1, of which waited for: 1 -> 0; matrix products, arithmetic and copies ran while one was open for 1% -> 1% of each run, Pallas kernels for 3% -> 3%
where the time goes in v11:
time: 87.1 us; the launch traced here: 86.7 us
  blocking collectives  69.7 us (80%)
  Pallas kernels  10.9 us (13%)
  local copies, waits for them, and re-layouts  2.32 us (3%)
  starting transfers between devices  2.29 us (3%)
  between operations  1.43 us (2%)
    all_to_all x1, blocking collectives, per_device(): lax.all_to_all(blocks, 'rows', 0, 0, tiled=True).reshape(2 * beams, quarter)  33.7 us
    all_to_all x1, blocking collectives, per_device(): stats = lax.all_to_all(stats, 'vocab', 0, 0, tiled=True)  23.7 us
    all_to_all x1, blocking collectives, per_device(): table = lax.all_to_all(table, 'rows', 0, 0, tiled=True)  12.4 us
    pallas_call x1, Pallas kernels, per_device(): pl.pallas_call(second_kernel, out_shape=jax.ShapeDtypeStruct((rows, 2 * o...  2.82 us
    pallas_call x1, Pallas kernels, per_device(): pl.pallas_call(norm_kernel, out_shape=jax.ShapeDtypeStruct((rows, 2 * own...  2.63 us
    pallas_call x1, Pallas kernels, per_device(): pl.pallas_call(first_kernel, out_shape=jax.ShapeDtypeStruct((2, beams, wi...  2.4 us
    ppermute x1, starting transfers between devices, per_device(): other_half = lax.ppermute(half, 'rows', [(r, r ^ 1) for r in range(rows)])  2.29 us
    pallas_call x1, Pallas kernels, per_device(): pl.pallas_call(functools.partial(stats_kernel, width), out_shape=small, i...  2.02 us
  transfers between devices with their start and end apart: 1, of which 0 were waited for; matrix products, arithmetic and copies ran while one was open for 1% of the time, Pallas kernels for 3%

profile of v11, /device:TPU:1, one launch (start us, length us, event | category | flops | bytes accessed | tf_op | source)
XLA Modules:
  0.0 86.7 jit_solution(9680097498834295123)
XLA Ops:
  0.6 0.0 copy-start
  0.6 0.0 copy-start.4
  0.7 2.6 %norms.1 = bf16[32,8,2944]{2,1,0:T(8,128)(2,1)} custom-call(bf16[4,8192]{1,0:T(4,128)(2,1)} %refs_0_.1, bf16[64,128]{1,0:T(8,128)(2,1)} %bitcast.14, bf16[4,3584]{1,0:T(4,128)(2,1)} %refs_2_.1, bf16[28,128]{1,0:T(8,128)(2,1)} %bitcast.15), custom_call_target="tpu_custom_call" | custom-call | tf_op jit(solution)/shard_map/norms/pallas_call | solution.py:322
  3.3 0.0 copy-start.1
  3.3 33.7 %all_to_all.20 = bf16[32,8,2944]{2,1,0:T(8,128)(2,1)} all-to-all(bf16[32,8,2944]{2,1,0:T(8,128)(2,1)} %norms.1), channel_id=1, replica_groups=mesh['rows'=32,'vocab'=16] {'rows'}, dimensions={0} | all-to-all | bytes 3014656 | tf_op jit(solution)/shard_map/all_to_all | solution.py:335
  37.0 2.3 %collective-permute-start = (bf16[256,2944]{1,0:T(8,128)(2,1)}, bf16[256,2944]{1,0:T(8,128)(2,1)}, u32[]{:S(2)}, u32[]{:S(2)}) collective-permute-start(bf16[256,2944]{1,0:T(8,128)(2,1)} %bitcast.4.part_ref), channel_id=1, source_target_pairs={{0,16},{16,0},{32,48},{48,32},{64,80},{80,64},{96,112},{112,96},{1... | collective-permute-start | bytes 4521992 | tf_op jit(solution)/shard_map/ppermute | solution.py:336
  39.3 0.0 copy-done.4
  39.3 0.1 reshape.38
  39.5 0.1 reshape.43.ids_ref
  39.6 0.0 copy-done
  39.6 0.1 dynamic-slice_bitcast_fusion
  39.6 0.1 copy.20._.gap_ref
  39.7 0.1 pad_add_fusion.pos_ref
  39.8 0.0 copy-done.1
  39.8 0.0 copy-start.2
  39.8 1.3 %copy-done.2 = bf16[192,3584]{1,0:T(8,128)(2,1)S(1)} copy-done((bf16[192,3584]{1,0:T(8,128)(2,1)S(1)}, bf16[192,3584]{1,0:T(8,128)(2,1)}, u32[]{:S(2)}) %copy-start.2) | copy-done | bytes 1376280
  41.2 0.0 copy-start.3
  41.2 2.4 %first_half.1.first_ref = f32[2,128,192]{2,1,0:T(8,128)S(1)} custom-call(s32[2]{0:T(128)S(1)} %pad_add_fusion.pos_ref, bf16[256,2944]{1,0:T(8,128)(2,1)} %bitcast.4.part_ref, bf16[192,8192]{1,0:T(8,128)(2,1)S(1)} %copy-done.1, bf16[192,3584]{1,0:T(8,128)(2,1)S(1)} %copy-done.2), custom_call_target="tpu_custom_call" | custom-call | flops 578813952 | bytes 1507328 | tf_op jit(solution)/shard_map/first_half/pallas_call | solution.py:340
  43.6 0.0 collective-permute-done.part_ref
  43.6 0.0 copy-done.3
  43.6 2.8 %second_half.1 = f32[32,8,256]{2,1,0:T(8,128)S(1)} custom-call(s32[2]{0:T(128)S(1)} %pad_add_fusion.pos_ref, bf16[256,2944]{1,0:T(8,128)(2,1)} %collective-permute-done.part_ref, bf16[192,8192]{1,0:T(8,128)(2,1)S(1)} %copy-done.1, bf16[192,3584]{1,0:T(8,128)(2,1)S(1)} %copy-done.2, f32[2,128,192]{2,1,0:T(8,128)S(1)} %first_half.1.first_ref, ...), custom_call_target="tpu_custom_call" | custom-call | flops 578813952 | bytes 1507328 | tf_op jit(solution)/shard_map/second_half/pallas_call | solution.py:349
  46.4 12.4 %all_to_all.21.table_ref = f32[32,8,256]{2,1,0:T(8,128)S(1)} all-to-all(f32[32,8,256]{2,1,0:T(8,128)S(1)} %second_half.1), channel_id=1, replica_groups=mesh['rows'=32,'vocab'=16] {'rows'}, dimensions={0} | all-to-all | bytes 524288 | tf_op jit(solution)/shard_map/all_to_all | solution.py:359
  58.8 2.0 %stats.1 = f32[16,4,128]{2,1,0:T(4,128)S(1)} custom-call(f32[32,8,256]{2,1,0:T(8,128)S(1)} %all_to_all.21.table_ref, s32[4,1]{1,0:T(4,128)S(1)} %copy.20._.gap_ref), custom_call_target="tpu_custom_call" | custom-call | tf_op jit(solution)/shard_map/stats/pallas_call | solution.py:363
  60.8 23.7 %all_to_all.22.stats_ref = f32[16,4,128]{2,1,0:T(4,128)S(1)} all-to-all(f32[16,4,128]{2,1,0:T(4,128)S(1)} %stats.1), channel_id=1, replica_groups=mesh['rows'=32,'vocab'=16] {'vocab'}, dimensions={0} | all-to-all | bytes 65536 | tf_op jit(solution)/shard_map/all_to_all | solution.py:371
  84.4 1.0 %finish.1 = (f32[4,4]{1,0:T(4,128)S(1)}, f32[2,4]{1,0:T(2,128)}, f32[1,4]{1,0:T(1,128)}, s32[1]{0:T(128)}) custom-call(f32[16,4,128]{2,1,0:T(4,128)S(1)} %all_to_all.22.stats_ref, s32[4,1]{1,0:T(4,128)S(1)} %copy.20._.gap_ref), custom_call_target="tpu_custom_call" | custom-call | tf_op jit(solution)/shard_map/finish/pallas_call | solution.py:372
  86.1 0.0 copy-start.5
  86.2 0.6 copy-done.5
  (2 shorter events, 0.0 us)
Async XLA Ops:
  0.6 38.9 %copy-start = (s32[128]{0:T(128)S(1)}, s32[128]{0:T(128)}, u32[]{:S(2)}) copy-start(s32[128]{0:T(128)} %param.19) | copy-start | bytes 1540
  0.6 38.7 %copy-start.4 = (s32[128]{0:T(128)S(1)}, s32[128]{0:T(128)}, u32[]{:S(2)}) copy-start(s32[128]{0:T(128)} %param.18) | copy-start | bytes 1540
  3.3 36.5 %copy-start.1 = (bf16[192,8192]{1,0:T(8,128)(2,1)S(1)}, bf16[192,8192]{1,0:T(8,128)(2,1)}, u32[]{:S(2)}) copy-start(bf16[192,8192]{1,0:T(8,128)(2,1)} %he_ref.3) | copy-start | bytes 9437188
  37.0 6.6 %collective-permute-start = (bf16[256,2944]{1,0:T(8,128)(2,1)}, bf16[256,2944]{1,0:T(8,128)(2,1)}, u32[]{:S(2)}, u32[]{:S(2)}) collective-permute-start(bf16[256,2944]{1,0:T(8,128)(2,1)} %bitcast.4.part_ref), channel_id=1, source_target_pairs={{0,16},{16,0},{32,48},{48,32},{64,80},{80,64},{96,112},{112,96},{1... | collective-permute-start | bytes 4521992 | tf_op jit(solution)/shard_map/ppermute | solution.py:336
  39.8 1.3 %copy-start.2 = (bf16[192,3584]{1,0:T(8,128)(2,1)S(1)}, bf16[192,3584]{1,0:T(8,128)(2,1)}, u32[]{:S(2)}) copy-start(bf16[192,3584]{1,0:T(8,128)(2,1)} %ha_ref.3) | copy-start | bytes 4128772
  41.2 2.4 %copy-start.3 = (s32[192]{0:T(256)S(1)}, s32[192]{0:T(256)}, u32[]{:S(2)}) copy-start(s32[192]{0:T(256)} %param.17) | copy-start | bytes 2308
  86.1 0.6 copy-start.5

commit v12 on v11

--- a/solution.py
+++ b/solution.py
@@ -332,6 +332,9 @@
         compiler_params=WIDE_PARAMS,
         name="norms",
     )(*norm_inputs)
+    blocks, expert_head, amateur_head = lax.optimization_barrier(
+        (blocks, expert_head, amateur_head)
+    )
     half = lax.all_to_all(blocks, "rows", 0, 0, tiled=True).reshape(2 * beams, quarter)
     other_half = lax.ppermute(half, "rows", [(r, r ^ 1) for r in range(rows)])
     cost = pl.CostEstimate(

time: 87.1 us -> 87.1 us (level)
  no operation moved by 1% of the time
where the time goes in v12:
time: 87.1 us; the launch traced here: 86.7 us
  blocking collectives  69.7 us (80%)
  Pallas kernels  10.9 us (13%)
  local copies, waits for them, and re-layouts  2.32 us (3%)
  starting transfers between devices  2.29 us (3%)
  between operations  1.43 us (2%)
    all_to_all x1, blocking collectives, per_device(): lax.all_to_all(blocks, 'rows', 0, 0, tiled=True).reshape(2 * beams, quarter)  33.7 us
    all_to_all x1, blocking collectives, per_device(): stats = lax.all_to_all(stats, 'vocab', 0, 0, tiled=True)  23.7 us
    all_to_all x1, blocking collectives, per_device(): table = lax.all_to_all(table, 'rows', 0, 0, tiled=True)  12.4 us
    pallas_call x1, Pallas kernels, per_device(): pl.pallas_call(second_kernel, out_shape=jax.ShapeDtypeStruct((rows, 2 * o...  2.82 us
    pallas_call x1, Pallas kernels, per_device(): pl.pallas_call(norm_kernel, out_shape=jax.ShapeDtypeStruct((rows, 2 * own...  2.63 us
    pallas_call x1, Pallas kernels, per_device(): pl.pallas_call(first_kernel, out_shape=jax.ShapeDtypeStruct((2, beams, wi...  2.4 us
    ppermute x1, starting transfers between devices, per_device(): other_half = lax.ppermute(half, 'rows', [(r, r ^ 1) for r in range(rows)])  2.29 us
    pallas_call x1, Pallas kernels, per_device(): pl.pallas_call(functools.partial(stats_kernel, width), out_shape=small, i...  2.02 us
  transfers between devices with their start and end apart: 1, of which 0 were waited for; matrix products, arithmetic and copies ran while one was open for 1% of the time, Pallas kernels for 3%

profile of v12, /device:TPU:1, one launch (start us, length us, event | category | flops | bytes accessed | tf_op | source)
XLA Modules:
  0.0 86.7 jit_solution(9680097498834295123)
XLA Ops:
  0.6 0.0 copy-start
  0.6 0.0 copy-start.4
  0.7 2.6 %norms.1 = bf16[32,8,2944]{2,1,0:T(8,128)(2,1)} custom-call(bf16[4,8192]{1,0:T(4,128)(2,1)} %refs_0_.1, bf16[64,128]{1,0:T(8,128)(2,1)} %bitcast.14, bf16[4,3584]{1,0:T(4,128)(2,1)} %refs_2_.1, bf16[28,128]{1,0:T(8,128)(2,1)} %bitcast.15), custom_call_target="tpu_custom_call" | custom-call | tf_op jit(solution)/shard_map/norms/pallas_call | solution.py:322
  3.3 0.0 copy-start.1
  3.3 33.7 %all_to_all.20 = bf16[32,8,2944]{2,1,0:T(8,128)(2,1)} all-to-all(bf16[32,8,2944]{2,1,0:T(8,128)(2,1)} %norms.1), channel_id=1, replica_groups=mesh['rows'=32,'vocab'=16] {'rows'}, dimensions={0} | all-to-all | bytes 3014656 | tf_op jit(solution)/shard_map/all_to_all | solution.py:338
  37.0 2.3 %collective-permute-start = (bf16[256,2944]{1,0:T(8,128)(2,1)}, bf16[256,2944]{1,0:T(8,128)(2,1)}, u32[]{:S(2)}, u32[]{:S(2)}) collective-permute-start(bf16[256,2944]{1,0:T(8,128)(2,1)} %bitcast.4.part_ref), channel_id=1, source_target_pairs={{0,16},{16,0},{32,48},{48,32},{64,80},{80,64},{96,112},{112,96},{1... | collective-permute-start | bytes 4521992 | tf_op jit(solution)/shard_map/ppermute | solution.py:339
  39.3 0.0 copy-done.4
  39.3 0.1 reshape.38
  39.5 0.1 reshape.43.ids_ref
  39.6 0.0 copy-done
  39.6 0.1 dynamic-slice_bitcast_fusion
  39.6 0.1 copy.20._.gap_ref
  39.7 0.1 pad_add_fusion.pos_ref
  39.8 0.0 copy-done.1
  39.8 0.0 copy-start.2
  39.8 1.3 %copy-done.2 = bf16[192,3584]{1,0:T(8,128)(2,1)S(1)} copy-done((bf16[192,3584]{1,0:T(8,128)(2,1)S(1)}, bf16[192,3584]{1,0:T(8,128)(2,1)}, u32[]{:S(2)}) %copy-start.2) | copy-done | bytes 1376280
  41.2 0.0 copy-start.3
  41.2 2.4 %first_half.1.first_ref = f32[2,128,192]{2,1,0:T(8,128)S(1)} custom-call(s32[2]{0:T(128)S(1)} %pad_add_fusion.pos_ref, bf16[256,2944]{1,0:T(8,128)(2,1)} %bitcast.4.part_ref, bf16[192,8192]{1,0:T(8,128)(2,1)S(1)} %copy-done.1, bf16[192,3584]{1,0:T(8,128)(2,1)S(1)} %copy-done.2), custom_call_target="tpu_custom_call" | custom-call | flops 578813952 | bytes 1507328 | tf_op jit(solution)/shard_map/first_half/pallas_call | solution.py:343
  43.6 0.0 collective-permute-done.part_ref
  43.6 0.0 copy-done.3
  43.6 2.8 %second_half.1 = f32[32,8,256]{2,1,0:T(8,128)S(1)} custom-call(s32[2]{0:T(128)S(1)} %pad_add_fusion.pos_ref, bf16[256,2944]{1,0:T(8,128)(2,1)} %collective-permute-done.part_ref, bf16[192,8192]{1,0:T(8,128)(2,1)S(1)} %copy-done.1, bf16[192,3584]{1,0:T(8,128)(2,1)S(1)} %copy-done.2, f32[2,128,192]{2,1,0:T(8,128)S(1)} %first_half.1.first_ref, ...), custom_call_target="tpu_custom_call" | custom-call | flops 578813952 | bytes 1507328 | tf_op jit(solution)/shard_map/second_half/pallas_call | solution.py:352
  46.4 12.4 %all_to_all.21.table_ref = f32[32,8,256]{2,1,0:T(8,128)S(1)} all-to-all(f32[32,8,256]{2,1,0:T(8,128)S(1)} %second_half.1), channel_id=1, replica_groups=mesh['rows'=32,'vocab'=16] {'rows'}, dimensions={0} | all-to-all | bytes 524288 | tf_op jit(solution)/shard_map/all_to_all | solution.py:362
  58.8 2.0 %stats.1 = f32[16,4,128]{2,1,0:T(4,128)S(1)} custom-call(f32[32,8,256]{2,1,0:T(8,128)S(1)} %all_to_all.21.table_ref, s32[4,1]{1,0:T(4,128)S(1)} %copy.20._.gap_ref), custom_call_target="tpu_custom_call" | custom-call | tf_op jit(solution)/shard_map/stats/pallas_call | solution.py:366
  60.8 23.7 %all_to_all.22.stats_ref = f32[16,4,128]{2,1,0:T(4,128)S(1)} all-to-all(f32[16,4,128]{2,1,0:T(4,128)S(1)} %stats.1), channel_id=1, replica_groups=mesh['rows'=32,'vocab'=16] {'vocab'}, dimensions={0} | all-to-all | bytes 65536 | tf_op jit(solution)/shard_map/all_to_all | solution.py:374
  84.4 1.0 %finish.1 = (f32[4,4]{1,0:T(4,128)S(1)}, f32[2,4]{1,0:T(2,128)}, f32[1,4]{1,0:T(1,128)}, s32[1]{0:T(128)}) custom-call(f32[16,4,128]{2,1,0:T(4,128)S(1)} %all_to_all.22.stats_ref, s32[4,1]{1,0:T(4,128)S(1)} %copy.20._.gap_ref), custom_call_target="tpu_custom_call" | custom-call | tf_op jit(solution)/shard_map/finish/pallas_call | solution.py:375
  86.1 0.0 copy-start.5
  86.2 0.6 copy-done.5
  (2 shorter events, 0.0 us)
Async XLA Ops:
  0.6 38.9 %copy-start = (s32[128]{0:T(128)S(1)}, s32[128]{0:T(128)}, u32[]{:S(2)}) copy-start(s32[128]{0:T(128)} %param.19) | copy-start | bytes 1540
  0.6 38.7 %copy-start.4 = (s32[128]{0:T(128)S(1)}, s32[128]{0:T(128)}, u32[]{:S(2)}) copy-start(s32[128]{0:T(128)} %param.18) | copy-start | bytes 1540
  3.3 36.5 %copy-start.1 = (bf16[192,8192]{1,0:T(8,128)(2,1)S(1)}, bf16[192,8192]{1,0:T(8,128)(2,1)}, u32[]{:S(2)}) copy-start(bf16[192,8192]{1,0:T(8,128)(2,1)} %he_ref.1) | copy-start | bytes 9437188
  37.0 6.6 %collective-permute-start = (bf16[256,2944]{1,0:T(8,128)(2,1)}, bf16[256,2944]{1,0:T(8,128)(2,1)}, u32[]{:S(2)}, u32[]{:S(2)}) collective-permute-start(bf16[256,2944]{1,0:T(8,128)(2,1)} %bitcast.4.part_ref), channel_id=1, source_target_pairs={{0,16},{16,0},{32,48},{48,32},{64,80},{80,64},{96,112},{112,96},{1... | collective-permute-start | bytes 4521992 | tf_op jit(solution)/shard_map/ppermute | solution.py:339
  39.8 1.3 %copy-start.2 = (bf16[192,3584]{1,0:T(8,128)(2,1)S(1)}, bf16[192,3584]{1,0:T(8,128)(2,1)}, u32[]{:S(2)}) copy-start(bf16[192,3584]{1,0:T(8,128)(2,1)} %ha_ref.1) | copy-start | bytes 4128772
  41.2 2.4 %copy-start.3 = (s32[192]{0:T(256)S(1)}, s32[192]{0:T(256)}, u32[]{:S(2)}) copy-start(s32[192]{0:T(256)} %param.17) | copy-start | bytes 2308
  86.1 0.6 copy-start.5

commit v13 on v12

--- a/solution.py
+++ b/solution.py
@@ -371,7 +371,8 @@
         compiler_params=PARAMS,
         name="stats",
     )(table, gap)
-    stats = lax.all_to_all(stats, "vocab", 0, 0, tiled=True)
+    around = [[(planes // 2 + z) % planes for z in range(planes)]]
+    stats = lax.all_to_all(stats, "vocab", 0, 0, tiled=True, axis_index_groups=around)
     top, peaks, chosen, lacking = pl.pallas_call(
         finish_kernel,
         out_shape=(

time: 87.1 us -> 102 us (1.17)
  the two profiles are of different devices: /device:TPU:1 before, /device:TPU:28 now
where the time goes in v13:
time: 102 us
  blocking collectives  83.6 us (82%)
  Pallas kernels  11.9 us (12%)
  local copies, waits for them, and re-layouts  2.42 us (2%)
  starting transfers between devices  2.16 us (2%)
  between operations  1.42 us (1%)
    all_to_all x1, blocking collectives, per_device(): lax.all_to_all(blocks, 'rows', 0, 0, tiled=True).reshape(2 * beams, quarter)  28.5 us
    all_to_all x1, blocking collectives, with_every_entry(): best = lax.all_to_all(best, 'vocab', 0, 0, tiled=True)  23.4 us
    all_to_all x1, blocking collectives, per_device(): lax.all_to_all(stats, 'vocab', 0, 0, tiled=True, axis_index_groups=around)  19.1 us
    all_to_all x1, blocking collectives, per_device(): table = lax.all_to_all(table, 'rows', 0, 0, tiled=True)  12.5 us
    pallas_call x1, Pallas kernels, per_device(): pl.pallas_call(second_kernel, out_shape=jax.ShapeDtypeStruct((rows, 2 * o...  2.83 us
    pallas_call x1, Pallas kernels, per_device(): pl.pallas_call(norm_kernel, out_shape=jax.ShapeDtypeStruct((rows, 2 * own...  2.63 us
    pallas_call x1, Pallas kernels, per_device(): pl.pallas_call(first_kernel, out_shape=jax.ShapeDtypeStruct((2, beams, wi...  2.4 us
    ppermute x1, starting transfers between devices, per_device(): other_half = lax.ppermute(half, 'rows', [(r, r ^ 1) for r in range(rows)])  2.16 us
  transfers between devices with their start and end apart: 1, of which 0 were waited for; matrix products, arithmetic and copies ran while one was open for 0% of the time, Pallas kernels for 2%

profile of v13, /device:TPU:28, one launch (start us, length us, event | category | flops | bytes accessed | tf_op | source)
XLA Modules:
  0.0 101.6 jit_solution(2889852897893848437)
XLA Ops:
  0.6 0.0 copy-start
  0.6 0.0 copy-start.4
  0.7 2.6 %norms.1 = bf16[32,8,2944]{2,1,0:T(8,128)(2,1)} custom-call(bf16[4,8192]{1,0:T(4,128)(2,1)} %refs_0_.1, bf16[64,128]{1,0:T(8,128)(2,1)} %bitcast.14, bf16[4,3584]{1,0:T(4,128)(2,1)} %refs_2_.1, bf16[28,128]{1,0:T(8,128)(2,1)} %bitcast.15), custom_call_target="tpu_custom_call" | custom-call | tf_op jit(solution)/shard_map/norms/pallas_call | solution.py:322
  3.3 0.0 copy-start.1
  3.3 28.5 %all_to_all.20 = bf16[32,8,2944]{2,1,0:T(8,128)(2,1)} all-to-all(bf16[32,8,2944]{2,1,0:T(8,128)(2,1)} %norms.1), channel_id=1, replica_groups=mesh['rows'=32,'vocab'=16] {'rows'}, dimensions={0} | all-to-all | bytes 3014656 | tf_op jit(solution)/shard_map/all_to_all | solution.py:338
  31.8 2.2 %collective-permute-start = (bf16[256,2944]{1,0:T(8,128)(2,1)}, bf16[256,2944]{1,0:T(8,128)(2,1)}, u32[]{:S(2)}, u32[]{:S(2)}) collective-permute-start(bf16[256,2944]{1,0:T(8,128)(2,1)} %bitcast.4.part_ref), channel_id=1, source_target_pairs={{0,16},{16,0},{32,48},{48,32},{64,80},{80,64},{96,112},{112,96},{1... | collective-permute-start | bytes 4521992 | tf_op jit(solution)/shard_map/ppermute | solution.py:339
  34.0 0.0 copy-done.4
  34.0 0.1 reshape.38
  34.2 0.1 reshape.43.ids_ref
  34.3 0.0 copy-done
  34.3 0.1 dynamic-slice_bitcast_fusion
  34.4 0.1 copy.20._.gap_ref
  34.4 0.1 pad_add_fusion.pos_ref
  34.5 0.0 copy-done.1
  34.5 0.0 copy-start.2
  34.5 1.3 %copy-done.2 = bf16[192,3584]{1,0:T(8,128)(2,1)S(1)} copy-done((bf16[192,3584]{1,0:T(8,128)(2,1)S(1)}, bf16[192,3584]{1,0:T(8,128)(2,1)}, u32[]{:S(2)}) %copy-start.2) | copy-done | bytes 1376280
  35.9 0.0 copy-start.3
  35.9 2.4 %first_half.1.first_ref = f32[2,128,192]{2,1,0:T(8,128)S(1)} custom-call(s32[2]{0:T(128)S(1)} %pad_add_fusion.pos_ref, bf16[256,2944]{1,0:T(8,128)(2,1)} %bitcast.4.part_ref, bf16[192,8192]{1,0:T(8,128)(2,1)S(1)} %copy-done.1, bf16[192,3584]{1,0:T(8,128)(2,1)S(1)} %copy-done.2), custom_call_target="tpu_custom_call" | custom-call | flops 578813952 | bytes 1507328 | tf_op jit(solution)/shard_map/first_half/pallas_call | solution.py:343
  38.3 0.0 collective-permute-done.part_ref
  38.3 0.0 copy-done.3
  38.3 2.8 %second_half.1 = f32[32,8,256]{2,1,0:T(8,128)S(1)} custom-call(s32[2]{0:T(128)S(1)} %pad_add_fusion.pos_ref, bf16[256,2944]{1,0:T(8,128)(2,1)} %collective-permute-done.part_ref, bf16[192,8192]{1,0:T(8,128)(2,1)S(1)} %copy-done.1, bf16[192,3584]{1,0:T(8,128)(2,1)S(1)} %copy-done.2, f32[2,128,192]{2,1,0:T(8,128)S(1)} %first_half.1.first_ref, ...), custom_call_target="tpu_custom_call" | custom-call | flops 578813952 | bytes 1507328 | tf_op jit(solution)/shard_map/second_half/pallas_call | solution.py:352
  41.1 12.5 %all_to_all.21.table_ref = f32[32,8,256]{2,1,0:T(8,128)S(1)} all-to-all(f32[32,8,256]{2,1,0:T(8,128)S(1)} %second_half.1), channel_id=1, replica_groups=mesh['rows'=32,'vocab'=16] {'rows'}, dimensions={0} | all-to-all | bytes 524288 | tf_op jit(solution)/shard_map/all_to_all | solution.py:362
  53.7 2.0 %stats.1 = f32[16,4,128]{2,1,0:T(4,128)S(1)} custom-call(f32[32,8,256]{2,1,0:T(8,128)S(1)} %all_to_all.21.table_ref, s32[4,1]{1,0:T(4,128)S(1)} %copy.20._.gap_ref), custom_call_target="tpu_custom_call" | custom-call | tf_op jit(solution)/shard_map/stats/pallas_call | solution.py:366
  55.7 19.1 %all_to_all.22.stats_ref = f32[16,4,128]{2,1,0:T(4,128)S(1)} all-to-all(f32[16,4,128]{2,1,0:T(4,128)S(1)} %stats.1), channel_id=1, replica_groups={{8,9,10,11,12,13,14,15,0,1,2,3,4,5,6,7},{24,25,26,27,28,29,30,31,16,17,..., dimensions={0} | all-to-all | bytes 65536 | tf_op jit(solution)/shard_map/all_to_all | solution.py:375
  74.8 1.0 %finish.1 = (f32[4,4]{1,0:T(4,128)S(1)}, f32[2,4]{1,0:T(2,128)}, f32[1,4]{1,0:T(1,128)}, s32[1]{0:T(128)}) custom-call(f32[16,4,128]{2,1,0:T(4,128)S(1)} %all_to_all.22.stats_ref, s32[4,1]{1,0:T(4,128)S(1)} %copy.20._.gap_ref), custom_call_target="tpu_custom_call" | custom-call | tf_op jit(solution)/shard_map/finish/pallas_call | solution.py:376
  76.5 24.5 %conditional.1 = (f32[4,4]{1,0:T(4,128)S(1)}) conditional(s32[]{:T(128)} %bitcast.8, f32[4,4]{1,0:T(4,128)S(1)} %get-tuple-element.27, (f32[32,8,256]{2,1,0:T(8,128)S(1)}, f32[16,4,128]{2,1,0:T(4,128)S(1)}, s32[4,1]{0,1:T(1,128)S(1)}) %tuple.16), branch_computations={%region_0.1_spmd, %region_1.2_spmd} | conditional | bytes 65704 | solution.py:409
  76.5 0.1 copy.23.gap_ref
  76.6 0.6 scores.1
  77.3 23.4 %all_to_all.19.parts_ref = f32[16,4,128]{2,1,0:T(4,128)S(1)} all-to-all(f32[16,4,128]{2,1,0:T(4,128)S(1)} %scores.1), channel_id=1, replica_groups=mesh['rows'=32,'vocab'=16] {'vocab'}, dimensions={0} | all-to-all | bytes 65536 | tf_op jit(solution)/shard_map/cond/branch_1_fun/all_to_all | solution.py:399
  100.7 0.3 merge.1
  101.0 0.0 copy-start.5
  101.0 0.6 copy-done.5
  (2 shorter events, 0.0 us)
Async XLA Ops:
  0.6 33.6 %copy-start = (s32[128]{0:T(128)S(1)}, s32[128]{0:T(128)}, u32[]{:S(2)}) copy-start(s32[128]{0:T(128)} %param.19) | copy-start | bytes 1540
  0.6 33.4 %copy-start.4 = (s32[128]{0:T(128)S(1)}, s32[128]{0:T(128)}, u32[]{:S(2)}) copy-start(s32[128]{0:T(128)} %param.18) | copy-start | bytes 1540
  3.3 31.2 %copy-start.1 = (bf16[192,8192]{1,0:T(8,128)(2,1)S(1)}, bf16[192,8192]{1,0:T(8,128)(2,1)}, u32[]{:S(2)}) copy-start(bf16[192,8192]{1,0:T(8,128)(2,1)} %he_ref.1) | copy-start | bytes 9437188
  31.8 6.4 %collective-permute-start = (bf16[256,2944]{1,0:T(8,128)(2,1)}, bf16[256,2944]{1,0:T(8,128)(2,1)}, u32[]{:S(2)}, u32[]{:S(2)}) collective-permute-start(bf16[256,2944]{1,0:T(8,128)(2,1)} %bitcast.4.part_ref), channel_id=1, source_target_pairs={{0,16},{16,0},{32,48},{48,32},{64,80},{80,64},{96,112},{112,96},{1... | collective-permute-start | bytes 4521992 | tf_op jit(solution)/shard_map/ppermute | solution.py:339
  34.5 1.3 %copy-start.2 = (bf16[192,3584]{1,0:T(8,128)(2,1)S(1)}, bf16[192,3584]{1,0:T(8,128)(2,1)}, u32[]{:S(2)}) copy-start(bf16[192,3584]{1,0:T(8,128)(2,1)} %ha_ref.1) | copy-start | bytes 4128772
  35.9 2.4 %copy-start.3 = (s32[192]{0:T(256)S(1)}, s32[192]{0:T(256)}, u32[]{:S(2)}) copy-start(s32[192]{0:T(256)} %param.17) | copy-start | bytes 2308
  101.0 0.6 copy-start.5

commit v14 on v13

--- a/solution.py
+++ b/solution.py
@@ -313,7 +313,10 @@
     quarter = (depth_e + depth_a) // 4
     row, plane = lax.axis_index("rows"), lax.axis_index("vocab")
     position = jnp.stack([row % NC, (row * planes + plane) * width]).astype(jnp.int32)
-    ids = token_ids.reshape(rows // 4, 2, 2, own).swapaxes(1, 2).reshape(beams, 1)
+    middle = rows // 2 + rows // 8
+    order = [(middle + r) % rows for r in range(rows)]
+    ids = jnp.roll(token_ids, -middle * own)
+    ids = ids.reshape(rows // 4, 2, 2, own).swapaxes(1, 2).reshape(beams, 1)
     gap = lax.dynamic_slice_in_dim(plaus_level, row * own, own, 0).reshape(own, 1)
 
     norm_inputs = (
@@ -335,7 +338,7 @@
     blocks, expert_head, amateur_head = lax.optimization_barrier(
         (blocks, expert_head, amateur_head)
     )
-    half = lax.all_to_all(blocks, "rows", 0, 0, tiled=True).reshape(2 * beams, quarter)
+    half = lax.all_to_all(blocks, "rows", 0, 0, tiled=True, axis_index_groups=[order]).reshape(2 * beams, quarter)
     other_half = lax.ppermute(half, "rows", [(r, r ^ 1) for r in range(rows)])
     cost = pl.CostEstimate(
         flops=4 * beams * width * 2 * quarter, bytes_accessed=4 * beams * quarter, transcendentals=0
@@ -359,7 +362,7 @@
         cost_estimate=cost,
         name="second_half",
     )(position, other_half, expert_head, amateur_head, first, live_mask.reshape(1, -1), ids, gap)
-    table = lax.all_to_all(table, "rows", 0, 0, tiled=True)
+    table = lax.all_to_all(table, "rows", 0, 0, tiled=True, axis_index_groups=[order])
 
     small = jax.ShapeDtypeStruct((planes, own, 128), jnp.float32)
     best_shape = jax.ShapeDtypeStruct((own, TOP), jnp.float32)

time: 102 us -> 79.1 us (0.78)
  the two profiles are of different devices: /device:TPU:28 before, /device:TPU:1 now
where the time goes in v14:
time: 79.1 us; the launch traced here: 78.7 us
  blocking collectives  61.5 us (78%)
  Pallas kernels  10.9 us (14%)
  local copies, waits for them, and re-layouts  2.39 us (3%)
  starting transfers between devices  2.3 us (3%)
  between operations  1.43 us (2%)
    all_to_all x1, blocking collectives, per_device(): lax.all_to_all(blocks, 'rows', 0, 0, tiled=True, axis_index_groups=[order])  31.8 us
    all_to_all x1, blocking collectives, per_device(): lax.all_to_all(stats, 'vocab', 0, 0, tiled=True, axis_index_groups=around)  17.7 us
    all_to_all x1, blocking collectives, per_device(): lax.all_to_all(table, 'rows', 0, 0, tiled=True, axis_index_groups=[order])  12 us
    pallas_call x1, Pallas kernels, per_device(): pl.pallas_call(second_kernel, out_shape=jax.ShapeDtypeStruct((rows, 2 * o...  2.83 us
    pallas_call x1, Pallas kernels, per_device(): pl.pallas_call(norm_kernel, out_shape=jax.ShapeDtypeStruct((rows, 2 * own...  2.63 us
    pallas_call x1, Pallas kernels, per_device(): pl.pallas_call(first_kernel, out_shape=jax.ShapeDtypeStruct((2, beams, wi...  2.4 us
    ppermute x1, starting transfers between devices, per_device(): other_half = lax.ppermute(half, 'rows', [(r, r ^ 1) for r in range(rows)])  2.3 us
    pallas_call x1, Pallas kernels, per_device(): pl.pallas_call(functools.partial(stats_kernel, width), out_shape=small, i...  2.02 us
  transfers between devices with their start and end apart: 1, of which 0 were waited for; matrix products, arithmetic and copies ran while one was open for 1% of the time, Pallas kernels for 3%

profile of v14, /device:TPU:1, one launch (start us, length us, event | category | flops | bytes accessed | tf_op | source)
XLA Modules:
  0.0 78.7 jit_solution(7758149356950923483)
XLA Ops:
  0.6 0.0 copy-start
  0.6 0.0 copy-start.5
  0.7 2.6 %norms.1 = bf16[32,8,2944]{2,1,0:T(8,128)(2,1)} custom-call(bf16[4,8192]{1,0:T(4,128)(2,1)} %refs_0_.1, bf16[64,128]{1,0:T(8,128)(2,1)} %bitcast.15, bf16[4,3584]{1,0:T(4,128)(2,1)} %refs_2_.1, bf16[28,128]{1,0:T(8,128)(2,1)} %bitcast.16), custom_call_target="tpu_custom_call" | custom-call | tf_op jit(solution)/shard_map/norms/pallas_call | solution.py:325
  3.3 0.0 copy-start.1
  3.3 31.8 %all_to_all.20 = bf16[32,8,2944]{2,1,0:T(8,128)(2,1)} all-to-all(bf16[32,8,2944]{2,1,0:T(8,128)(2,1)} %norms.1), channel_id=1, replica_groups={{320,336,352,368,384,400,416,432,448,464,480,496,0,16,32,48,64,80,96,11..., dimensions={0} | all-to-all | bytes 3014656 | tf_op jit(solution)/shard_map/all_to_all | solution.py:341
  35.1 2.3 %collective-permute-start = (bf16[256,2944]{1,0:T(8,128)(2,1)}, bf16[256,2944]{1,0:T(8,128)(2,1)}, u32[]{:S(2)}, u32[]{:S(2)}) collective-permute-start(bf16[256,2944]{1,0:T(8,128)(2,1)} %bitcast.4.part_ref), channel_id=1, source_target_pairs={{0,16},{16,0},{32,48},{48,32},{64,80},{80,64},{96,112},{112,96},{1... | collective-permute-start | bytes 4521992 | tf_op jit(solution)/shard_map/ppermute | solution.py:342
  37.4 0.0 copy-done.5
  37.4 0.1 slice.8
  37.5 0.1 pad_add_fusion.1
  37.6 0.1 reshape.38
  37.7 0.1 reshape.43.ids_ref
  37.8 0.0 copy-done
  37.8 0.1 dynamic-slice_bitcast_fusion
  37.9 0.1 copy.20._.gap_ref
  38.0 0.1 pad_add_fusion.pos_ref
  38.1 0.0 copy-done.1
  38.1 0.0 copy-start.2
  38.1 1.3 %copy-done.2 = bf16[192,3584]{1,0:T(8,128)(2,1)S(1)} copy-done((bf16[192,3584]{1,0:T(8,128)(2,1)S(1)}, bf16[192,3584]{1,0:T(8,128)(2,1)}, u32[]{:S(2)}) %copy-start.2) | copy-done | bytes 1376280
  39.4 0.0 copy-start.3
  39.4 2.4 %first_half.1.first_ref = f32[2,128,192]{2,1,0:T(8,128)S(1)} custom-call(s32[2]{0:T(128)S(1)} %pad_add_fusion.pos_ref, bf16[256,2944]{1,0:T(8,128)(2,1)} %bitcast.4.part_ref, bf16[192,8192]{1,0:T(8,128)(2,1)S(1)} %copy-done.1, bf16[192,3584]{1,0:T(8,128)(2,1)S(1)} %copy-done.2), custom_call_target="tpu_custom_call" | custom-call | flops 578813952 | bytes 1507328 | tf_op jit(solution)/shard_map/first_half/pallas_call | solution.py:346
  41.8 0.0 collective-permute-done.part_ref
  41.8 0.0 copy-done.3
  41.8 2.8 %second_half.1 = f32[32,8,256]{2,1,0:T(8,128)S(1)} custom-call(s32[2]{0:T(128)S(1)} %pad_add_fusion.pos_ref, bf16[256,2944]{1,0:T(8,128)(2,1)} %collective-permute-done.part_ref, bf16[192,8192]{1,0:T(8,128)(2,1)S(1)} %copy-done.1, bf16[192,3584]{1,0:T(8,128)(2,1)S(1)} %copy-done.2, f32[2,128,192]{2,1,0:T(8,128)S(1)} %first_half.1.first_ref, ...), custom_call_target="tpu_custom_call" | custom-call | flops 578813952 | bytes 1507328 | tf_op jit(solution)/shard_map/second_half/pallas_call | solution.py:355
  44.7 12.0 %all_to_all.21.table_ref = f32[32,8,256]{2,1,0:T(8,128)S(1)} all-to-all(f32[32,8,256]{2,1,0:T(8,128)S(1)} %second_half.1), channel_id=1, replica_groups={{320,336,352,368,384,400,416,432,448,464,480,496,0,16,32,48,64,80,96,11..., dimensions={0} | all-to-all | bytes 524288 | tf_op jit(solution)/shard_map/all_to_all | solution.py:365
  56.6 2.0 %stats.1 = f32[16,4,128]{2,1,0:T(4,128)S(1)} custom-call(f32[32,8,256]{2,1,0:T(8,128)S(1)} %all_to_all.21.table_ref, s32[4,1]{1,0:T(4,128)S(1)} %copy.20._.gap_ref), custom_call_target="tpu_custom_call" | custom-call | tf_op jit(solution)/shard_map/stats/pallas_call | solution.py:369
  58.7 17.7 %all_to_all.22.stats_ref = f32[16,4,128]{2,1,0:T(4,128)S(1)} all-to-all(f32[16,4,128]{2,1,0:T(4,128)S(1)} %stats.1), channel_id=1, replica_groups={{8,9,10,11,12,13,14,15,0,1,2,3,4,5,6,7},{24,25,26,27,28,29,30,31,16,17,..., dimensions={0} | all-to-all | bytes 65536 | tf_op jit(solution)/shard_map/all_to_all | solution.py:378
  76.4 1.0 %finish.1 = (f32[4,4]{1,0:T(4,128)S(1)}, f32[2,4]{1,0:T(2,128)}, f32[1,4]{1,0:T(1,128)}, s32[1]{0:T(128)}) custom-call(f32[16,4,128]{2,1,0:T(4,128)S(1)} %all_to_all.22.stats_ref, s32[4,1]{1,0:T(4,128)S(1)} %copy.20._.gap_ref), custom_call_target="tpu_custom_call" | custom-call | tf_op jit(solution)/shard_map/finish/pallas_call | solution.py:379
  78.1 0.0 copy-start.4
  78.1 0.6 copy-done.4
  (2 shorter events, 0.0 us)
Async XLA Ops:
  0.6 37.2 %copy-start = (s32[128]{0:T(128)S(1)}, s32[128]{0:T(128)}, u32[]{:S(2)}) copy-start(s32[128]{0:T(128)} %param.19) | copy-start | bytes 1540
  0.6 36.8 %copy-start.5 = (s32[128]{0:T(128)S(1)}, s32[128]{0:T(128)}, u32[]{:S(2)}) copy-start(s32[128]{0:T(128)} %param.18) | copy-start | bytes 1540
  3.3 34.8 %copy-start.1 = (bf16[192,8192]{1,0:T(8,128)(2,1)S(1)}, bf16[192,8192]{1,0:T(8,128)(2,1)}, u32[]{:S(2)}) copy-start(bf16[192,8192]{1,0:T(8,128)(2,1)} %he_ref.1) | copy-start | bytes 9437188
  35.1 6.7 %collective-permute-start = (bf16[256,2944]{1,0:T(8,128)(2,1)}, bf16[256,2944]{1,0:T(8,128)(2,1)}, u32[]{:S(2)}, u32[]{:S(2)}) collective-permute-start(bf16[256,2944]{1,0:T(8,128)(2,1)} %bitcast.4.part_ref), channel_id=1, source_target_pairs={{0,16},{16,0},{32,48},{48,32},{64,80},{80,64},{96,112},{112,96},{1... | collective-permute-start | bytes 4521992 | tf_op jit(solution)/shard_map/ppermute | solution.py:342
  38.1 1.3 %copy-start.2 = (bf16[192,3584]{1,0:T(8,128)(2,1)S(1)}, bf16[192,3584]{1,0:T(8,128)(2,1)}, u32[]{:S(2)}) copy-start(bf16[192,3584]{1,0:T(8,128)(2,1)} %ha_ref.1) | copy-start | bytes 4128772
  39.4 2.4 %copy-start.3 = (s32[192]{0:T(256)S(1)}, s32[192]{0:T(256)}, u32[]{:S(2)}) copy-start(s32[192]{0:T(256)} %param.17) | copy-start | bytes 2308
  78.1 0.6 copy-start.4

commit v15 on v14

--- a/solution.py
+++ b/solution.py
@@ -64,37 +64,38 @@
     return [x.reshape(part.shape[0] // 2, part.shape[1]) for x in apart]
 
 
-def half_sums(core, part_ref, head_refs, acc_ref):
-    low = 0
-    for model, head in enumerate(head_refs):
-        size = head.shape[1] // 4
-        total = None
-        for p, rows in enumerate(quarters_apart(part_ref[:, low:low + size])):
-            columns = pl.ds(pl.multiple_of((2 * core + p) * size, 128), size)
-            product = lax.dot_general(
-                rows, head[:, columns], (((1,), (1,)), ((), ())), preferred_element_type=jnp.float32
-            )
-            total = product if total is None else total + product
-        acc_ref[model] = total
-        low += size
-
-
-def first_kernel(pos_ref, part_ref, he_ref, ha_ref, out_ref):
-    half_sums(pos_ref[0], part_ref, (he_ref, ha_ref), out_ref)
+def half_sums(core, part, head, low):
+    size = head.shape[1] // 4
+    total = None
+    for p, rows in enumerate(quarters_apart(part[:, low:low + size])):
+        columns = pl.ds(pl.multiple_of((2 * core + p) * size, 128), size)
+        product = lax.dot_general(
+            rows, head[:, columns], (((1,), (1,)), ((), ())), preferred_element_type=jnp.float32
+        )
+        total = product if total is None else total + product
+    return total
+
+
+def first_kernel(pos_ref, part_ref, he_ref, out_ref, rest_ref):
+    out_ref[...] = half_sums(pos_ref[0], part_ref, he_ref, 0)
+    rest_ref[...] = part_ref[:, he_ref.shape[1] // 4:]
 
 
 def second_kernel(
-    pos_ref, part_ref, he_ref, ha_ref, first_ref, live_ref, ids_ref, _, out_ref, acc_ref
+    pos_ref, part_ref, he_ref, ha_ref, first_ref, rest_ref, live_ref, ids_ref, _, out_ref, acc_ref
 ):
     beams, width = ids_ref.shape[0], he_ref.shape[0]
-    half_sums(1 - pos_ref[0], part_ref, (he_ref, ha_ref), acc_ref)
+    mine, other = pos_ref[0], 1 - pos_ref[0]
+    acc_ref[0] = first_ref[...] + half_sums(other, part_ref, he_ref, 0)
+    acc_ref[1] = half_sums(mine, rest_ref, ha_ref, 0)
+    acc_ref[1] += half_sums(other, part_ref, ha_ref, he_ref.shape[1] // 4)
     hits = ids_ref[...] == pos_ref[1] + lax.broadcasted_iota(jnp.int32, (1, width), 1)
     live = live_ref[...] == 1
     half = width // 2
     tiles = (beams // 8, 8, 128)
     upper = lax.broadcasted_iota(jnp.int32, tiles, 1) < 4
     for model in range(2):
-        logits = first_ref[model] + acc_ref[model]
+        logits = acc_ref[model]
         pick = jnp.sum(jnp.where(hits, logits, 0.0), axis=1, keepdims=True)
         pick = jnp.broadcast_to(pick, (beams, 128 - half))
         held = jnp.where(live, logits, masked_floor)
@@ -343,25 +344,28 @@
     cost = pl.CostEstimate(
         flops=4 * beams * width * 2 * quarter, bytes_accessed=4 * beams * quarter, transcendentals=0
     )
-    first = pl.pallas_call(
+    first, rest = pl.pallas_call(
         first_kernel,
-        out_shape=jax.ShapeDtypeStruct((2, beams, width), jnp.float32),
-        in_specs=[SMEM] + [VMEM] * 3,
-        out_specs=VMEM,
+        out_shape=(
+            jax.ShapeDtypeStruct((beams, width), jnp.float32),
+            jax.ShapeDtypeStruct((2 * beams, depth_a // 4), jnp.bfloat16),
+        ),
+        in_specs=[SMEM] + [VMEM] * 2,
+        out_specs=(VMEM, VMEM),
         compiler_params=PARAMS,
         cost_estimate=cost,
         name="first_half",
-    )(position, half, expert_head, amateur_head)
+    )(position, half, expert_head)
     table = pl.pallas_call(
         second_kernel,
         out_shape=jax.ShapeDtypeStruct((rows, 2 * own, 256), jnp.float32),
-        in_specs=[SMEM] + [VMEM] * 7,
+        in_specs=[SMEM] + [VMEM] * 8,
         out_specs=VMEM,
         scratch_shapes=[pltpu.VMEM((2, beams, width), jnp.float32)],
         compiler_params=PARAMS,
         cost_estimate=cost,
         name="second_half",
-    )(position, other_half, expert_head, amateur_head, first, live_mask.reshape(1, -1), ids, gap)
+    )(position, other_half, expert_head, amateur_head, first, rest, live_mask.reshape(1, -1), ids, gap)
     table = lax.all_to_all(table, "rows", 0, 0, tiled=True, axis_index_groups=[order])
 
     small = jax.ShapeDtypeStruct((planes, own, 128), jnp.float32)

time: 79.1 us -> 78.2 us (0.989)
  local copies, waits for them, and re-layouts: 2.39 us -> 1.06 us
    unnamed x12, local copies, waits for them, and re-layouts: 1.94 us -> 0.6 us
  transfers between devices with their start and end apart: 1 -> 1, of which waited for: 0 -> 1; matrix products, arithmetic and copies ran while one was open for 1% -> 1% of each run, Pallas kernels for 3% -> 3%
where the time goes in v15:
time: 78.2 us; the launch traced here: 77.8 us
  blocking collectives  61.5 us (79%)
  Pallas kernels  11 us (14%)
  starting transfers between devices  2.3 us (3%)
  between operations  1.41 us (2%)
  local copies, waits for them, and re-layouts  1.06 us (1%)
    all_to_all x1, blocking collectives, per_device(): lax.all_to_all(blocks, 'rows', 0, 0, tiled=True, axis_index_groups=[order])  31.8 us
    all_to_all x1, blocking collectives, per_device(): lax.all_to_all(stats, 'vocab', 0, 0, tiled=True, axis_index_groups=around)  17.7 us
    all_to_all x1, blocking collectives, per_device(): lax.all_to_all(table, 'rows', 0, 0, tiled=True, axis_index_groups=[order])  12 us
    pallas_call x1, Pallas kernels, per_device(): pl.pallas_call(second_kernel, out_shape=jax.ShapeDtypeStruct((rows, 2 * o...  3.07 us
    pallas_call x1, Pallas kernels, per_device(): pl.pallas_call(norm_kernel, out_shape=jax.ShapeDtypeStruct((rows, 2 * own...  2.62 us
    ppermute x1, starting transfers between devices, per_device(): other_half = lax.ppermute(half, 'rows', [(r, r ^ 1) for r in range(rows)])  2.3 us
    pallas_call x1, Pallas kernels, per_device(): pl.pallas_call(first_kernel, out_shape=(jax.ShapeDtypeStruct((beams, widt...  2.23 us
    pallas_call x1, Pallas kernels, per_device(): pl.pallas_call(functools.partial(stats_kernel, width), out_shape=small, i...  2.02 us
  transfers between devices with their start and end apart: 1, of which 1 were waited for; matrix products, arithmetic and copies ran while one was open for 1% of the time, Pallas kernels for 3%

profile of v15, /device:TPU:1, one launch (start us, length us, event | category | flops | bytes accessed | tf_op | source)
XLA Modules:
  0.0 77.8 jit_solution(10550580623847139848)
XLA Ops:
  0.6 0.0 copy-start
  0.6 0.0 copy-start.5
  0.7 2.6 %norms.1 = bf16[32,8,2944]{2,1,0:T(8,128)(2,1)} custom-call(bf16[4,8192]{1,0:T(4,128)(2,1)} %refs_0_.1, bf16[64,128]{1,0:T(8,128)(2,1)} %bitcast.15, bf16[4,3584]{1,0:T(4,128)(2,1)} %refs_2_.1, bf16[28,128]{1,0:T(8,128)(2,1)} %bitcast.16), custom_call_target="tpu_custom_call" | custom-call | tf_op jit(solution)/shard_map/norms/pallas_call | solution.py:326
  3.3 0.0 copy-start.1
  3.3 31.8 %all_to_all.20 = bf16[32,8,2944]{2,1,0:T(8,128)(2,1)} all-to-all(bf16[32,8,2944]{2,1,0:T(8,128)(2,1)} %norms.1), channel_id=1, replica_groups={{320,336,352,368,384,400,416,432,448,464,480,496,0,16,32,48,64,80,96,11..., dimensions={0} | all-to-all | bytes 3014656 | tf_op jit(solution)/shard_map/all_to_all | solution.py:342
  35.1 2.3 %collective-permute-start = (bf16[256,2944]{1,0:T(8,128)(2,1)}, bf16[256,2944]{1,0:T(8,128)(2,1)}, u32[]{:S(2)}, u32[]{:S(2)}) collective-permute-start(bf16[256,2944]{1,0:T(8,128)(2,1)} %bitcast.4.part_ref), channel_id=1, source_target_pairs={{0,16},{16,0},{32,48},{48,32},{64,80},{80,64},{96,112},{112,96},{1... | collective-permute-start | bytes 4521992 | tf_op jit(solution)/shard_map/ppermute | solution.py:343
  37.4 0.0 copy-done.5
  37.4 0.1 slice.8
  37.5 0.1 pad_add_fusion.1
  37.6 0.1 reshape.38
  37.7 0.1 reshape.43.ids_ref
  37.8 0.0 copy-done
  37.8 0.1 dynamic-slice_bitcast_fusion
  37.9 0.1 copy.20._.gap_ref
  38.0 0.1 pad_add_fusion.pos_ref
  38.1 0.0 copy-done.1
  38.1 0.0 copy-start.2
  38.1 0.0 copy-start.3
  38.1 2.2 %first_half.1 = (f32[128,192]{1,0:T(8,128)S(1)}, bf16[256,896]{1,0:T(8,128)(2,1)S(1)}) custom-call(s32[2]{0:T(128)S(1)} %pad_add_fusion.pos_ref, bf16[256,2944]{1,0:T(8,128)(2,1)} %bitcast.4.part_ref, bf16[192,8192]{1,0:T(8,128)(2,1)S(1)} %copy-done.1), custom_call_target="tpu_custom_call" | custom-call | flops 578813952 | bytes 1507328 | tf_op jit(solution)/shard_map/first_half/pallas_call | solution.py:347
  40.3 0.3 collective-permute-done.part_ref
  40.7 0.0 copy-done.2
  40.7 0.0 copy-done.3
  40.7 3.1 %second_half.1 = f32[32,8,256]{2,1,0:T(8,128)S(1)} custom-call(s32[2]{0:T(128)S(1)} %pad_add_fusion.pos_ref, bf16[256,2944]{1,0:T(8,128)(2,1)} %collective-permute-done.part_ref, bf16[192,8192]{1,0:T(8,128)(2,1)S(1)} %copy-done.1, bf16[192,3584]{1,0:T(8,128)(2,1)S(1)} %copy-done.2, f32[128,192]{1,0:T(8,128)S(1)} %get-tuple-element.28.first_ref, ...), custom_call_target="tpu_custom_call" | custom-call | flops 578813952 | bytes 1507328 | tf_op jit(solution)/shard_map/second_half/pallas_call | solution.py:359
  43.7 12.0 %all_to_all.21.table_ref = f32[32,8,256]{2,1,0:T(8,128)S(1)} all-to-all(f32[32,8,256]{2,1,0:T(8,128)S(1)} %second_half.1), channel_id=1, replica_groups={{320,336,352,368,384,400,416,432,448,464,480,496,0,16,32,48,64,80,96,11..., dimensions={0} | all-to-all | bytes 524288 | tf_op jit(solution)/shard_map/all_to_all | solution.py:369
  55.7 2.0 %stats.1 = f32[16,4,128]{2,1,0:T(4,128)S(1)} custom-call(f32[32,8,256]{2,1,0:T(8,128)S(1)} %all_to_all.21.table_ref, s32[4,1]{1,0:T(4,128)S(1)} %copy.20._.gap_ref), custom_call_target="tpu_custom_call" | custom-call | tf_op jit(solution)/shard_map/stats/pallas_call | solution.py:373
  57.8 17.7 %all_to_all.22.stats_ref = f32[16,4,128]{2,1,0:T(4,128)S(1)} all-to-all(f32[16,4,128]{2,1,0:T(4,128)S(1)} %stats.1), channel_id=1, replica_groups={{8,9,10,11,12,13,14,15,0,1,2,3,4,5,6,7},{24,25,26,27,28,29,30,31,16,17,..., dimensions={0} | all-to-all | bytes 65536 | tf_op jit(solution)/shard_map/all_to_all | solution.py:382
  75.5 1.0 %finish.1 = (f32[4,4]{1,0:T(4,128)S(1)}, f32[2,4]{1,0:T(2,128)}, f32[1,4]{1,0:T(1,128)}, s32[1]{0:T(128)}) custom-call(f32[16,4,128]{2,1,0:T(4,128)S(1)} %all_to_all.22.stats_ref, s32[4,1]{1,0:T(4,128)S(1)} %copy.20._.gap_ref), custom_call_target="tpu_custom_call" | custom-call | tf_op jit(solution)/shard_map/finish/pallas_call | solution.py:383
  77.2 0.0 copy-start.4
  77.2 0.6 copy-done.4
  (2 shorter events, 0.0 us)
Async XLA Ops:
  0.6 37.2 %copy-start = (s32[128]{0:T(128)S(1)}, s32[128]{0:T(128)}, u32[]{:S(2)}) copy-start(s32[128]{0:T(128)} %param.19) | copy-start | bytes 1540
  0.6 36.8 %copy-start.5 = (s32[128]{0:T(128)S(1)}, s32[128]{0:T(128)}, u32[]{:S(2)}) copy-start(s32[128]{0:T(128)} %param.18) | copy-start | bytes 1540
  3.3 34.8 %copy-start.1 = (bf16[192,8192]{1,0:T(8,128)(2,1)S(1)}, bf16[192,8192]{1,0:T(8,128)(2,1)}, u32[]{:S(2)}) copy-start(bf16[192,8192]{1,0:T(8,128)(2,1)} %he_ref.1) | copy-start | bytes 9437188
  35.1 5.6 %collective-permute-start = (bf16[256,2944]{1,0:T(8,128)(2,1)}, bf16[256,2944]{1,0:T(8,128)(2,1)}, u32[]{:S(2)}, u32[]{:S(2)}) collective-permute-start(bf16[256,2944]{1,0:T(8,128)(2,1)} %bitcast.4.part_ref), channel_id=1, source_target_pairs={{0,16},{16,0},{32,48},{48,32},{64,80},{80,64},{96,112},{112,96},{1... | collective-permute-start | bytes 4521992 | tf_op jit(solution)/shard_map/ppermute | solution.py:343
  38.1 2.6 %copy-start.2 = (bf16[192,3584]{1,0:T(8,128)(2,1)S(1)}, bf16[192,3584]{1,0:T(8,128)(2,1)}, u32[]{:S(2)}) copy-start(bf16[192,3584]{1,0:T(8,128)(2,1)} %ha_ref) | copy-start | bytes 4128772
  38.1 2.6 %copy-start.3 = (s32[192]{0:T(256)S(1)}, s32[192]{0:T(256)}, u32[]{:S(2)}) copy-start(s32[192]{0:T(256)} %param.17) | copy-start | bytes 2308
  77.2 0.6 copy-start.4
